TPU v7x, 128 devices: a whole 4x4x4 slice. The times are simulated.
128 devices in a mesh: feat: 32 (over y, z, core), pair: 4 (over x).
Axes of the slice: x: 4, y: 4, z: 4, core: 2. Of those that a mesh axis runs over, the one named last changes fastest.
Arguments:
- in_factors: bfloat16 [2048, 2, 512, 256], P(('feat', 'pair')), may hold values from -6 to 6
- out_factors: bfloat16 [2048, 2, 512, 256], P(('feat', 'pair')), may hold values from -0.26367188 to 0.26367188
- token_counts: int32 [2048, 2], P(('feat', 'pair')), may hold values from 1 to 512, as said below
- slot_pair: int32 [4, 512], P('pair'), may hold values from 0 to 511, each once within a row
- factor_panels: float32 [65536, 1536], P('feat'), as said below
Outputs:
- reduced: float32 [2048, 65536], P('pair', 'feat')
Inputs may be any that keep to these rules, and one draw needn't show every extreme that they name: `token_counts`: column 0 counts the chosen response's tokens, column 1 the rejected one's; positions at or beyond the count are padding. `slot_pair`: each row is a permutation of 0 to 511. `factor_panels`: entries above the diagonal in the unknowns' order are zero: rows of panel j hold zeros in the columns of panels after j, and D_k has a positive diagonal.
All inputs are finite; a program needn't handle non-finite values.
Results may differ from a plain program's by a relative error of at most 0.0003.
Values sent between devices are 32-bit elements; how exact they have to be, the bound alone decides.
No kernel may reach another device: no remote copies, remote signals or barrier semaphores. Data moves between devices by JAX's collectives and lax.ppermute only.
A program may use at most 128 MiB of HBM per device.

v0:
```python
import jax
import jax.numpy as jnp
from jax import lax
from jax.experimental import pallas as pl
from jax.experimental.pallas import tpu as pltpu
from jax.sharding import PartitionSpec as P

PANEL = 512
PANELS = 3
HIGHEST = lax.Precision.HIGHEST


def gradient_kernel(counts_ref, out_ref, in_ref, send_ref, panel_ref):
    slot = pl.program_id(0)
    depth, rank = out_ref.shape[2:]
    position = lax.broadcasted_iota(jnp.int32, (depth, 128), 0)
    total = None
    for side in range(2):
        kept = jnp.where(position < counts_ref[slot, side], 1.0, 0.0).astype(jnp.bfloat16)
        weights = jnp.concatenate([kept] * (rank // 128), axis=1)
        product = lax.dot_general(
            out_ref[0, side] * weights,
            in_ref[0, side],
            (((0,), (0,)), ((), ())),
            preferred_element_type=jnp.float32,
        )
        total = product if side == 0 else total - product
    feats, _, _, lanes, parts, lane = send_ref.shape
    for h in range(lanes):
        columns = total[:, h * lane : (h + 1) * lane]
        send_ref[:, 0, 0, h] = columns.reshape(feats, parts, lane)
    for k in range(PANELS):
        for i in range(PANEL // rank):
            columns = slice(k * PANEL + i * rank, k * PANEL + (i + 1) * rank)
            panel_ref[pl.ds(slot, 1), columns] = total[8 * k + i : 8 * k + i + 1, :]


def slot_gradients(token_counts, out_factors, in_factors, n_feat, n_pair):
    slots, sides, depth, rank = in_factors.shape
    per_group = slots // n_pair
    factors = pl.BlockSpec((1, sides, depth, rank), lambda k, counts: (k, 0, 0, 0))
    return pl.pallas_call(
        gradient_kernel,
        grid_spec=pltpu.PrefetchScalarGridSpec(
            num_scalar_prefetch=1,
            grid=(slots,),
            in_specs=[factors, factors],
            out_specs=[
                pl.BlockSpec(
                    (n_feat, 1, 1, rank // 128, rank // n_feat, 128),
                    lambda k, counts: (0, k // per_group, k % per_group, 0, 0, 0),
                ),
                pl.BlockSpec((slots, PANELS * PANEL), lambda k, counts: (0, 0)),
            ],
        ),
        out_shape=[
            jax.ShapeDtypeStruct(
                (n_feat, n_pair, per_group, rank // 128, rank // n_feat, 128), jnp.float32
            ),
            jax.ShapeDtypeStruct((slots, PANELS * PANEL), jnp.float32),
        ],
        compiler_params=pltpu.CompilerParams(vmem_limit_bytes=48 * 2**20),
        cost_estimate=pl.CostEstimate(
            flops=2 * slots * sides * depth * rank * rank, bytes_accessed=24 * 2**20, transcendentals=0
        ),
        name="slot_gradients",
    )(token_counts, out_factors, in_factors)


def invert_kernel(place_ref, panel_ref, send_ref, d_ref, x_ref):
    def dot(a, b):
        return jnp.dot(a, b, precision=HIGHEST, preferred_element_type=jnp.float32)

    whole_row = lax.broadcasted_iota(jnp.int32, d_ref.shape, 0)
    whole_col = lax.broadcasted_iota(jnp.int32, d_ref.shape, 1)
    d_ref[...] = jnp.where(whole_row == whole_col, 1.0, 0.0)
    for k in range(PANELS):

        @pl.when((place_ref[1] == 1) & (place_ref[0] == k))
        def _():
            d_ref[...] = panel_ref[:, k * PANEL : (k + 1) * PANEL]

    base = 128
    count = PANEL // base
    row = lax.broadcasted_iota(jnp.int32, (base, base), 0)
    col = lax.broadcasted_iota(jnp.int32, (base, base), 1)
    blocks = [d_ref[n * base : (n + 1) * base, n * base : (n + 1) * base] for n in range(count)]
    inverses = [jnp.where(row == col, 1.0 / jnp.where(row == col, b, 1.0), 0.0) for b in blocks]
    size = 1
    while size < base:
        joins = (row // (2 * size) == col // (2 * size)) & (row // size != col // size) & (row > col)
        inner = [dot(jnp.where(joins, b, 0.0), x) for b, x in zip(blocks, inverses)]
        inverses = [x - dot(x, y) for x, y in zip(inverses, inner)]
        size *= 2
    x_ref[...] = jnp.zeros_like(x_ref)
    for n in range(count):
        x_ref[n * base : (n + 1) * base, n * base : (n + 1) * base] = inverses[n]
    size = base
    while size < PANEL:
        for start in range(0, PANEL, 2 * size):
            top = slice(start, start + size)
            low = slice(start + size, start + 2 * size)
            x_ref[low, top] = -dot(x_ref[low, low], dot(d_ref[low, top], x_ref[top, top]))
        size *= 2
    chips, _, depth, _ = send_ref.shape
    groups = PANEL // (chips * depth)
    for chip in range(chips):
        rows = pl.ds(pl.multiple_of((chip * groups + place_ref[3]) * depth, depth), depth)
        send_ref[chip, 0, :, :PANEL] = x_ref[rows, :]
        send_ref[chip, 0, :, PANEL:] = jnp.zeros((depth, PANEL), jnp.float32)
        send_ref[chip, 1] = panel_ref[rows, : 2 * PANEL]


def invert_and_cut(place, factor_panels, n_feat, n_pair):
    width = factor_panels.shape[1]
    chips = n_feat // 2
    depth = PANEL // (chips * n_pair)
    return pl.pallas_call(
        invert_kernel,
        grid=(1,),
        in_specs=[
            pl.BlockSpec(memory_space=pltpu.SMEM),
            pl.BlockSpec((PANEL, width), lambda i: (0, 0)),
        ],
        out_specs=pl.BlockSpec((chips, 2, depth, 2 * PANEL), lambda i: (0, 0, 0, 0)),
        out_shape=jax.ShapeDtypeStruct((chips, 2, depth, 2 * PANEL), jnp.float32),
        scratch_shapes=[
            pltpu.VMEM((PANEL, PANEL), jnp.float32),
            pltpu.VMEM((PANEL, PANEL), jnp.float32),
        ],
        compiler_params=pltpu.CompilerParams(vmem_limit_bytes=60 * 2**20),
        name="invert_and_cut",
    )(place, factor_panels)


def split(value):
    high = value.astype(jnp.bfloat16)
    return high, (value - high.astype(jnp.float32)).astype(jnp.bfloat16)


def one_hot(pairs, first, rows):
    pair = lax.broadcasted_iota(jnp.int32, (rows, pairs.shape[1]), 0) + first
    return jnp.where(pair == pairs, 1.0, 0.0).astype(jnp.bfloat16)


def place_kernel(place_ref, pairs_ref, received_ref, update_ref, out_ref, high_ref, low_ref):
    step = pl.program_id(0)
    rows = out_ref.shape[0]
    parts, total, rank = high_ref.shape

    @pl.when(step == 0)
    def _():
        for i in range(parts):
            lanes = rank // 128
            value = jnp.concatenate(
                [
                    received_ref[pl.ds(h * parts + i, total, stride=lanes * parts), :]
                    for h in range(lanes)
                ],
                axis=1,
            )
            if i * rank < PANEL:
                value = jnp.where(place_ref[1] == 1, 0.0, value)
            high_ref[i], low_ref[i] = split(value)

    chosen = one_hot(pairs_ref[...], step * rows, rows)
    for i in range(parts):
        placed = jnp.dot(chosen, high_ref[i], preferred_element_type=jnp.float32)
        placed += jnp.dot(chosen, low_ref[i], preferred_element_type=jnp.float32)
        columns = slice(i * rank, (i + 1) * rank)
        out_ref[:, columns] = placed - update_ref[:, columns]


def place_rows(place, slot_pair, received, update):
    total, width = update.shape
    rank = 2 * received.shape[1]
    parts = width // rank
    rows = 128
    return pl.pallas_call(
        place_kernel,
        grid=(total // rows,),
        in_specs=[
            pl.BlockSpec(memory_space=pltpu.SMEM),
            pl.BlockSpec((1, total), lambda i: (0, 0)),
            pl.BlockSpec(received.shape, lambda i: (0, 0)),
            pl.BlockSpec((rows, width), lambda i: (i, 0)),
        ],
        out_specs=pl.BlockSpec((rows, width), lambda i: (i, 0)),
        out_shape=jax.ShapeDtypeStruct((total, width), jnp.float32),
        scratch_shapes=[
            pltpu.VMEM((parts, total, rank), jnp.bfloat16),
            pltpu.VMEM((parts, total, rank), jnp.bfloat16),
        ],
        compiler_params=pltpu.CompilerParams(vmem_limit_bytes=48 * 2**20),
        name="place_rows",
    )(place, slot_pair, received, update)


def dot_split(a, b):
    def dot(x, y):
        return lax.dot_general(x, y, (((1,), (1,)), ((), ())), preferred_element_type=jnp.float32)

    return dot(a[0], b[0]) + (dot(a[0], b[1]) + dot(a[1], b[0]))


def arrange_kernel(pairs_ref, near_ref, far_ref, out_ref):
    half = near_ref.shape[0]
    right = None
    for n, ref in enumerate((near_ref, far_ref)):
        chosen = one_hot(pairs_ref[:, n * half : (n + 1) * half], 0, 2 * half)
        for part in split(ref[...]):
            moved = jnp.dot(chosen, part, preferred_element_type=jnp.float32)
            right = moved if right is None else right + moved
    out_ref[...] = right


def arrange_rows(pairs, near, far):
    half, width = near.shape
    rows = pl.BlockSpec((half, PANEL), lambda k: (0, k))
    return pl.pallas_call(
        arrange_kernel,
        grid=(width // PANEL,),
        in_specs=[pl.BlockSpec(pairs.shape, lambda k: (0, 0)), rows, rows],
        out_specs=pl.BlockSpec((2 * half, PANEL), lambda k: (0, k)),
        out_shape=jax.ShapeDtypeStruct((2 * half, width), jnp.float32),
        compiler_params=pltpu.CompilerParams(vmem_limit_bytes=40 * 2**20),
        name="arrange_rows",
    )(pairs, near, far)


def split_kernel(value_ref, high_ref, low_ref):
    high_ref[...], low_ref[...] = split(value_ref[...])


def split_factor(factor_panels):
    rows, depth = factor_panels.shape
    block = pl.BlockSpec((256, depth), lambda i: (i, 0))
    return pl.pallas_call(
        split_kernel,
        grid=(rows // 256,),
        in_specs=[block],
        out_specs=[block, block],
        out_shape=[jax.ShapeDtypeStruct((rows, depth), jnp.bfloat16)] * 2,
        compiler_params=pltpu.CompilerParams(vmem_limit_bytes=60 * 2**20),
        name="split_factor",
    )(factor_panels)


def solve_kernel(
    place_ref, right_ref, mine_ref, other_ref, factor_high_ref, factor_low_ref, out_ref,
    solved_ref, high_ref, low_ref,
):
    step = pl.program_id(0)
    width = out_ref.shape[1]

    @pl.when(step == 0)
    def _():
        first_core = place_ref[2] == 0

        def factor(k, below):
            columns = slice(k * PANEL, (k + 1) * PANEL)
            return split(
                jnp.where(first_core != below, mine_ref[:, columns], other_ref[:, columns])
            )

        for k in range(PANELS):
            columns = slice(k * PANEL, (k + 1) * PANEL)
            right = right_ref[:, columns]
            for j in range(k):
                before = slice(j * PANEL, (j + 1) * PANEL)
                solved = (high_ref[:, before], low_ref[:, before])
                right -= dot_split(solved, factor(k * (k - 1) // 2 + j, True))
            value = dot_split(split(right), factor(k, False))
            solved_ref[k] = value
            high_ref[:, columns], low_ref[:, columns] = split(value)

    out_ref[...] = dot_split(
        (high_ref[...], low_ref[...]), (factor_high_ref[...], factor_low_ref[...])
    )

    for i in range(PANEL // width):

        @pl.when((place_ref[1] == 1) & (step == i))
        def _():
            out_ref[...] = -solved_ref[place_ref[0], :, i * width : (i + 1) * width]


def solve_and_update(place, right, mine, other, factor_parts):
    rows, depth = factor_parts[0].shape
    total = right.shape[0]
    width = 256
    whole = lambda v: pl.BlockSpec(v.shape, lambda i: (0, 0))
    block = pl.BlockSpec((width, depth), lambda i: (i, 0))
    return pl.pallas_call(
        solve_kernel,
        grid=(rows // width,),
        in_specs=[
            pl.BlockSpec(memory_space=pltpu.SMEM),
            whole(right),
            whole(mine),
            whole(other),
            block,
            block,
        ],
        out_specs=pl.BlockSpec((total, width), lambda i: (0, i)),
        out_shape=jax.ShapeDtypeStruct((total, rows), jnp.float32),
        scratch_shapes=[
            pltpu.VMEM((PANELS, total, PANEL), jnp.float32),
            pltpu.VMEM((total, depth), jnp.bfloat16),
            pltpu.VMEM((total, depth), jnp.bfloat16),
        ],
        compiler_params=pltpu.CompilerParams(vmem_limit_bytes=48 * 2**20),
        name="solve_and_update",
    )(place, right, mine, other, *factor_parts)


def gather_factor(arrived, feat, n_feat, n_pair):
    first = jnp.concatenate([arrived[k, :, :PANEL] for k in range(3)], axis=1)
    second = jnp.concatenate([arrived[1, :, :PANEL], arrived[2]], axis=1)
    shard = jnp.where(feat % 2 == 0, first, second)
    groups = [
        [f * n_pair + p for f in range(c, n_feat, 2) for p in range(n_pair)] for c in range(2)
    ]
    return lax.all_gather(shard, ("feat", "pair"), axis_index_groups=groups, tiled=True)


def along(value, axis, shift):
    if axis == "pair":
        return lax.ppermute(value, "pair", [(p, (p + shift) % 4) for p in range(4)])
    stride = 8 if axis == "y" else 2
    ring = lambda f: f - f // stride % 4 * stride + (f // stride + shift) % 4 * stride
    n_feat = lax.axis_size("feat")
    return lax.ppermute(value, "feat", [(f, ring(f)) for f in range(n_feat)])


def gather_rows(panel_part, feat, pair, slot_pair):
    slots, width = panel_part.shape
    groups = panel_part.reshape(4, slots // 4, width)
    piece = lambda k: lax.dynamic_index_in_dim(groups, (pair + k) % 4, 0, keepdims=False)
    rows = jnp.concatenate([piece(0)] + [along(piece(k), "pair", k) for k in range(1, 4)], axis=0)
    half = slots // 2
    gathered = []
    for part, axes in ((rows[:half], ("z", "y")), (rows[half:], ("y", "z"))):
        for axis in axes:
            part = jnp.concatenate([part] + [along(part, axis, k) for k in range(1, 4)], axis=0)
        gathered.append(part)
    near = jnp.concatenate(gathered, axis=0)
    far = lax.ppermute(near, "feat", [(f, f ^ 1) for f in range(lax.axis_size("feat"))])
    n = lax.broadcasted_iota(jnp.int32, (128, 128), 0)
    other_core, second, outer, inner, back = n // 64, n // 32 % 2, n // 8 % 4, n // 2 % 4, n % 2
    y_back = jnp.where(second == 0, outer, inner)
    z_back = jnp.where(second == 0, inner, outer)
    y = (feat // 8 + 4 - y_back) % 4
    z = (feat // 2 % 4 + 4 - z_back) % 4
    core = (feat % 2 + other_core) % 2
    x = (pair + 4 - (2 * second + back)) % 4
    source = ((y * 4 + z) * 2 + core) * 4 + x
    chosen = (source == lax.broadcasted_iota(jnp.int32, (128, 128), 1)).astype(jnp.float32)
    table = slot_pair.reshape(128, slots // 4).astype(jnp.float32)
    pairs = jnp.dot(chosen, table, precision=HIGHEST, preferred_element_type=jnp.float32)
    pairs = jnp.round(pairs).astype(jnp.int32).reshape(1, 32 * slots)
    return near, far, pairs


def per_device(in_factors, out_factors, token_counts, slot_pair, factor_panels):
    slots, _, _, rank = in_factors.shape
    n_pair = lax.axis_size("pair")
    n_feat = lax.axis_size("feat")
    per_group = slots // n_pair
    feat = lax.axis_index("feat")
    pair = lax.axis_index("pair")
    total = n_feat * slots

    place = jnp.stack(
        [jnp.minimum(feat, PANELS - 1), (feat < PANELS).astype(jnp.int32), feat % 2, pair]
    ).astype(jnp.int32)
    outgoing = invert_and_cut(place, factor_panels, n_feat, n_pair)
    arrived = lax.all_to_all(
        outgoing.reshape((n_feat,) + outgoing.shape[2:]), "feat", split_axis=0, concat_axis=0, tiled=True
    )
    send, panel_part = slot_gradients(token_counts, out_factors, in_factors, n_feat, n_pair)
    arrived, panel_part = lax.optimization_barrier((arrived, panel_part))
    mine = gather_factor(arrived, feat, n_feat, n_pair)
    near, far, pairs = gather_rows(panel_part, feat, pair, slot_pair)
    send, near = lax.optimization_barrier((send, near))
    right = arrange_rows(pairs, near, far)
    parts = split_factor(factor_panels)
    mine, right, parts = lax.optimization_barrier((mine, right, parts))
    other = lax.ppermute(mine, "feat", [(f, f ^ 1) for f in range(n_feat)])
    received = lax.all_to_all(
        send.reshape((n_feat * n_pair,) + send.shape[2:]),
        ("feat", "pair"),
        split_axis=0,
        concat_axis=0,
        tiled=True,
    ).reshape(total * (rank // 128) * (rank // n_feat), 128)
    update = solve_and_update(place, right, mine, other, parts)
    return place_rows(place, slot_pair, received, update)


def solution(mesh):
    return jax.shard_map(
        per_device,
        mesh=mesh,
        in_specs=(
            P(("feat", "pair"), None, None, None),
            P(("feat", "pair"), None, None, None),
            P(("feat", "pair"), None),
            P("pair", None),
            P("feat", None),
        ),
        out_specs=P("pair", "feat"),
        check_vma=False,
    )
```

profile of v0, /device:TPU:1, one launch (start us, length us, event | category | flops | bytes accessed | tf_op | source)
XLA Modules:
  0.0 189.8 jit_solution(12806951635005824735)
XLA Ops:
  7.1 8.3 %invert_and_cut.1 = f32[16,2,8,1024]{3,2,1,0:T(8,128)} custom-call(s32[4]{0:T(128)} %pad_add_fusion.place_ref, f32[2048,1536]{1,0:T(8,128)} %value_ref.1), custom_call_target="tpu_custom_call" | custom-call | tf_op jit(solution)/shard_map/invert_and_cut/pallas_call | solution.py:118
  15.4 9.6 %all-to-all-start = ((f32[32,8,1024]{2,1,0:T(8,128)}), f32[32,8,1024]{2,1,0:T(8,128)S(1)}, u32[]{:S(2)}, u32[]{:S(2)}) async-start(f32[32,8,1024]{2,1,0:T(8,128)} %bitcast.25), calls=%async_computation | async-start | bytes 2097152 | tf_op jit(solution)/shard_map/all_to_all | solution.py:378
  25.1 14.6 %slot_gradients.1 = (f32[32,4,4,2,8,128]{5,4,3,2,1,0:T(8,128)S(1)}, f32[16,1536]{1,0:T(8,128)S(1)}) custom-call(s32[16,2]{1,0:T(8,128)S(1)} %copy.8.counts_ref, bf16[16,2,512,256]{3,2,1,0:T(8,128)(2,1)} %out_ref.1, bf16[16,2,512,256]{3,2,1,0:T(8,128)(2,1)} %in_ref.1), custom_call_target="tpu_custom_call" | custom-call | flops 2147483648 | bytes 25165824 | tf_op jit(solution)/shard_map/slot_gradients/pallas_call | solution.py:42
  39.7 2.0 %copy-done.2 = f32[32,4,4,2,8,128]{5,4,3,2,1,0:T(8,128)} copy-done((f32[32,4,4,2,8,128]{5,4,3,2,1,0:T(8,128)}, f32[32,4,4,2,8,128]{5,4,3,2,1,0:T(8,128)S(1)}, u32[]{:S(2)}) %copy-start.2) | copy-done | bytes 4194328
  42.7 2.5 %collective-permute-start.8 = (f32[4,1536]{1,0:T(4,128)S(1)}, f32[4,1536]{1,0:T(4,128)S(1)}, u32[]{:S(2)}, u32[]{:S(2)}) collective-permute-start(f32[4,1536]{1,0:T(4,128)S(1)} %get-tuple-element.32), channel_id=1, source_target_pairs={{0,3},{1,0},{2,1},{3,2},{4,7},{5,4},{6,5},{7,6},{8,11},{9,8},{10,9... | collective-permute-start | bytes 73736 | tf_op jit(solution)/shard_map/ppermute | solution.py:329
  46.2 3.2 %collective-permute-done.7 = f32[4,1536]{1,0:T(4,128)S(1)} collective-permute-done((f32[4,1536]{1,0:T(4,128)S(1)}, f32[4,1536]{1,0:T(4,128)S(1)}, u32[]{:S(2)}, u32[]{:S(2)}) %collective-permute-start.7) | collective-permute-done | bytes 24608 | tf_op jit(solution)/shard_map/ppermute | solution.py:329
  49.4 2.5 %collective-permute-start.11 = (f32[8,1536]{1,0:T(8,128)S(1)}, f32[8,1536]{1,0:T(8,128)S(1)}, u32[]{:S(2)}, u32[]{:S(2)}) collective-permute-start(f32[8,1536]{1,0:T(8,128)S(1)} %pad_maximum_fusion.1), channel_id=1, source_target_pairs={{0,96},{4,100},{8,104},{12,108},{16,112},{20,116},{24,120},{28,124... | collective-permute-start | bytes 147464 | tf_op jit(solution)/shard_map/ppermute | solution.py:333
  53.1 3.3 %collective-permute-done.10 = f32[8,1536]{1,0:T(8,128)S(1)} collective-permute-done((f32[8,1536]{1,0:T(8,128)S(1)}, f32[8,1536]{1,0:T(8,128)S(1)}, u32[]{:S(2)}, u32[]{:S(2)}) %collective-permute-start.10) | collective-permute-done | bytes 49184 | tf_op jit(solution)/shard_map/ppermute | solution.py:333
  57.0 2.5 %collective-permute-start.14 = (f32[32,1536]{1,0:T(8,128)S(1)}, f32[32,1536]{1,0:T(8,128)S(1)}, u32[]{:S(2)}, u32[]{:S(2)}) collective-permute-start(f32[32,1536]{1,0:T(8,128)S(1)} %concatenate.29), channel_id=1, source_target_pairs={{0,24},{4,28},{8,0},{12,4},{16,8},{20,12},{24,16},{28,20},{32,56},... | collective-permute-start | bytes 589832 | tf_op jit(solution)/shard_map/ppermute | solution.py:333
  61.0 3.6 %collective-permute-start.13 = (f32[32,1536]{1,0:T(8,128)S(1)}, f32[32,1536]{1,0:T(8,128)S(1)}, u32[]{:S(2)}, u32[]{:S(2)}) collective-permute-start(f32[32,1536]{1,0:T(8,128)S(1)} %concatenate.29), channel_id=1, source_target_pairs={{0,16},{4,20},{8,24},{12,28},{16,0},{20,4},{24,8},{28,12},{32,48},... | collective-permute-start | bytes 589832 | tf_op jit(solution)/shard_map/ppermute | solution.py:333
  65.1 2.1 %collective-permute-start.6 = (f32[32,1536]{1,0:T(8,128)S(1)}, f32[32,1536]{1,0:T(8,128)S(1)}, u32[]{:S(2)}, u32[]{:S(2)}) collective-permute-start(f32[32,1536]{1,0:T(8,128)S(1)} %concatenate.27), channel_id=1, source_target_pairs={{0,96},{4,100},{8,104},{12,108},{16,112},{20,116},{24,120},{28,124... | collective-permute-start | bytes 589832 | tf_op jit(solution)/shard_map/ppermute | solution.py:333
  68.4 3.7 %collective-permute-done.12 = f32[32,1536]{1,0:T(8,128)S(1)} collective-permute-done((f32[32,1536]{1,0:T(8,128)S(1)}, f32[32,1536]{1,0:T(8,128)S(1)}, u32[]{:S(2)}, u32[]{:S(2)}) %collective-permute-start.12) | collective-permute-done | bytes 196640 | tf_op jit(solution)/shard_map/ppermute | solution.py:333
  72.0 1.6 collective-permute-done.5
  73.6 1.8 collective-permute-done.4
  75.6 8.1 %collective-permute-start.15 = (f32[256,1536]{1,0:T(8,128)S(1)}, f32[256,1536]{1,0:T(8,128)S(1)}, u32[]{:S(2)}, u32[]{:S(2)}) collective-permute-start(f32[256,1536]{1,0:T(8,128)S(1)} %concatenate.30.near_ref), channel_id=1, source_target_pairs={{0,4},{4,0},{8,12},{12,8},{16,20},{20,16},{24,28},{28,24},{32,36},... | collective-permute-start | bytes 4718600 | tf_op jit(solution)/shard_map/ppermute | solution.py:348
  83.7 7.7 %all-to-all-start.1 = ((f32[128,4,2,8,128]{4,3,2,1,0:T(8,128)}), f32[128,4,2,8,128]{4,3,2,1,0:T(8,128)}, u32[]{:S(2)}, u32[]{:S(2)}) async-start(f32[128,4,2,8,128]{4,3,2,1,0:T(8,128)} %bitcast.24), calls=%async_computation.1 | async-start | bytes 8388608 | tf_op jit(solution)/shard_map/all_to_all | solution.py:390
  91.5 11.5 %split_factor.1 = (bf16[2048,1536]{1,0:T(8,128)(2,1)}, bf16[2048,1536]{1,0:T(8,128)(2,1)}) custom-call(f32[2048,1536]{1,0:T(8,128)} %value_ref.1), custom_call_target="tpu_custom_call" | custom-call | tf_op jit(solution)/shard_map/split_factor/pallas_call | solution.py:238
  105.2 1.4 copy-done.1
  108.0 2.6 %arrange_rows.1.right_ref = f32[512,1536]{1,0:T(8,128)S(1)} custom-call(s32[1,512]{1,0:T(1,128)S(1)} %reshape.21.pairs_ref, f32[256,1536]{1,0:T(8,128)S(1)} %copy-done.1, f32[256,1536]{1,0:T(8,128)S(1)} %copy-done.4), custom_call_target="tpu_custom_call" | custom-call | tf_op jit(solution)/shard_map/arrange_rows/pallas_call | solution.py:220
  110.6 34.1 %all-gather.2.cloned.1.call-done.mine_ref = f32[512,1536]{1,0:T(8,128)} async-done(((f32[8,1536]{1,0:T(8,128)}), f32[512,1536]{1,0:T(8,128)}) %all-gather.2.cloned.1.call-update) | async-done | bytes 3145744 | tf_op jit(solution)/shard_map/all_gather | solution.py:324
  145.2 5.5 %collective-permute-done.16.other_ref = f32[512,1536]{1,0:T(8,128)S(1)} collective-permute-done((f32[512,1536]{1,0:T(8,128)}, f32[512,1536]{1,0:T(8,128)S(1)}, u32[]{:S(2)}, u32[]{:S(2)}) %collective-permute-start.16) | collective-permute-done | bytes 3145760 | tf_op jit(solution)/shard_map/ppermute | solution.py:389
  150.7 1.8 copy-done.7
  152.4 21.7 %solve_and_update.1.update_ref = f32[512,2048]{1,0:T(8,128)} custom-call(s32[4]{0:T(128)S(1)} %copy-done.5, f32[512,1536]{1,0:T(8,128)S(1)} %arrange_rows.1.right_ref, f32[512,1536]{1,0:T(8,128)} %all-gather.2.cloned.1.call-done.mine_ref, f32[512,1536]{1,0:T(8,128)} %copy-done.7, bf16[2048,1536]{1,0:T(8,128)(2,1)} %get-tuple-element.27.factor_high_ref, ...), custom_call_target="tpu_custom_call" | custom-call | tf_op jit(solution)/shard_map/solve_and_update/pallas_call | solution.py:294
  174.2 8.8 %place_rows.1 = f32[512,2048]{1,0:T(8,128)} custom-call(s32[4]{0:T(128)S(1)} %copy-done.5, s32[1,512]{1,0:T(1,128)S(1)} %copy-done.6, f32[8192,128]{1,0:T(8,128)} %bitcast.10.received_ref, f32[512,2048]{1,0:T(8,128)} %solve_and_update.1.update_ref), custom_call_target="tpu_custom_call" | custom-call | tf_op jit(solution)/shard_map/place_rows/pallas_call | solution.py:179
  (66 shorter events, 11.6 us)
Async XLA Ops:
  7.1 17.9 %copy-start.8 = (s32[16,2]{0,1:T(2,128)S(1)}, s32[16,2]{0,1:T(2,128)}, u32[]{:S(2)}) copy-start(s32[16,2]{0,1:T(2,128)} %param.7) | copy-start | bytes 388
  15.4 26.5 %all-to-all-start = ((f32[32,8,1024]{2,1,0:T(8,128)}), f32[32,8,1024]{2,1,0:T(8,128)S(1)}, u32[]{:S(2)}, u32[]{:S(2)}) async-start(f32[32,8,1024]{2,1,0:T(8,128)} %bitcast.25), calls=%async_computation | async-start | bytes 2097152 | tf_op jit(solution)/shard_map/all_to_all | solution.py:378
  25.0 119.7 %all-gather.2.cloned.1.call-start = ((), (), s32[]{:S(2)}) async-start(), calls=%async_computation.2 | async-start | bytes 3194880 | tf_op jit(solution)/shard_map/all_gather | solution.py:324
  41.7 42.0 %copy-start.6 = (s32[1,512]{1,0:T(1,128)S(1)}, s32[1,512]{1,0:T(1,128)}, u32[]{:S(2)}) copy-start(s32[1,512]{1,0:T(1,128)} %pairs_ref.1) | copy-start | bytes 6148
  42.7 3.5 %collective-permute-start.8 = (f32[4,1536]{1,0:T(4,128)S(1)}, f32[4,1536]{1,0:T(4,128)S(1)}, u32[]{:S(2)}, u32[]{:S(2)}) collective-permute-start(f32[4,1536]{1,0:T(4,128)S(1)} %get-tuple-element.32), channel_id=1, source_target_pairs={{0,3},{1,0},{2,1},{3,2},{4,7},{5,4},{6,5},{7,6},{8,11},{9,8},{10,9... | collective-permute-start | bytes 73736 | tf_op jit(solution)/shard_map/ppermute | solution.py:329
  45.2 4.2 %collective-permute-start.7 = (f32[4,1536]{1,0:T(4,128)S(1)}, f32[4,1536]{1,0:T(4,128)S(1)}, u32[]{:S(2)}, u32[]{:S(2)}) collective-permute-start(f32[4,1536]{1,0:T(4,128)S(1)} %get-tuple-element.33), channel_id=1, source_target_pairs={{0,2},{1,3},{2,0},{3,1},{4,6},{5,7},{6,4},{7,5},{8,10},{9,11},{10,... | collective-permute-start | bytes 73736 | tf_op jit(solution)/shard_map/ppermute | solution.py:329
  49.4 3.7 %collective-permute-start.11 = (f32[8,1536]{1,0:T(8,128)S(1)}, f32[8,1536]{1,0:T(8,128)S(1)}, u32[]{:S(2)}, u32[]{:S(2)}) collective-permute-start(f32[8,1536]{1,0:T(8,128)S(1)} %pad_maximum_fusion.1), channel_id=1, source_target_pairs={{0,96},{4,100},{8,104},{12,108},{16,112},{20,116},{24,120},{28,124... | collective-permute-start | bytes 147464 | tf_op jit(solution)/shard_map/ppermute | solution.py:333
  52.0 4.5 %collective-permute-start.10 = (f32[8,1536]{1,0:T(8,128)S(1)}, f32[8,1536]{1,0:T(8,128)S(1)}, u32[]{:S(2)}, u32[]{:S(2)}) collective-permute-start(f32[8,1536]{1,0:T(8,128)S(1)} %pad_maximum_fusion.1), channel_id=1, source_target_pairs={{0,64},{4,68},{8,72},{12,76},{16,80},{20,84},{24,88},{28,92},{32,9... | collective-permute-start | bytes 147464 | tf_op jit(solution)/shard_map/ppermute | solution.py:333
  52.5 4.4 %collective-permute-start.9 = (f32[8,1536]{1,0:T(8,128)S(1)}, f32[8,1536]{1,0:T(8,128)S(1)}, u32[]{:S(2)}, u32[]{:S(2)}) collective-permute-start(f32[8,1536]{1,0:T(8,128)S(1)} %pad_maximum_fusion.1), channel_id=1, source_target_pairs={{0,32},{4,36},{8,40},{12,44},{16,48},{20,52},{24,56},{28,60},{32,6... | collective-permute-start | bytes 147464 | tf_op jit(solution)/shard_map/ppermute | solution.py:333
  53.1 6.4 %collective-permute-start = (f32[4,1536]{1,0:T(4,128)S(1)}, f32[4,1536]{1,0:T(4,128)S(1)}, u32[]{:S(2)}, u32[]{:S(2)}) collective-permute-start(f32[4,1536]{1,0:T(4,128)S(1)} %get-tuple-element.34), channel_id=1, source_target_pairs={{0,1},{1,2},{2,3},{3,0},{4,5},{5,6},{6,7},{7,4},{8,9},{9,10},{10,1... | collective-permute-start | bytes 73736 | tf_op jit(solution)/shard_map/ppermute | solution.py:329
  57.0 11.0 %collective-permute-start.14 = (f32[32,1536]{1,0:T(8,128)S(1)}, f32[32,1536]{1,0:T(8,128)S(1)}, u32[]{:S(2)}, u32[]{:S(2)}) collective-permute-start(f32[32,1536]{1,0:T(8,128)S(1)} %concatenate.29), channel_id=1, source_target_pairs={{0,24},{4,28},{8,0},{12,4},{16,8},{20,12},{24,16},{28,20},{32,56},... | collective-permute-start | bytes 589832 | tf_op jit(solution)/shard_map/ppermute | solution.py:333
  59.5 5.1 %collective-permute-start.3 = (f32[8,1536]{1,0:T(8,128)S(1)}, f32[8,1536]{1,0:T(8,128)S(1)}, u32[]{:S(2)}, u32[]{:S(2)}) collective-permute-start(f32[8,1536]{1,0:T(8,128)S(1)} %pad_maximum_fusion), channel_id=1, source_target_pairs={{0,24},{4,28},{8,0},{12,4},{16,8},{20,12},{24,16},{28,20},{32,56},... | collective-permute-start | bytes 147464 | tf_op jit(solution)/shard_map/ppermute | solution.py:333
  60.1 4.5 %collective-permute-start.2 = (f32[8,1536]{1,0:T(8,128)S(1)}, f32[8,1536]{1,0:T(8,128)S(1)}, u32[]{:S(2)}, u32[]{:S(2)}) collective-permute-start(f32[8,1536]{1,0:T(8,128)S(1)} %pad_maximum_fusion), channel_id=1, source_target_pairs={{0,16},{4,20},{8,24},{12,28},{16,0},{20,4},{24,8},{28,12},{32,48},... | collective-permute-start | bytes 147464 | tf_op jit(solution)/shard_map/ppermute | solution.py:333
  60.4 4.7 %collective-permute-start.1 = (f32[8,1536]{1,0:T(8,128)S(1)}, f32[8,1536]{1,0:T(8,128)S(1)}, u32[]{:S(2)}, u32[]{:S(2)}) collective-permute-start(f32[8,1536]{1,0:T(8,128)S(1)} %pad_maximum_fusion), channel_id=1, source_target_pairs={{0,8},{4,12},{8,16},{12,20},{16,24},{20,28},{24,0},{28,4},{32,40},... | collective-permute-start | bytes 147464 | tf_op jit(solution)/shard_map/ppermute | solution.py:333
  61.0 7.3 %collective-permute-start.13 = (f32[32,1536]{1,0:T(8,128)S(1)}, f32[32,1536]{1,0:T(8,128)S(1)}, u32[]{:S(2)}, u32[]{:S(2)}) collective-permute-start(f32[32,1536]{1,0:T(8,128)S(1)} %concatenate.29), channel_id=1, source_target_pairs={{0,16},{4,20},{8,24},{12,28},{16,0},{20,4},{24,8},{28,12},{32,48},... | collective-permute-start | bytes 589832 | tf_op jit(solution)/shard_map/ppermute | solution.py:333
  64.6 7.4 %collective-permute-start.12 = (f32[32,1536]{1,0:T(8,128)S(1)}, f32[32,1536]{1,0:T(8,128)S(1)}, u32[]{:S(2)}, u32[]{:S(2)}) collective-permute-start(f32[32,1536]{1,0:T(8,128)S(1)} %concatenate.29), channel_id=1, source_target_pairs={{0,8},{4,12},{8,16},{12,20},{16,24},{20,28},{24,0},{28,4},{32,40},... | collective-permute-start | bytes 589832 | tf_op jit(solution)/shard_map/ppermute | solution.py:333
  65.1 6.9 %collective-permute-start.6 = (f32[32,1536]{1,0:T(8,128)S(1)}, f32[32,1536]{1,0:T(8,128)S(1)}, u32[]{:S(2)}, u32[]{:S(2)}) collective-permute-start(f32[32,1536]{1,0:T(8,128)S(1)} %concatenate.27), channel_id=1, source_target_pairs={{0,96},{4,100},{8,104},{12,108},{16,112},{20,116},{24,120},{28,124... | collective-permute-start | bytes 589832 | tf_op jit(solution)/shard_map/ppermute | solution.py:333
  67.3 6.3 %collective-permute-start.5 = (f32[32,1536]{1,0:T(8,128)S(1)}, f32[32,1536]{1,0:T(8,128)S(1)}, u32[]{:S(2)}, u32[]{:S(2)}) collective-permute-start(f32[32,1536]{1,0:T(8,128)S(1)} %concatenate.27), channel_id=1, source_target_pairs={{0,64},{4,68},{8,72},{12,76},{16,80},{20,84},{24,88},{28,92},{32,9... | collective-permute-start | bytes 589832 | tf_op jit(solution)/shard_map/ppermute | solution.py:333
  67.9 7.5 %collective-permute-start.4 = (f32[32,1536]{1,0:T(8,128)S(1)}, f32[32,1536]{1,0:T(8,128)S(1)}, u32[]{:S(2)}, u32[]{:S(2)}) collective-permute-start(f32[32,1536]{1,0:T(8,128)S(1)} %concatenate.27), channel_id=1, source_target_pairs={{0,32},{4,36},{8,40},{12,44},{16,48},{20,52},{24,56},{28,60},{32,6... | collective-permute-start | bytes 589832 | tf_op jit(solution)/shard_map/ppermute | solution.py:333
  75.6 8.2 %copy-start = (f32[256,1536]{1,0:T(8,128)}, f32[256,1536]{1,0:T(8,128)S(1)}, u32[]{:S(2)}) copy-start(f32[256,1536]{1,0:T(8,128)S(1)} %concatenate.30.near_ref) | copy-start | bytes 4718596
  75.6 28.4 %collective-permute-start.15 = (f32[256,1536]{1,0:T(8,128)S(1)}, f32[256,1536]{1,0:T(8,128)S(1)}, u32[]{:S(2)}, u32[]{:S(2)}) collective-permute-start(f32[256,1536]{1,0:T(8,128)S(1)} %concatenate.30.near_ref), channel_id=1, source_target_pairs={{0,4},{4,0},{8,12},{12,8},{16,20},{20,16},{24,28},{28,24},{32,36},... | collective-permute-start | bytes 4718600 | tf_op jit(solution)/shard_map/ppermute | solution.py:348
  83.7 90.4 %all-to-all-start.1 = ((f32[128,4,2,8,128]{4,3,2,1,0:T(8,128)}), f32[128,4,2,8,128]{4,3,2,1,0:T(8,128)}, u32[]{:S(2)}, u32[]{:S(2)}) async-start(f32[128,4,2,8,128]{4,3,2,1,0:T(8,128)} %bitcast.24), calls=%async_computation.1 | async-start | bytes 8388608 | tf_op jit(solution)/shard_map/all_to_all | solution.py:390
  103.2 49.2 %copy-start.5 = (s32[4]{0:T(128)S(1)}, s32[4]{0:T(128)}, u32[]{:S(2)}) copy-start(s32[4]{0:T(128)} %pad_add_fusion.place_ref) | copy-start | bytes 52
  144.7 6.0 %collective-permute-start.16 = (f32[512,1536]{1,0:T(8,128)}, f32[512,1536]{1,0:T(8,128)S(1)}, u32[]{:S(2)}, u32[]{:S(2)}) collective-permute-start(f32[512,1536]{1,0:T(8,128)} %all-gather.2.cloned.1.call-done.mine_ref), channel_id=1, source_target_pairs={{0,4},{4,0},{8,12},{12,8},{16,20},{20,16},{24,28},{28,24},{32,36},... | collective-permute-start | bytes 9437192 | tf_op jit(solution)/shard_map/ppermute | solution.py:389
  (5 other events, 7.8 us)
Sparse Core Ops, SparseCore 0:
  42.7 102.0 all-gather.1
where the time goes:
time: 193 us; the launch traced here: 190 us
  Pallas kernels  67.5 us (35%)
  waiting for transfers between devices  55.2 us (29%)
  starting transfers between devices  43.1 us (22%)
  between operations  13.7 us (7%)
  local copies, waits for them, and re-layouts  8.53 us (4%)
    all_gather x1, waiting for transfers between devices, gather_factor(): lax.all_gather(shard, ('feat', 'pair'), axis_index_groups=groups, tiled=T...  34.1 us
    pallas_call x1, Pallas kernels, solve_and_update(): pl.pallas_call(solve_kernel, grid=(rows // width,), in_specs=[pl.BlockSpe...  21.7 us
    pallas_call x1, Pallas kernels, slot_gradients(): pl.pallas_call(gradient_kernel, grid_spec=pltpu.PrefetchScalarGridSpec(nu...  14.6 us
    ppermute x12, starting transfers between devices, along(): return lax.ppermute(value, 'feat', [(f, ring(f)) for f in range(n_feat)])  14.1 us
    ppermute x12, waiting for transfers between devices, along(): return lax.ppermute(value, 'feat', [(f, ring(f)) for f in range(n_feat)])  11.8 us
    pallas_call x1, Pallas kernels, split_factor(): pl.pallas_call(split_kernel, grid=(rows // 256,), in_specs=[block], out_s...  11.5 us
    all_to_all x1, starting transfers between devices, per_device(): lax.all_to_all(outgoing.reshape((n_feat,) + outgoing.shape[2:]), 'feat',...  9.56 us
    pallas_call x1, Pallas kernels, place_rows(): pl.pallas_call(place_kernel, grid=(total // rows,), in_specs=[pl.BlockSpe...  8.82 us
  transfers between devices with their start and end apart: 20, of which 13 were waited for; matrix products, arithmetic and copies ran while one was open for 1% of the time, Pallas kernels for 27%

commit v1 on v0

--- a/solution.py
+++ b/solution.py
@@ -203,29 +203,52 @@
     return dot(a[0], b[0]) + (dot(a[0], b[1]) + dot(a[1], b[0]))
 
 
-def arrange_kernel(pairs_ref, near_ref, far_ref, out_ref):
-    half = near_ref.shape[0]
+def arrange_kernel(place_ref, pairs_ref, near_ref, far_ref, right_ref, panels_ref):
+    blocks = near_ref.shape[0]
+    half = blocks * 8
+    core, pair, y, z = place_ref[2], place_ref[3], place_ref[4], place_ref[5]
     right = None
     for n, ref in enumerate((near_ref, far_ref)):
         chosen = one_hot(pairs_ref[:, n * half : (n + 1) * half], 0, 2 * half)
-        for part in split(ref[...]):
+        for part in split(ref[:, 16:, :].reshape(half, PANEL)):
             moved = jnp.dot(chosen, part, preferred_element_type=jnp.float32)
             right = moved if right is None else right + moved
-    out_ref[...] = right
-
-
-def arrange_rows(pairs, near, far):
-    half, width = near.shape
-    rows = pl.BlockSpec((half, PANEL), lambda k: (0, k))
+        kind = core if n == 0 else 1 - core
+        for block in range(blocks):
+            second, outer, inner = block // 16, block // 4 % 4, block % 4
+            y_back, z_back = (outer, inner) if second == 0 else (inner, outer)
+            chip = lax.rem(y + 4 - y_back, 4) * 4 + lax.rem(z + 4 - z_back, 4)
+            for j in range(2):
+                unit = chip * 4 + lax.rem(pair + 4 - (2 * second + j), 4)
+                rows = pl.ds(pl.multiple_of(unit * 8, 8), 8)
+                panels_ref[kind, rows, :] = ref[block, 8 * j : 8 * j + 8, :]
+    right_ref[...] = right
+
+
+def arrange_rows(place, pairs, near, far):
+    blocks, depth, width = near.shape
+    total = pairs.shape[1]
+    rows = pl.BlockSpec((blocks, depth, PANEL), lambda k: (0, 0, k))
     return pl.pallas_call(
         arrange_kernel,
         grid=(width // PANEL,),
-        in_specs=[pl.BlockSpec(pairs.shape, lambda k: (0, 0)), rows, rows],
-        out_specs=pl.BlockSpec((2 * half, PANEL), lambda k: (0, k)),
-        out_shape=jax.ShapeDtypeStruct((2 * half, width), jnp.float32),
+        in_specs=[
+            pl.BlockSpec(memory_space=pltpu.SMEM),
+            pl.BlockSpec(pairs.shape, lambda k: (0, 0)),
+            rows,
+            rows,
+        ],
+        out_specs=[
+            pl.BlockSpec((total, PANEL), lambda k: (0, k)),
+            pl.BlockSpec((2, PANEL, PANEL), lambda k: (0, 0, k)),
+        ],
+        out_shape=[
+            jax.ShapeDtypeStruct((total, width), jnp.float32),
+            jax.ShapeDtypeStruct((2, PANEL, width), jnp.float32),
+        ],
         compiler_params=pltpu.CompilerParams(vmem_limit_bytes=40 * 2**20),
         name="arrange_rows",
-    )(pairs, near, far)
+    )(place, pairs, near, far)
 
 
 def split_kernel(value_ref, high_ref, low_ref):
@@ -247,7 +270,7 @@
 
 
 def solve_kernel(
-    place_ref, right_ref, mine_ref, other_ref, factor_high_ref, factor_low_ref, out_ref,
+    place_ref, right_ref, panels_ref, factor_high_ref, factor_low_ref, out_ref,
     solved_ref, high_ref, low_ref,
 ):
     step = pl.program_id(0)
@@ -255,13 +278,9 @@
 
     @pl.when(step == 0)
     def _():
-        first_core = place_ref[2] == 0
-
-        def factor(k, below):
-            columns = slice(k * PANEL, (k + 1) * PANEL)
-            return split(
-                jnp.where(first_core != below, mine_ref[:, columns], other_ref[:, columns])
-            )
+
+        def factor(k, kind):
+            return split(panels_ref[kind, :, k * PANEL : (k + 1) * PANEL])
 
         for k in range(PANELS):
             columns = slice(k * PANEL, (k + 1) * PANEL)
@@ -269,8 +288,8 @@
             for j in range(k):
                 before = slice(j * PANEL, (j + 1) * PANEL)
                 solved = (high_ref[:, before], low_ref[:, before])
-                right -= dot_split(solved, factor(k * (k - 1) // 2 + j, True))
-            value = dot_split(split(right), factor(k, False))
+                right -= dot_split(solved, factor(k * (k - 1) // 2 + j, 1))
+            value = dot_split(split(right), factor(k, 0))
             solved_ref[k] = value
             high_ref[:, columns], low_ref[:, columns] = split(value)
 
@@ -285,7 +304,7 @@
             out_ref[...] = -solved_ref[place_ref[0], :, i * width : (i + 1) * width]
 
 
-def solve_and_update(place, right, mine, other, factor_parts):
+def solve_and_update(place, right, panels, factor_parts):
     rows, depth = factor_parts[0].shape
     total = right.shape[0]
     width = 256
@@ -297,8 +316,7 @@
         in_specs=[
             pl.BlockSpec(memory_space=pltpu.SMEM),
             whole(right),
-            whole(mine),
-            whole(other),
+            pl.BlockSpec(panels.shape, lambda i: (0, 0, 0)),
             block,
             block,
         ],
@@ -311,17 +329,7 @@
         ],
         compiler_params=pltpu.CompilerParams(vmem_limit_bytes=48 * 2**20),
         name="solve_and_update",
-    )(place, right, mine, other, *factor_parts)
-
-
-def gather_factor(arrived, feat, n_feat, n_pair):
-    first = jnp.concatenate([arrived[k, :, :PANEL] for k in range(3)], axis=1)
-    second = jnp.concatenate([arrived[1, :, :PANEL], arrived[2]], axis=1)
-    shard = jnp.where(feat % 2 == 0, first, second)
-    groups = [
-        [f * n_pair + p for f in range(c, n_feat, 2) for p in range(n_pair)] for c in range(2)
-    ]
-    return lax.all_gather(shard, ("feat", "pair"), axis_index_groups=groups, tiled=True)
+    )(place, right, panels, *factor_parts)
 
 
 def along(value, axis, shift):
@@ -333,18 +341,27 @@
     return lax.ppermute(value, "feat", [(f, ring(f)) for f in range(n_feat)])
 
 
-def gather_rows(panel_part, feat, pair, slot_pair):
+def gather_panels(arrived, panel_part, send, feat, pair, slot_pair):
     slots, width = panel_part.shape
+    first = jnp.concatenate([arrived[k, :, :PANEL] for k in range(3)], axis=1)
+    second = jnp.concatenate([arrived[1, :, :PANEL], arrived[2]], axis=1)
+    shard = jnp.where(feat % 2 == 0, first, second)
+    depth = shard.shape[0]
     groups = panel_part.reshape(4, slots // 4, width)
     piece = lambda k: lax.dynamic_index_in_dim(groups, (pair + k) % 4, 0, keepdims=False)
-    rows = jnp.concatenate([piece(0)] + [along(piece(k), "pair", k) for k in range(1, 4)], axis=0)
-    half = slots // 2
-    gathered = []
-    for part, axes in ((rows[:half], ("z", "y")), (rows[half:], ("y", "z"))):
-        for axis in axes:
-            part = jnp.concatenate([part] + [along(part, axis, k) for k in range(1, 4)], axis=0)
-        gathered.append(part)
-    near = jnp.concatenate(gathered, axis=0)
+    load = lambda k: jnp.concatenate([shard, piece(k)], axis=0)
+    pieces = [load(0)] + [along(load(k), "pair", k) for k in range(1, 4)]
+    halves = [
+        jnp.concatenate([v[:depth] for v in two] + [v[depth:] for v in two], axis=0)[None]
+        for two in (pieces[:2], pieces[2:])
+    ]
+    orders = (("z", "y"), ("y", "z"))
+    ring = lambda part, axis: jnp.concatenate(
+        [part] + [along(part, axis, k) for k in range(1, 4)], axis=0
+    )
+    halves = [ring(part, order[0]) for part, order in zip(halves, orders)]
+    halves, send = lax.optimization_barrier((halves, send))
+    near = jnp.concatenate([ring(part, order[1]) for part, order in zip(halves, orders)], axis=0)
     far = lax.ppermute(near, "feat", [(f, f ^ 1) for f in range(lax.axis_size("feat"))])
     n = lax.broadcasted_iota(jnp.int32, (128, 128), 0)
     other_core, second, outer, inner, back = n // 64, n // 32 % 2, n // 8 % 4, n // 2 % 4, n % 2
@@ -359,7 +376,7 @@
     table = slot_pair.reshape(128, slots // 4).astype(jnp.float32)
     pairs = jnp.dot(chosen, table, precision=HIGHEST, preferred_element_type=jnp.float32)
     pairs = jnp.round(pairs).astype(jnp.int32).reshape(1, 32 * slots)
-    return near, far, pairs
+    return near, far, pairs, send
 
 
 def per_device(in_factors, out_factors, token_counts, slot_pair, factor_panels):
@@ -373,6 +390,7 @@
 
     place = jnp.stack(
         [jnp.minimum(feat, PANELS - 1), (feat < PANELS).astype(jnp.int32), feat % 2, pair]
+        + [feat // 8, feat // 2 % 4]
     ).astype(jnp.int32)
     outgoing = invert_and_cut(place, factor_panels, n_feat, n_pair)
     arrived = lax.all_to_all(
@@ -380,13 +398,7 @@
     )
     send, panel_part = slot_gradients(token_counts, out_factors, in_factors, n_feat, n_pair)
     arrived, panel_part = lax.optimization_barrier((arrived, panel_part))
-    mine = gather_factor(arrived, feat, n_feat, n_pair)
-    near, far, pairs = gather_rows(panel_part, feat, pair, slot_pair)
-    send, near = lax.optimization_barrier((send, near))
-    right = arrange_rows(pairs, near, far)
-    parts = split_factor(factor_panels)
-    mine, right, parts = lax.optimization_barrier((mine, right, parts))
-    other = lax.ppermute(mine, "feat", [(f, f ^ 1) for f in range(n_feat)])
+    near, far, pairs, send = gather_panels(arrived, panel_part, send, feat, pair, slot_pair)
     received = lax.all_to_all(
         send.reshape((n_feat * n_pair,) + send.shape[2:]),
         ("feat", "pair"),
@@ -394,7 +406,9 @@
         concat_axis=0,
         tiled=True,
     ).reshape(total * (rank // 128) * (rank // n_feat), 128)
-    update = solve_and_update(place, right, mine, other, parts)
+    right, panels = arrange_rows(place, pairs, near, far)
+    parts = split_factor(factor_panels)
+    update = solve_and_update(place, right, panels, parts)
     return place_rows(place, slot_pair, received, update)
 
 

time: 193 us -> 170 us (0.88); the launches traced: 190 us -> 169 us
  waiting for transfers between devices: 55.2 us -> 34.7 us
  between operations: 13.7 us -> 0.34 us
  starting transfers between devices: 43.1 us -> 50.3 us
  Pallas kernels: 67.5 us -> 72.9 us
    all_gather x1 -> x0, waiting for transfers between devices: 34.1 us -> none  [gather_factor(): lax.all_gather(shard, ('feat', 'pair'), axis_index_groups=groups, tiled=T...]
    ppermute x12, waiting for transfers between devices: 11.8 us -> 23 us  [along(): return lax.ppermute(value, 'feat', [(f, ring(f)) for f in range(n_feat)])]
    all_to_all x1, waiting for transfers between devices: 0.01 us -> 10.8 us  [per_device(): lax.all_to_all(send.reshape((n_feat * n_pair,) + send.shape[2:]), ('feat'...]
    pallas_call x1, Pallas kernels: 2.62 us -> 8.44 us  [arrange_rows(): pl.pallas_call(arrange_kernel, grid=(width // PANEL,), in_specs=[pl.Block...]
    ppermute x2 -> x1, waiting for transfers between devices: 5.5 us -> 0.01 us  [gather_panels(): lax.ppermute(near, 'feat', [(f, f ^ 1) for f in range(lax.axis_size('feat...]
    ppermute x3, waiting for transfers between devices: 3.67 us -> 0.66 us  [along(): return lax.ppermute(value, 'pair', [(p, (p + shift) % 4) for p in range(4)])]
    ppermute x12, starting transfers between devices: 14.1 us -> 16.7 us  [along(): return lax.ppermute(value, 'feat', [(f, ring(f)) for f in range(n_feat)])]
    ppermute x2 -> x1, starting transfers between devices: 8.6 us -> 10.3 us  [gather_panels(): lax.ppermute(near, 'feat', [(f, f ^ 1) for f in range(lax.axis_size('feat...]
  transfers between devices with their start and end apart: 20 -> 18, of which waited for: 13 -> 9; matrix products, arithmetic and copies ran while one was open for 1% -> 4% of each run, Pallas kernels for 27% -> 33%
where the time goes in v1:
time: 170 us; the launch traced here: 169 us
  Pallas kernels  72.9 us (43%)
  starting transfers between devices  50.3 us (30%)
  waiting for transfers between devices  34.7 us (20%)
  local copies, waits for them, and re-layouts  10.3 us (6%)
    ppermute x12, waiting for transfers between devices, along(): return lax.ppermute(value, 'feat', [(f, ring(f)) for f in range(n_feat)])  23 us
    pallas_call x1, Pallas kernels, solve_and_update(): pl.pallas_call(solve_kernel, grid=(rows // width,), in_specs=[pl.BlockSpe...  21.4 us
    ppermute x12, starting transfers between devices, along(): return lax.ppermute(value, 'feat', [(f, ring(f)) for f in range(n_feat)])  16.7 us
    pallas_call x1, Pallas kernels, slot_gradients(): pl.pallas_call(gradient_kernel, grid_spec=pltpu.PrefetchScalarGridSpec(nu...  14.6 us
    pallas_call x1, Pallas kernels, split_factor(): pl.pallas_call(split_kernel, grid=(rows // 256,), in_specs=[block], out_s...  11.4 us
    all_to_all x1, waiting for transfers between devices, per_device(): lax.all_to_all(send.reshape((n_feat * n_pair,) + send.shape[2:]), ('feat'...  10.8 us
    ppermute x1, starting transfers between devices, gather_panels(): lax.ppermute(near, 'feat', [(f, f ^ 1) for f in range(lax.axis_size('feat...  10.3 us
    all_to_all x1, starting transfers between devices, per_device(): lax.all_to_all(outgoing.reshape((n_feat,) + outgoing.shape[2:]), 'feat',...  9.56 us
  transfers between devices with their start and end apart: 18, of which 9 were waited for; matrix products, arithmetic and copies ran while one was open for 4% of the time, Pallas kernels for 33%

profile of v1, /device:TPU:1, one launch (start us, length us, event | category | flops | bytes accessed | tf_op | source)
XLA Modules:
  0.0 169.2 jit_solution(17406488402743045583)
XLA Ops:
  0.7 8.3 %invert_and_cut.1 = f32[16,2,8,1024]{3,2,1,0:T(8,128)} custom-call(s32[6]{0:T(128)} %stack.31.place_ref, f32[2048,1536]{1,0:T(8,128)} %value_ref.1), custom_call_target="tpu_custom_call" | custom-call | tf_op jit(solution)/shard_map/invert_and_cut/pallas_call | solution.py:118
  8.9 9.6 %all-to-all-start = ((f32[32,8,1024]{2,1,0:T(8,128)}), f32[32,8,1024]{2,1,0:T(8,128)S(1)}, u32[]{:S(2)}, u32[]{:S(2)}) async-start(f32[32,8,1024]{2,1,0:T(8,128)} %bitcast.31), calls=%async_computation | async-start | bytes 2097152 | tf_op jit(solution)/shard_map/all_to_all | solution.py:396
  18.7 14.6 %slot_gradients.1 = (f32[32,4,4,2,8,128]{5,4,3,2,1,0:T(8,128)S(1)}, f32[16,1536]{1,0:T(8,128)S(1)}) custom-call(s32[16,2]{1,0:T(8,128)S(1)} %copy.8.counts_ref, bf16[16,2,512,256]{3,2,1,0:T(8,128)(2,1)} %out_ref.1, bf16[16,2,512,256]{3,2,1,0:T(8,128)(2,1)} %in_ref.1), custom_call_target="tpu_custom_call" | custom-call | flops 2147483648 | bytes 25165824 | tf_op jit(solution)/shard_map/slot_gradients/pallas_call | solution.py:42
  33.3 2.0 %copy-done = f32[32,4,4,2,8,128]{5,4,3,2,1,0:T(8,128)} copy-done((f32[32,4,4,2,8,128]{5,4,3,2,1,0:T(8,128)}, f32[32,4,4,2,8,128]{5,4,3,2,1,0:T(8,128)S(1)}, u32[]{:S(2)}) %copy-start) | copy-done | bytes 4194328
  35.6 1.3 collective-permute-start
  36.8 2.5 %collective-permute-start.4 = (f32[12,1536]{1,0:T(8,128)S(1)}, f32[12,1536]{1,0:T(8,128)S(1)}, u32[]{:S(2)}, u32[]{:S(2)}) collective-permute-start(f32[12,1536]{1,0:T(8,128)S(1)} %get-tuple-element.34), channel_id=1, source_target_pairs={{0,2},{1,3},{2,0},{3,1},{4,6},{5,7},{6,4},{7,5},{8,10},{9,11},{10,... | collective-permute-start | bytes 221192 | tf_op jit(solution)/shard_map/ppermute | solution.py:337
  39.3 1.1 collective-permute-start.5
  41.1 2.3 %collective-permute-start.3 = (f32[1,24,1536]{2,1,0:T(8,128)S(1)}, f32[1,24,1536]{2,1,0:T(8,128)S(1)}, u32[]{:S(2)}, u32[]{:S(2)}) collective-permute-start(f32[1,24,1536]{2,1,0:T(8,128)S(1)} %maximum_bitcast_fusion), channel_id=1, source_target_pairs={{0,24},{4,28},{8,0},{12,4},{16,8},{20,12},{24,16},{28,20},{32,56},... | collective-permute-start | bytes 442376 | tf_op jit(solution)/shard_map/ppermute | solution.py:341
  44.6 2.6 %collective-permute-start.8 = (f32[1,24,1536]{2,1,0:T(8,128)S(1)}, f32[1,24,1536]{2,1,0:T(8,128)S(1)}, u32[]{:S(2)}, u32[]{:S(2)}) collective-permute-start(f32[1,24,1536]{2,1,0:T(8,128)S(1)} %maximum_bitcast_fusion.1), channel_id=1, source_target_pairs={{0,96},{4,100},{8,104},{12,108},{16,112},{20,116},{24,120},{28,124... | collective-permute-start | bytes 442376 | tf_op jit(solution)/shard_map/ppermute | solution.py:341
  49.0 4.2 %collective-permute-done.1 = f32[1,24,1536]{2,1,0:T(8,128)S(1)} collective-permute-done((f32[1,24,1536]{2,1,0:T(8,128)S(1)}, f32[1,24,1536]{2,1,0:T(8,128)S(1)}, u32[]{:S(2)}, u32[]{:S(2)}) %collective-permute-start.1) | collective-permute-done | bytes 147488 | tf_op jit(solution)/shard_map/ppermute | solution.py:341
  53.3 1.6 collective-permute-done.6
  55.0 2.1 %collective-permute-start.10 = (f32[4,24,1536]{2,1,0:T(8,128)S(1)}, f32[4,24,1536]{2,1,0:T(8,128)S(1)}, u32[]{:S(2)}, u32[]{:S(2)}) collective-permute-start(f32[4,24,1536]{2,1,0:T(8,128)S(1)} %pad_maximum_fusion), channel_id=1, source_target_pairs={{0,64},{4,68},{8,72},{12,76},{16,80},{20,84},{24,88},{28,92},{32,9... | collective-permute-start | bytes 1769480 | tf_op jit(solution)/shard_map/ppermute | solution.py:341
  58.2 2.8 %collective-permute-start.14 = (f32[4,24,1536]{2,1,0:T(8,128)S(1)}, f32[4,24,1536]{2,1,0:T(8,128)S(1)}, u32[]{:S(2)}, u32[]{:S(2)}) collective-permute-start(f32[4,24,1536]{2,1,0:T(8,128)S(1)} %pad_maximum_fusion.1), channel_id=1, source_target_pairs={{0,24},{4,28},{8,0},{12,4},{16,8},{20,12},{24,16},{28,20},{32,56},... | collective-permute-start | bytes 1769480 | tf_op jit(solution)/shard_map/ppermute | solution.py:341
  62.5 5.3 %collective-permute-done.9 = f32[4,24,1536]{2,1,0:T(8,128)S(1)} collective-permute-done((f32[4,24,1536]{2,1,0:T(8,128)S(1)}, f32[4,24,1536]{2,1,0:T(8,128)S(1)}, u32[]{:S(2)}, u32[]{:S(2)}) %collective-permute-start.9) | collective-permute-done | bytes 589856 | tf_op jit(solution)/shard_map/ppermute | solution.py:341
  67.8 2.9 %collective-permute-start.12 = (f32[4,24,1536]{2,1,0:T(8,128)S(1)}, f32[4,24,1536]{2,1,0:T(8,128)S(1)}, u32[]{:S(2)}, u32[]{:S(2)}) collective-permute-start(f32[4,24,1536]{2,1,0:T(8,128)S(1)} %pad_maximum_fusion.1), channel_id=1, source_target_pairs={{0,8},{4,12},{8,16},{12,20},{16,24},{20,28},{24,0},{28,4},{32,40},... | collective-permute-start | bytes 1769480 | tf_op jit(solution)/shard_map/ppermute | solution.py:341
  71.6 8.9 %collective-permute-done.10 = f32[4,24,1536]{2,1,0:T(8,128)S(1)} collective-permute-done((f32[4,24,1536]{2,1,0:T(8,128)S(1)}, f32[4,24,1536]{2,1,0:T(8,128)S(1)}, u32[]{:S(2)}, u32[]{:S(2)}) %collective-permute-start.10) | collective-permute-done | bytes 589856 | tf_op jit(solution)/shard_map/ppermute | solution.py:341
  81.4 2.3 %collective-permute-done.11 = f32[4,24,1536]{2,1,0:T(8,128)S(1)} collective-permute-done((f32[4,24,1536]{2,1,0:T(8,128)S(1)}, f32[4,24,1536]{2,1,0:T(8,128)S(1)}, u32[]{:S(2)}, u32[]{:S(2)}) %collective-permute-start.11) | collective-permute-done | bytes 589856 | tf_op jit(solution)/shard_map/ppermute | solution.py:341
  88.0 10.3 %collective-permute-start.15 = (f32[32,24,1536]{2,1,0:T(8,128)}, f32[32,24,1536]{2,1,0:T(8,128)}, u32[]{:S(2)}, u32[]{:S(2)}) collective-permute-start(f32[32,24,1536]{2,1,0:T(8,128)} %constant_dynamic-update-slice_fusion.near_ref), channel_id=1, source_target_pairs={{0,4},{4,0},{8,12},{12,8},{16,20},{20,16},{24,28},{28,24},{32,36},... | collective-permute-start | bytes 14155784 | tf_op jit(solution)/shard_map/ppermute | solution.py:365
  98.3 9.0 %all-to-all-start.1 = ((f32[128,4,2,8,128]{4,3,2,1,0:T(8,128)}), f32[128,4,2,8,128]{4,3,2,1,0:T(8,128)}, u32[]{:S(2)}, u32[]{:S(2)}) async-start(f32[128,4,2,8,128]{4,3,2,1,0:T(8,128)} %bitcast.30), calls=%async_computation.1 | async-start | bytes 8388608 | tf_op jit(solution)/shard_map/all_to_all | solution.py:402
  107.3 11.4 %split_factor.1 = (bf16[2048,1536]{1,0:T(8,128)(2,1)}, bf16[2048,1536]{1,0:T(8,128)(2,1)}) custom-call(f32[2048,1536]{1,0:T(8,128)} %value_ref.1), custom_call_target="tpu_custom_call" | custom-call | tf_op jit(solution)/shard_map/split_factor/pallas_call | solution.py:261
  119.7 8.4 %arrange_rows.1 = (f32[512,1536]{1,0:T(8,128)S(1)}, f32[2,512,1536]{2,1,0:T(8,128)}) custom-call(s32[6]{0:T(128)S(1)} %copy-done.1, s32[1,512]{1,0:T(1,128)S(1)} %reshape.21.pairs_ref, f32[32,24,1536]{2,1,0:T(8,128)} %constant_dynamic-update-slice_fusion.near_ref, f32[32,24,1536]{2,1,0:T(8,128)} %collective-permute-done.15.far_ref), custom_call_target="tpu_custom_call" | custom-call | tf_op jit(solution)/shard_map/arrange_rows/pallas_call | solution.py:232
  128.1 21.4 %solve_and_update.1.update_ref = f32[512,2048]{1,0:T(8,128)} custom-call(s32[6]{0:T(128)S(1)} %copy-done.1, f32[512,1536]{1,0:T(8,128)S(1)} %get-tuple-element.23.right_ref, f32[2,512,1536]{2,1,0:T(8,128)} %get-tuple-element.24.panels_ref, bf16[2048,1536]{1,0:T(8,128)(2,1)} %get-tuple-element.25.factor_high_ref, ...), custom_call_target="tpu_custom_call" | custom-call | tf_op jit(solution)/shard_map/solve_and_update/pallas_call | solution.py:313
  149.5 10.8 %all-to-all-done.1 = f32[128,4,2,8,128]{4,3,2,1,0:T(8,128)} async-done(((f32[128,4,2,8,128]{4,3,2,1,0:T(8,128)}), f32[128,4,2,8,128]{4,3,2,1,0:T(8,128)}, u32[]{:S(2)}, u32[]{:S(2)}) %all-to-all-start.1) | async-done | bytes 4194336 | tf_op jit(solution)/shard_map/all_to_all | solution.py:402
  160.4 8.8 %place_rows.1 = f32[512,2048]{1,0:T(8,128)} custom-call(s32[6]{0:T(128)S(1)} %copy-done.1, s32[1,512]{1,0:T(1,128)S(1)} %copy-done.2, f32[8192,128]{1,0:T(8,128)} %bitcast.18.received_ref, f32[512,2048]{1,0:T(8,128)} %solve_and_update.1.update_ref), custom_call_target="tpu_custom_call" | custom-call | tf_op jit(solution)/shard_map/place_rows/pallas_call | solution.py:179
  (65 shorter events, 14.6 us)
Async XLA Ops:
  0.7 17.9 %copy-start.3 = (s32[16,2]{0,1:T(2,128)S(1)}, s32[16,2]{0,1:T(2,128)}, u32[]{:S(2)}) copy-start(s32[16,2]{0,1:T(2,128)} %param.7) | copy-start | bytes 388
  8.9 26.5 %all-to-all-start = ((f32[32,8,1024]{2,1,0:T(8,128)}), f32[32,8,1024]{2,1,0:T(8,128)S(1)}, u32[]{:S(2)}, u32[]{:S(2)}) async-start(f32[32,8,1024]{2,1,0:T(8,128)} %bitcast.31), calls=%async_computation | async-start | bytes 2097152 | tf_op jit(solution)/shard_map/all_to_all | solution.py:396
  33.2 2.0 %copy-start = (f32[32,4,4,2,8,128]{5,4,3,2,1,0:T(8,128)}, f32[32,4,4,2,8,128]{5,4,3,2,1,0:T(8,128)S(1)}, u32[]{:S(2)}) copy-start(f32[32,4,4,2,8,128]{5,4,3,2,1,0:T(8,128)S(1)} %get-tuple-element.20) | copy-start | bytes 12582916
  35.6 5.5 %collective-permute-start = (f32[12,1536]{1,0:T(8,128)S(1)}, f32[12,1536]{1,0:T(8,128)S(1)}, u32[]{:S(2)}, u32[]{:S(2)}) collective-permute-start(f32[12,1536]{1,0:T(8,128)S(1)} %get-tuple-element.36), channel_id=1, source_target_pairs={{0,1},{1,2},{2,3},{3,0},{4,5},{5,6},{6,7},{7,4},{8,9},{9,10},{10,1... | collective-permute-start | bytes 221192 | tf_op jit(solution)/shard_map/ppermute | solution.py:337
  36.8 7.7 %collective-permute-start.4 = (f32[12,1536]{1,0:T(8,128)S(1)}, f32[12,1536]{1,0:T(8,128)S(1)}, u32[]{:S(2)}, u32[]{:S(2)}) collective-permute-start(f32[12,1536]{1,0:T(8,128)S(1)} %get-tuple-element.34), channel_id=1, source_target_pairs={{0,2},{1,3},{2,0},{3,1},{4,6},{5,7},{6,4},{7,5},{8,10},{9,11},{10,... | collective-permute-start | bytes 221192 | tf_op jit(solution)/shard_map/ppermute | solution.py:337
  39.3 5.3 %collective-permute-start.5 = (f32[12,1536]{1,0:T(8,128)S(1)}, f32[12,1536]{1,0:T(8,128)S(1)}, u32[]{:S(2)}, u32[]{:S(2)}) collective-permute-start(f32[12,1536]{1,0:T(8,128)S(1)} %get-tuple-element.35), channel_id=1, source_target_pairs={{0,3},{1,0},{2,1},{3,2},{4,7},{5,4},{6,5},{7,6},{8,11},{9,8},{10,9... | collective-permute-start | bytes 221192 | tf_op jit(solution)/shard_map/ppermute | solution.py:337
  41.1 6.6 %collective-permute-start.3 = (f32[1,24,1536]{2,1,0:T(8,128)S(1)}, f32[1,24,1536]{2,1,0:T(8,128)S(1)}, u32[]{:S(2)}, u32[]{:S(2)}) collective-permute-start(f32[1,24,1536]{2,1,0:T(8,128)S(1)} %maximum_bitcast_fusion), channel_id=1, source_target_pairs={{0,24},{4,28},{8,0},{12,4},{16,8},{20,12},{24,16},{28,20},{32,56},... | collective-permute-start | bytes 442376 | tf_op jit(solution)/shard_map/ppermute | solution.py:341
  43.4 5.6 %collective-permute-start.2 = (f32[1,24,1536]{2,1,0:T(8,128)S(1)}, f32[1,24,1536]{2,1,0:T(8,128)S(1)}, u32[]{:S(2)}, u32[]{:S(2)}) collective-permute-start(f32[1,24,1536]{2,1,0:T(8,128)S(1)} %maximum_bitcast_fusion), channel_id=1, source_target_pairs={{0,16},{4,20},{8,24},{12,28},{16,0},{20,4},{24,8},{28,12},{32,48},... | collective-permute-start | bytes 442376 | tf_op jit(solution)/shard_map/ppermute | solution.py:341
  44.0 9.2 %collective-permute-start.1 = (f32[1,24,1536]{2,1,0:T(8,128)S(1)}, f32[1,24,1536]{2,1,0:T(8,128)S(1)}, u32[]{:S(2)}, u32[]{:S(2)}) collective-permute-start(f32[1,24,1536]{2,1,0:T(8,128)S(1)} %maximum_bitcast_fusion), channel_id=1, source_target_pairs={{0,8},{4,12},{8,16},{12,20},{16,24},{20,28},{24,0},{28,4},{32,40},... | collective-permute-start | bytes 442376 | tf_op jit(solution)/shard_map/ppermute | solution.py:341
  44.6 8.6 %collective-permute-start.8 = (f32[1,24,1536]{2,1,0:T(8,128)S(1)}, f32[1,24,1536]{2,1,0:T(8,128)S(1)}, u32[]{:S(2)}, u32[]{:S(2)}) collective-permute-start(f32[1,24,1536]{2,1,0:T(8,128)S(1)} %maximum_bitcast_fusion.1), channel_id=1, source_target_pairs={{0,96},{4,100},{8,104},{12,108},{16,112},{20,116},{24,120},{28,124... | collective-permute-start | bytes 442376 | tf_op jit(solution)/shard_map/ppermute | solution.py:341
  47.2 6.1 %collective-permute-start.7 = (f32[1,24,1536]{2,1,0:T(8,128)S(1)}, f32[1,24,1536]{2,1,0:T(8,128)S(1)}, u32[]{:S(2)}, u32[]{:S(2)}) collective-permute-start(f32[1,24,1536]{2,1,0:T(8,128)S(1)} %maximum_bitcast_fusion.1), channel_id=1, source_target_pairs={{0,64},{4,68},{8,72},{12,76},{16,80},{20,84},{24,88},{28,92},{32,9... | collective-permute-start | bytes 442376 | tf_op jit(solution)/shard_map/ppermute | solution.py:341
  47.7 7.2 %collective-permute-start.6 = (f32[1,24,1536]{2,1,0:T(8,128)S(1)}, f32[1,24,1536]{2,1,0:T(8,128)S(1)}, u32[]{:S(2)}, u32[]{:S(2)}) collective-permute-start(f32[1,24,1536]{2,1,0:T(8,128)S(1)} %maximum_bitcast_fusion.1), channel_id=1, source_target_pairs={{0,32},{4,36},{8,40},{12,44},{16,48},{20,52},{24,56},{28,60},{32,6... | collective-permute-start | bytes 442376 | tf_op jit(solution)/shard_map/ppermute | solution.py:341
  54.9 12.9 %collective-permute-start.9 = (f32[4,24,1536]{2,1,0:T(8,128)S(1)}, f32[4,24,1536]{2,1,0:T(8,128)S(1)}, u32[]{:S(2)}, u32[]{:S(2)}) collective-permute-start(f32[4,24,1536]{2,1,0:T(8,128)S(1)} %pad_maximum_fusion), channel_id=1, source_target_pairs={{0,32},{4,36},{8,40},{12,44},{16,48},{20,52},{24,56},{28,60},{32,6... | collective-permute-start | bytes 1769480 | tf_op jit(solution)/shard_map/ppermute | solution.py:341
  55.0 25.5 %collective-permute-start.10 = (f32[4,24,1536]{2,1,0:T(8,128)S(1)}, f32[4,24,1536]{2,1,0:T(8,128)S(1)}, u32[]{:S(2)}, u32[]{:S(2)}) collective-permute-start(f32[4,24,1536]{2,1,0:T(8,128)S(1)} %pad_maximum_fusion), channel_id=1, source_target_pairs={{0,64},{4,68},{8,72},{12,76},{16,80},{20,84},{24,88},{28,92},{32,9... | collective-permute-start | bytes 1769480 | tf_op jit(solution)/shard_map/ppermute | solution.py:341
  57.1 26.6 %collective-permute-start.11 = (f32[4,24,1536]{2,1,0:T(8,128)S(1)}, f32[4,24,1536]{2,1,0:T(8,128)S(1)}, u32[]{:S(2)}, u32[]{:S(2)}) collective-permute-start(f32[4,24,1536]{2,1,0:T(8,128)S(1)} %pad_maximum_fusion), channel_id=1, source_target_pairs={{0,96},{4,100},{8,104},{12,108},{16,112},{20,116},{24,120},{28,124... | collective-permute-start | bytes 1769480 | tf_op jit(solution)/shard_map/ppermute | solution.py:341
  58.2 29.0 %collective-permute-start.14 = (f32[4,24,1536]{2,1,0:T(8,128)S(1)}, f32[4,24,1536]{2,1,0:T(8,128)S(1)}, u32[]{:S(2)}, u32[]{:S(2)}) collective-permute-start(f32[4,24,1536]{2,1,0:T(8,128)S(1)} %pad_maximum_fusion.1), channel_id=1, source_target_pairs={{0,24},{4,28},{8,0},{12,4},{16,8},{20,12},{24,16},{28,20},{32,56},... | collective-permute-start | bytes 1769480 | tf_op jit(solution)/shard_map/ppermute | solution.py:341
  61.0 25.3 %collective-permute-start.13 = (f32[4,24,1536]{2,1,0:T(8,128)S(1)}, f32[4,24,1536]{2,1,0:T(8,128)S(1)}, u32[]{:S(2)}, u32[]{:S(2)}) collective-permute-start(f32[4,24,1536]{2,1,0:T(8,128)S(1)} %pad_maximum_fusion.1), channel_id=1, source_target_pairs={{0,16},{4,20},{8,24},{12,28},{16,0},{20,4},{24,8},{28,12},{32,48},... | collective-permute-start | bytes 1769480 | tf_op jit(solution)/shard_map/ppermute | solution.py:341
  67.8 17.6 %collective-permute-start.12 = (f32[4,24,1536]{2,1,0:T(8,128)S(1)}, f32[4,24,1536]{2,1,0:T(8,128)S(1)}, u32[]{:S(2)}, u32[]{:S(2)}) collective-permute-start(f32[4,24,1536]{2,1,0:T(8,128)S(1)} %pad_maximum_fusion.1), channel_id=1, source_target_pairs={{0,8},{4,12},{8,16},{12,20},{16,24},{20,28},{24,0},{28,4},{32,40},... | collective-permute-start | bytes 1769480 | tf_op jit(solution)/shard_map/ppermute | solution.py:341
  88.0 31.6 %collective-permute-start.15 = (f32[32,24,1536]{2,1,0:T(8,128)}, f32[32,24,1536]{2,1,0:T(8,128)}, u32[]{:S(2)}, u32[]{:S(2)}) collective-permute-start(f32[32,24,1536]{2,1,0:T(8,128)} %constant_dynamic-update-slice_fusion.near_ref), channel_id=1, source_target_pairs={{0,4},{4,0},{8,12},{12,8},{16,20},{20,16},{24,28},{28,24},{32,36},... | collective-permute-start | bytes 14155784 | tf_op jit(solution)/shard_map/ppermute | solution.py:365
  98.3 62.1 %all-to-all-start.1 = ((f32[128,4,2,8,128]{4,3,2,1,0:T(8,128)}), f32[128,4,2,8,128]{4,3,2,1,0:T(8,128)}, u32[]{:S(2)}, u32[]{:S(2)}) async-start(f32[128,4,2,8,128]{4,3,2,1,0:T(8,128)} %bitcast.30), calls=%async_computation.1 | async-start | bytes 8388608 | tf_op jit(solution)/shard_map/all_to_all | solution.py:402
  107.3 11.4 %copy-start.2 = (s32[1,512]{1,0:T(1,128)S(1)}, s32[1,512]{1,0:T(1,128)}, u32[]{:S(2)}) copy-start(s32[1,512]{1,0:T(1,128)} %pairs_ref.1) | copy-start | bytes 6148
  107.3 12.4 %copy-start.1 = (s32[6]{0:T(128)S(1)}, s32[6]{0:T(128)}, u32[]{:S(2)}) copy-start(s32[6]{0:T(128)} %stack.31.place_ref) | copy-start | bytes 76

commit v2 on v1

v2 whole, which is shorter than its diff:
```python
import jax
import jax.numpy as jnp
from jax import lax
from jax.experimental import pallas as pl
from jax.experimental.pallas import tpu as pltpu
from jax.sharding import PartitionSpec as P

PANEL = 512
PANELS = 3
HIGHEST = lax.Precision.HIGHEST
SMALL = pl.CostEstimate(flops=1, bytes_accessed=1, transcendentals=0)


def gradient_kernel(counts_ref, out_ref, in_ref, send_ref, panel_ref):
    slot = pl.program_id(0)
    depth, rank = out_ref.shape[2:]
    position = lax.broadcasted_iota(jnp.int32, (depth, 128), 0)
    total = None
    for side in range(2):
        kept = jnp.where(position < counts_ref[slot, side], 1.0, 0.0).astype(jnp.bfloat16)
        weights = jnp.concatenate([kept] * (rank // 128), axis=1)
        product = lax.dot_general(
            out_ref[0, side] * weights,
            in_ref[0, side],
            (((0,), (0,)), ((), ())),
            preferred_element_type=jnp.float32,
        )
        total = product if side == 0 else total - product
    feats, _, _, lanes, parts, lane = send_ref.shape
    for h in range(lanes):
        columns = total[:, h * lane : (h + 1) * lane]
        send_ref[:, 0, 0, h] = columns.reshape(feats, parts, lane)
    for k in range(PANELS):
        for i in range(PANEL // rank):
            columns = slice(k * PANEL + i * rank, k * PANEL + (i + 1) * rank)
            panel_ref[pl.ds(slot, 1), columns] = total[8 * k + i : 8 * k + i + 1, :]


def slot_gradients(token_counts, out_factors, in_factors, n_feat, n_pair):
    slots, sides, depth, rank = in_factors.shape
    per_group = slots // n_pair
    factors = pl.BlockSpec((1, sides, depth, rank), lambda k, counts: (k, 0, 0, 0))
    return pl.pallas_call(
        gradient_kernel,
        grid_spec=pltpu.PrefetchScalarGridSpec(
            num_scalar_prefetch=1,
            grid=(slots,),
            in_specs=[factors, factors],
            out_specs=[
                pl.BlockSpec(
                    (n_feat, 1, 1, rank // 128, rank // n_feat, 128),
                    lambda k, counts: (0, k // per_group, k % per_group, 0, 0, 0),
                ),
                pl.BlockSpec((slots, PANELS * PANEL), lambda k, counts: (0, 0)),
            ],
        ),
        out_shape=[
            jax.ShapeDtypeStruct(
                (n_feat, n_pair, per_group, rank // 128, rank // n_feat, 128), jnp.float32
            ),
            jax.ShapeDtypeStruct((slots, PANELS * PANEL), jnp.float32),
        ],
        compiler_params=pltpu.CompilerParams(vmem_limit_bytes=60 * 2**20),
        cost_estimate=pl.CostEstimate(
            flops=2 * slots * sides * depth * rank * rank, bytes_accessed=24 * 2**20, transcendentals=0
        ),
        name="slot_gradients",
    )(token_counts, out_factors, in_factors)


def cut_kernel(place_ref, panel_ref, send_ref):
    chips, _, depth, _ = send_ref.shape
    groups = PANEL // (chips * depth)
    for chip in range(chips):
        rows = pl.ds(pl.multiple_of((chip * groups + place_ref[3]) * depth, depth), depth)
        diagonal = panel_ref[rows, (PANELS - 1) * PANEL :]
        for k in range(PANELS - 1):
            diagonal = jnp.where(
                place_ref[0] == k, panel_ref[rows, k * PANEL : (k + 1) * PANEL], diagonal
            )
        send_ref[chip, 0, :, :PANEL] = diagonal
        send_ref[chip, 0, :, PANEL:] = jnp.zeros((depth, PANEL), jnp.float32)
        send_ref[chip, 1] = panel_ref[rows, : 2 * PANEL]


def cut_panel(place, factor_panels, n_feat, n_pair):
    width = factor_panels.shape[1]
    chips = n_feat // 2
    depth = PANEL // (chips * n_pair)
    return pl.pallas_call(
        cut_kernel,
        grid=(1,),
        in_specs=[
            pl.BlockSpec(memory_space=pltpu.SMEM),
            pl.BlockSpec((PANEL, width), lambda i: (0, 0)),
        ],
        out_specs=pl.BlockSpec((chips, 2, depth, 2 * PANEL), lambda i: (0, 0, 0, 0)),
        out_shape=jax.ShapeDtypeStruct((chips, 2, depth, 2 * PANEL), jnp.float32),
        compiler_params=pltpu.CompilerParams(vmem_limit_bytes=60 * 2**20),
        name="cut_panel",
    )(place, factor_panels)


def invert_kernel(d_ref, x_ref):
    def dot(a, b):
        return jnp.dot(a, b, precision=HIGHEST, preferred_element_type=jnp.float32)

    base = 128
    row = lax.broadcasted_iota(jnp.int32, (base, base), 0)
    col = lax.broadcasted_iota(jnp.int32, (base, base), 1)
    spots = [
        (slice(n, n + base), slice(k * PANEL + n, k * PANEL + n + base))
        for k in range(PANELS)
        for n in range(0, PANEL, base)
    ]
    blocks = [d_ref[0, r, c] for r, c in spots]
    inverses = [jnp.where(row == col, 1.0 / jnp.where(row == col, b, 1.0), 0.0) for b in blocks]
    size = 1
    while size < base:
        joins = (row // (2 * size) == col // (2 * size)) & (row // size != col // size) & (row > col)
        inner = [dot(jnp.where(joins, b, 0.0), x) for b, x in zip(blocks, inverses)]
        inverses = [x - dot(x, y) for x, y in zip(inverses, inner)]
        size *= 2
    x_ref[...] = jnp.zeros_like(x_ref)
    for (r, c), x in zip(spots, inverses):
        x_ref[r, c] = x
    size = base
    while size < PANEL:
        for k in range(PANELS):
            for start in range(0, PANEL, 2 * size):
                top = slice(start, start + size)
                low = slice(start + size, start + 2 * size)
                left = slice(k * PANEL + start, k * PANEL + start + size)
                right = slice(k * PANEL + start + size, k * PANEL + start + 2 * size)
                x_ref[low, left] = -dot(x_ref[low, right], dot(d_ref[0, low, left], x_ref[top, left]))
        size *= 2


def invert_panels(panels):
    _, rows, width = panels.shape
    return pl.pallas_call(
        invert_kernel,
        grid=(1,),
        in_specs=[pl.BlockSpec((1, rows, width), lambda i: (0, 0, 0))],
        out_specs=pl.BlockSpec((rows, width), lambda i: (0, 0)),
        out_shape=jax.ShapeDtypeStruct((rows, width), jnp.float32),
        compiler_params=pltpu.CompilerParams(vmem_limit_bytes=40 * 2**20),
        cost_estimate=SMALL,
        name="invert_panels",
    )(panels)


def split(value):
    high = value.astype(jnp.bfloat16)
    return high, (value - high.astype(jnp.float32)).astype(jnp.bfloat16)


def one_hot(pairs, first, rows):
    pair = lax.broadcasted_iota(jnp.int32, (rows, pairs.shape[1]), 0) + first
    return jnp.where(pair == pairs, 1.0, 0.0).astype(jnp.bfloat16)


def place_kernel(place_ref, pairs_ref, received_ref, update_ref, out_ref, chosen_ref):
    part = pl.program_id(0)
    total, rank = out_ref.shape
    stride = received_ref.shape[0] // total
    lanes = rank // 128
    parts = stride // lanes

    @pl.when(part == 0)
    def _():
        chosen_ref[...] = one_hot(pairs_ref[...], 0, total)

    value = jnp.concatenate(
        [received_ref[pl.ds(h * parts + part, total, stride=stride), :] for h in range(lanes)], axis=1
    )
    own = (place_ref[1] == 1) & (part * rank < PANEL)
    high, low = split(jnp.where(own, 0.0, value))
    placed = jnp.dot(chosen_ref[...], high, preferred_element_type=jnp.float32)
    placed += jnp.dot(chosen_ref[...], low, preferred_element_type=jnp.float32)
    out_ref[...] = placed - update_ref[...]


def place_rows(place, slot_pair, received, update):
    total, width = update.shape
    rank = 256
    columns = pl.BlockSpec((total, rank), lambda i: (0, i))
    return pl.pallas_call(
        place_kernel,
        grid=(width // rank,),
        in_specs=[
            pl.BlockSpec(memory_space=pltpu.SMEM),
            pl.BlockSpec((1, total), lambda i: (0, 0)),
            pl.BlockSpec(received.shape, lambda i: (0, 0)),
            columns,
        ],
        out_specs=columns,
        out_shape=jax.ShapeDtypeStruct((total, width), jnp.float32),
        scratch_shapes=[pltpu.VMEM((total, total), jnp.bfloat16)],
        compiler_params=pltpu.CompilerParams(vmem_limit_bytes=48 * 2**20),
        name="place_rows",
    )(place, slot_pair, received, update)


def dot_split(a, b):
    def dot(x, y):
        return lax.dot_general(x, y, (((1,), (1,)), ((), ())), preferred_element_type=jnp.float32)

    return dot(a[0], b[0]) + (dot(a[0], b[1]) + dot(a[1], b[0]))


def arrange_kernel(place_ref, pairs_ref, *refs):
    pieces, (right_ref, panels_ref) = refs[:-2], refs[-2:]
    half = len(pieces) // 2
    inner_count = pieces[0].shape[0]
    rows = inner_count * 8
    core, pair, y, z = place_ref[2], place_ref[3], place_ref[4], place_ref[5]
    gradients = jnp.concatenate([ref[:, 16:, :].reshape(rows, PANEL) for ref in pieces], axis=0)
    chosen = one_hot(pairs_ref[...], 0, pairs_ref.shape[1])
    right = None
    for part in split(gradients):
        moved = jnp.dot(chosen, part, preferred_element_type=jnp.float32)
        right = moved if right is None else right + moved
    right_ref[...] = right
    for n, ref in enumerate(pieces):
        kind = core if n < half else 1 - core
        second, outer = n % half // 4, n % 4
        for inner in range(inner_count):
            y_back, z_back = (outer, inner) if second == 0 else (inner, outer)
            chip = lax.rem(y + 4 - y_back, 4) * 4 + lax.rem(z + 4 - z_back, 4)
            for j in range(2):
                unit = chip * 4 + lax.rem(pair + 4 - (2 * second + j), 4)
                place_rows_at = pl.ds(pl.multiple_of(unit * 8, 8), 8)
                panels_ref[kind, place_rows_at, :] = ref[inner, 8 * j : 8 * j + 8, :]


def arrange_rows(place, pairs, pieces):
    inner, depth, width = pieces[0].shape
    total = pairs.shape[1]
    return pl.pallas_call(
        arrange_kernel,
        grid=(width // PANEL,),
        in_specs=[
            pl.BlockSpec(memory_space=pltpu.SMEM),
            pl.BlockSpec(pairs.shape, lambda k: (0, 0)),
        ]
        + [pl.BlockSpec((inner, depth, PANEL), lambda k: (0, 0, k))] * len(pieces),
        out_specs=[
            pl.BlockSpec((total, PANEL), lambda k: (0, k)),
            pl.BlockSpec((2, PANEL, PANEL), lambda k: (0, 0, k)),
        ],
        out_shape=[
            jax.ShapeDtypeStruct((total, width), jnp.float32),
            jax.ShapeDtypeStruct((2, PANEL, width), jnp.float32),
        ],
        compiler_params=pltpu.CompilerParams(vmem_limit_bytes=60 * 2**20),
        cost_estimate=SMALL,
        name="arrange_rows",
    )(place, pairs, *pieces)


def split_kernel(value_ref, high_ref, low_ref):
    high_ref[...], low_ref[...] = split(value_ref[...])


def split_factor(factor_panels):
    rows, depth = factor_panels.shape
    block = pl.BlockSpec((256, depth), lambda i: (i, 0))
    return pl.pallas_call(
        split_kernel,
        grid=(rows // 256,),
        in_specs=[block],
        out_specs=[block, block],
        out_shape=[jax.ShapeDtypeStruct((rows, depth), jnp.bfloat16)] * 2,
        compiler_params=pltpu.CompilerParams(vmem_limit_bytes=60 * 2**20),
        cost_estimate=pl.CostEstimate(
            flops=3 * rows * depth, bytes_accessed=8 * rows * depth, transcendentals=0
        ),
        name="split_factor",
    )(factor_panels)


def solve_kernel(
    place_ref, right_ref, inverse_ref, panels_ref, factor_high_ref, factor_low_ref, out_ref,
    solved_ref, high_ref, low_ref,
):
    step = pl.program_id(0)
    width = out_ref.shape[1]

    @pl.when(step == 0)
    def _():

        def factor(ref, k):
            return split(ref[:, k * PANEL : (k + 1) * PANEL])

        for k in range(PANELS):
            columns = slice(k * PANEL, (k + 1) * PANEL)
            right = right_ref[:, columns]
            for j in range(k):
                before = slice(j * PANEL, (j + 1) * PANEL)
                solved = (high_ref[:, before], low_ref[:, before])
                right -= dot_split(solved, factor(panels_ref.at[0], k * (k - 1) // 2 + j))
            value = dot_split(split(right), factor(inverse_ref, k))
            solved_ref[k] = value
            high_ref[:, columns], low_ref[:, columns] = split(value)

    out_ref[...] = dot_split(
        (high_ref[...], low_ref[...]), (factor_high_ref[...], factor_low_ref[...])
    )

    for i in range(PANEL // width):

        @pl.when((place_ref[1] == 1) & (step == i))
        def _():
            out_ref[...] = -solved_ref[place_ref[0], :, i * width : (i + 1) * width]


def solve_and_update(place, right, inverse, panels, factor_parts):
    rows, depth = factor_parts[0].shape
    total = right.shape[0]
    width = 256
    whole = lambda v: pl.BlockSpec(v.shape, lambda i: (0, 0))
    block = pl.BlockSpec((width, depth), lambda i: (i, 0))
    return pl.pallas_call(
        solve_kernel,
        grid=(rows // width,),
        in_specs=[
            pl.BlockSpec(memory_space=pltpu.SMEM),
            whole(right),
            whole(inverse),
            pl.BlockSpec((1,) + panels.shape[1:], lambda i: (1, 0, 0)),
            block,
            block,
        ],
        out_specs=pl.BlockSpec((total, width), lambda i: (0, i)),
        out_shape=jax.ShapeDtypeStruct((total, rows), jnp.float32),
        scratch_shapes=[
            pltpu.VMEM((PANELS, total, PANEL), jnp.float32),
            pltpu.VMEM((total, depth), jnp.bfloat16),
            pltpu.VMEM((total, depth), jnp.bfloat16),
        ],
        compiler_params=pltpu.CompilerParams(vmem_limit_bytes=48 * 2**20),
        cost_estimate=SMALL,
        name="solve_and_update",
    )(place, right, inverse, panels, *factor_parts)


def along(value, axis, shift):
    if axis == "pair":
        return lax.ppermute(value, "pair", [(p, (p + shift) % 4) for p in range(4)])
    stride = 8 if axis == "y" else 2
    ring = lambda f: f - f // stride % 4 * stride + (f // stride + shift) % 4 * stride
    n_feat = lax.axis_size("feat")
    return lax.ppermute(value, "feat", [(f, ring(f)) for f in range(n_feat)])


def gather_panels(arrived, panel_part, send, factor_panels, feat, pair, slot_pair):
    slots, width = panel_part.shape
    first = jnp.concatenate([arrived[k, :, :PANEL] for k in range(3)], axis=1)
    second = jnp.concatenate([arrived[1, :, :PANEL], arrived[2]], axis=1)
    shard = jnp.where(feat % 2 == 0, first, second)
    depth = shard.shape[0]
    groups = panel_part.reshape(4, slots // 4, width)
    piece = lambda k: lax.dynamic_index_in_dim(groups, (pair + k) % 4, 0, keepdims=False)
    load = lambda k: jnp.concatenate([shard, piece(k)], axis=0)
    pieces = [load(0)] + [along(load(k), "pair", k) for k in range(1, 4)]
    halves = [
        jnp.concatenate([v[:depth] for v in two] + [v[depth:] for v in two], axis=0)[None]
        for two in (pieces[:2], pieces[2:])
    ]
    orders = (("z", "y"), ("y", "z"))
    ring = lambda part, axis: jnp.concatenate(
        [part] + [along(part, axis, k) for k in range(1, 4)], axis=0
    )
    halves = [ring(part, order[0]) for part, order in zip(halves, orders)]
    halves, factor_panels = lax.optimization_barrier((halves, factor_panels))
    parts = split_factor(factor_panels)
    a, b = [[along(part, order[1], k) for k in range(1, 4)] for part, order in zip(halves, orders)]
    a, b, send, parts = lax.optimization_barrier((a, b, send, parts))
    near = [halves[0]] + a + [halves[1]] + b
    cores = [(f, f ^ 1) for f in range(lax.axis_size("feat"))]
    pieces = near + [lax.ppermute(piece, "feat", cores) for piece in near]
    n = lax.broadcasted_iota(jnp.int32, (128, 128), 0)
    other_core, second, outer, inner, back = n // 64, n // 32 % 2, n // 8 % 4, n // 2 % 4, n % 2
    y_back = jnp.where(second == 0, outer, inner)
    z_back = jnp.where(second == 0, inner, outer)
    y = (feat // 8 + 4 - y_back) % 4
    z = (feat // 2 % 4 + 4 - z_back) % 4
    core = (feat % 2 + other_core) % 2
    x = (pair + 4 - (2 * second + back)) % 4
    source = ((y * 4 + z) * 2 + core) * 4 + x
    chosen = (source == lax.broadcasted_iota(jnp.int32, (128, 128), 1)).astype(jnp.float32)
    table = slot_pair.reshape(128, slots // 4).astype(jnp.float32)
    pairs = jnp.dot(chosen, table, precision=HIGHEST, preferred_element_type=jnp.float32)
    pairs = jnp.round(pairs).astype(jnp.int32).reshape(1, 32 * slots)
    return pieces, pairs, send, parts


def per_device(in_factors, out_factors, token_counts, slot_pair, factor_panels):
    slots, _, _, rank = in_factors.shape
    n_pair = lax.axis_size("pair")
    n_feat = lax.axis_size("feat")
    per_group = slots // n_pair
    feat = lax.axis_index("feat")
    pair = lax.axis_index("pair")
    total = n_feat * slots

    place = jnp.stack(
        [jnp.minimum(feat, PANELS - 1), (feat < PANELS).astype(jnp.int32), feat % 2, pair]
        + [feat // 8, feat // 2 % 4]
    ).astype(jnp.int32)
    outgoing = cut_panel(place, factor_panels, n_feat, n_pair)
    arrived = lax.all_to_all(
        outgoing.reshape((n_feat,) + outgoing.shape[2:]), "feat", split_axis=0, concat_axis=0, tiled=True
    )
    send, panel_part = slot_gradients(token_counts, out_factors, in_factors, n_feat, n_pair)
    arrived, panel_part = lax.optimization_barrier((arrived, panel_part))
    pieces, pairs, send, parts = gather_panels(
        arrived, panel_part, send, factor_panels, feat, pair, slot_pair
    )
    received = lax.all_to_all(
        send.reshape((n_feat * n_pair,) + send.shape[2:]),
        ("feat", "pair"),
        split_axis=0,
        concat_axis=0,
        tiled=True,
    ).reshape(total * (rank // 128) * (rank // n_feat), 128)
    right, panels = arrange_rows(place, pairs, pieces)
    inverse = invert_panels(panels)
    update = solve_and_update(place, right, inverse, panels, parts)
    return place_rows(place, slot_pair, received, update)


def solution(mesh):
    return jax.shard_map(
        per_device,
        mesh=mesh,
        in_specs=(
            P(("feat", "pair"), None, None, None),
            P(("feat", "pair"), None, None, None),
            P(("feat", "pair"), None),
            P("pair", None),
            P("feat", None),
        ),
        out_specs=P("pair", "feat"),
        check_vma=False,
    )
```

time: 170 us -> 163 us (0.959)
  waiting for transfers between devices: 34.7 us -> 20.5 us
  Pallas kernels: 72.9 us -> 83.8 us
  starting transfers between devices: 50.3 us -> 41.6 us
  other arithmetic: 0.22 us -> 2.55 us
    all_to_all x1, waiting for transfers between devices: 10.8 us -> 0.01 us  [per_device(): lax.all_to_all(send.reshape((n_feat * n_pair,) + send.shape[2:]), ('feat'...]
    pallas_call x2 -> x3, Pallas kernels: 17.1 us -> 25.4 us  [the longest x1 12.7 us: invert_panels(): pl.pallas_call(invert_kernel, grid=(1,), in_specs=[pl.BlockSpec((1, rows,...]
    ppermute x1 -> x8, starting transfers between devices: 10.3 us -> 2.93 us  [gather_panels(): pieces = near + [lax.ppermute(piece, 'feat', cores) for piece in near]]
    ppermute x12, waiting for transfers between devices: 23 us -> 19.7 us  [along(): return lax.ppermute(value, 'feat', [(f, ring(f)) for f in range(n_feat)])]
    ppermute x12, starting transfers between devices: 16.7 us -> 14.3 us  [along(): return lax.ppermute(value, 'feat', [(f, ring(f)) for f in range(n_feat)])]
    unnamed x16 -> x35, local copies, waits for them, and re-layouts: 8.27 us -> 7.2 us
  transfers between devices with their start and end apart: 18 -> 25, of which waited for: 9 -> 8; matrix products, arithmetic and copies ran while one was open for 4% -> 5% of each run, Pallas kernels for 33% -> 44%
where the time goes in v2:
time: 163 us; the launch traced here: 162 us
  Pallas kernels  83.8 us (51%)
  starting transfers between devices  41.6 us (26%)
  waiting for transfers between devices  20.5 us (13%)
  local copies, waits for them, and re-layouts  11.8 us (7%)
  other arithmetic  2.55 us (2%)
    pallas_call x1, Pallas kernels, solve_and_update(): pl.pallas_call(solve_kernel, grid=(rows // width,), in_specs=[pl.BlockSpe...  21.6 us
    ppermute x12, waiting for transfers between devices, along(): return lax.ppermute(value, 'feat', [(f, ring(f)) for f in range(n_feat)])  19.7 us
    pallas_call x1, Pallas kernels, slot_gradients(): pl.pallas_call(gradient_kernel, grid_spec=pltpu.PrefetchScalarGridSpec(nu...  16 us
    ppermute x12, starting transfers between devices, along(): return lax.ppermute(value, 'feat', [(f, ring(f)) for f in range(n_feat)])  14.3 us
    pallas_call x1, Pallas kernels, invert_panels(): pl.pallas_call(invert_kernel, grid=(1,), in_specs=[pl.BlockSpec((1, rows,...  12.7 us
    pallas_call x1, Pallas kernels, split_factor(): pl.pallas_call(split_kernel, grid=(rows // 256,), in_specs=[block], out_s...  11.4 us
    all_to_all x1, starting transfers between devices, per_device(): lax.all_to_all(send.reshape((n_feat * n_pair,) + send.shape[2:]), ('feat'...  9.81 us
    pallas_call x1, Pallas kernels, place_rows(): pl.pallas_call(place_kernel, grid=(width // rank,), in_specs=[pl.BlockSpe...  9.75 us
  transfers between devices with their start and end apart: 25, of which 8 were waited for; matrix products, arithmetic and copies ran while one was open for 5% of the time, Pallas kernels for 44%

profile of v2, /device:TPU:1, one launch (start us, length us, event | category | flops | bytes accessed | tf_op | source)
XLA Modules:
  0.0 161.8 jit_solution(6099997331398689141)
XLA Ops:
  0.6 3.0 %cut_panel.1 = f32[16,2,8,1024]{3,2,1,0:T(8,128)} custom-call(s32[6]{0:T(128)} %stack.31.place_ref, f32[2048,1536]{1,0:T(8,128)} %value_ref), custom_call_target="tpu_custom_call" | custom-call | tf_op jit(solution)/shard_map/cut_panel/pallas_call | solution.py:90
  3.5 9.6 %all-to-all-start = ((f32[32,8,1024]{2,1,0:T(8,128)}), f32[32,8,1024]{2,1,0:T(8,128)S(1)}, u32[]{:S(2)}, u32[]{:S(2)}) async-start(f32[32,8,1024]{2,1,0:T(8,128)} %bitcast.31), calls=%async_computation | async-start | bytes 2097152 | tf_op jit(solution)/shard_map/all_to_all | solution.py:413
  13.9 16.0 %slot_gradients.1 = (f32[32,4,4,2,8,128]{5,4,3,2,1,0:T(8,128)}, f32[16,1536]{1,0:T(8,128)}) custom-call(s32[16,2]{1,0:T(8,128)} %copy.8.counts_ref, bf16[16,2,512,256]{3,2,1,0:T(8,128)(2,1)} %out_ref.1, bf16[16,2,512,256]{3,2,1,0:T(8,128)(2,1)} %in_ref.1), custom_call_target="tpu_custom_call" | custom-call | flops 2147483648 | bytes 25165824 | tf_op jit(solution)/shard_map/slot_gradients/pallas_call | solution.py:43
  31.1 1.3 collective-permute-start
  32.4 2.5 %collective-permute-start.4 = (f32[12,1536]{1,0:T(8,128)S(1)}, f32[12,1536]{1,0:T(8,128)S(1)}, u32[]{:S(2)}, u32[]{:S(2)}) collective-permute-start(f32[12,1536]{1,0:T(8,128)S(1)} %get-tuple-element.52), channel_id=1, source_target_pairs={{0,2},{1,3},{2,0},{3,1},{4,6},{5,7},{6,4},{7,5},{8,10},{9,11},{10,... | collective-permute-start | bytes 221192 | tf_op jit(solution)/shard_map/ppermute | solution.py:350
  36.7 2.3 %collective-permute-start.3 = (f32[1,24,1536]{2,1,0:T(8,128)S(1)}, f32[1,24,1536]{2,1,0:T(8,128)S(1)}, u32[]{:S(2)}, u32[]{:S(2)}) collective-permute-start(f32[1,24,1536]{2,1,0:T(8,128)S(1)} %maximum_bitcast_fusion), channel_id=1, source_target_pairs={{0,24},{4,28},{8,0},{12,4},{16,8},{20,12},{24,16},{28,20},{32,56},... | collective-permute-start | bytes 442376 | tf_op jit(solution)/shard_map/ppermute | solution.py:354
  40.2 2.5 %collective-permute-start.8 = (f32[1,24,1536]{2,1,0:T(8,128)S(1)}, f32[1,24,1536]{2,1,0:T(8,128)S(1)}, u32[]{:S(2)}, u32[]{:S(2)}) collective-permute-start(f32[1,24,1536]{2,1,0:T(8,128)S(1)} %maximum_bitcast_fusion.1), channel_id=1, source_target_pairs={{0,96},{4,100},{8,104},{12,108},{16,112},{20,116},{24,120},{28,124... | collective-permute-start | bytes 442376 | tf_op jit(solution)/shard_map/ppermute | solution.py:354
  44.6 4.2 %collective-permute-done.1 = f32[1,24,1536]{2,1,0:T(8,128)S(1)} collective-permute-done((f32[1,24,1536]{2,1,0:T(8,128)S(1)}, f32[1,24,1536]{2,1,0:T(8,128)S(1)}, u32[]{:S(2)}, u32[]{:S(2)}) %collective-permute-start.1) | collective-permute-done | bytes 147488 | tf_op jit(solution)/shard_map/ppermute | solution.py:354
  48.9 1.6 collective-permute-done.6
  52.6 2.7 %collective-permute-start.14 = (f32[4,24,1536]{2,1,0:T(8,128)S(1)}, f32[4,24,1536]{2,1,0:T(8,128)S(1)}, u32[]{:S(2)}, u32[]{:S(2)}) collective-permute-start(f32[4,24,1536]{2,1,0:T(8,128)S(1)} %pad_maximum_fusion.1.refs_4_), channel_id=1, source_target_pairs={{0,24},{4,28},{8,0},{12,4},{16,8},{20,12},{24,16},{28,20},{32,56},... | collective-permute-start | bytes 1769480 | tf_op jit(solution)/shard_map/ppermute | solution.py:354
  56.0 6.2 %collective-permute-done.11.refs_3_ = f32[4,24,1536]{2,1,0:T(8,128)S(1)} collective-permute-done((f32[4,24,1536]{2,1,0:T(8,128)S(1)}, f32[4,24,1536]{2,1,0:T(8,128)S(1)}, u32[]{:S(2)}, u32[]{:S(2)}) %collective-permute-start.11) | collective-permute-done | bytes 589856 | tf_op jit(solution)/shard_map/ppermute | solution.py:354
  62.1 1.8 %collective-permute-start.12 = (f32[4,24,1536]{2,1,0:T(8,128)S(1)}, f32[4,24,1536]{2,1,0:T(8,128)}, u32[]{:S(2)}, u32[]{:S(2)}) collective-permute-start(f32[4,24,1536]{2,1,0:T(8,128)S(1)} %pad_maximum_fusion.1.refs_4_), channel_id=1, source_target_pairs={{0,8},{4,12},{8,16},{12,20},{16,24},{20,28},{24,0},{28,4},{32,40},... | collective-permute-start | bytes 1769480 | tf_op jit(solution)/shard_map/ppermute | solution.py:354
  63.9 11.4 %split_factor.1 = (bf16[2048,1536]{1,0:T(8,128)(2,1)}, bf16[2048,1536]{1,0:T(8,128)(2,1)}) custom-call(f32[2048,1536]{1,0:T(8,128)} %value_ref), custom_call_target="tpu_custom_call" | custom-call | flops 9437184 | bytes 25165824 | tf_op jit(solution)/shard_map/split_factor/pallas_call | solution.py:269
  75.3 5.7 %collective-permute-done.9.refs_1_ = f32[4,24,1536]{2,1,0:T(8,128)S(1)} collective-permute-done((f32[4,24,1536]{2,1,0:T(8,128)S(1)}, f32[4,24,1536]{2,1,0:T(8,128)S(1)}, u32[]{:S(2)}, u32[]{:S(2)}) %collective-permute-start.9) | collective-permute-done | bytes 589856 | tf_op jit(solution)/shard_map/ppermute | solution.py:354
  81.0 1.2 collective-permute-done.12.refs_5_
  82.3 9.8 %all-to-all-start.1 = ((f32[128,4,2,8,128]{4,3,2,1,0:T(8,128)}), f32[128,4,2,8,128]{4,3,2,1,0:T(8,128)}, u32[]{:S(2)}, u32[]{:S(2)}) async-start(f32[128,4,2,8,128]{4,3,2,1,0:T(8,128)} %bitcast.30), calls=%async_computation.1 | async-start | bytes 8388608 | tf_op jit(solution)/shard_map/all_to_all | solution.py:421
  99.2 1.3 fusion
  101.4 1.5 reshape.21.pairs_ref
  103.9 9.4 %arrange_rows.1 = (f32[512,1536]{1,0:T(8,128)}, f32[2,512,1536]{2,1,0:T(8,128)}) custom-call(s32[6]{0:T(128)} %stack.31.place_ref, s32[1,512]{1,0:T(1,128)} %reshape.21.pairs_ref, f32[4,24,1536]{2,1,0:T(8,128)} %copy-done.5, f32[4,24,1536]{2,1,0:T(8,128)} %copy-done.9, f32[4,24,1536]{2,1,0:T(8,128)} %copy-done.8, f32[4,24,1536]{2,1,0:T(8,128)} %copy-done.7, ...), custom_call_target="tpu_custom_call" | custom-call | flops 1 | bytes 1 | tf_op jit(solution)/shard_map/arrange_rows/pallas_call | solution.py:240
  113.3 2.8 %copy-done = f32[2,512,1536]{2,1,0:T(8,128)S(1)} copy-done((f32[2,512,1536]{2,1,0:T(8,128)S(1)}, f32[2,512,1536]{2,1,0:T(8,128)}, u32[]{:S(2)}) %copy-start) | copy-done | bytes 6291480
  116.0 12.7 %invert_panels.1.inverse_ref = f32[512,1536]{1,0:T(8,128)S(1)} custom-call(f32[2,512,1536]{2,1,0:T(8,128)S(1)} %copy-done), custom_call_target="tpu_custom_call" | custom-call | flops 1 | bytes 1 | tf_op jit(solution)/shard_map/invert_panels/pallas_call | solution.py:141
  128.7 1.7 %copy-done.1 = f32[512,1536]{1,0:T(8,128)} copy-done((f32[512,1536]{1,0:T(8,128)}, f32[512,1536]{1,0:T(8,128)S(1)}, u32[]{:S(2)}) %copy-start.1) | copy-done | bytes 3145752
  130.4 21.6 %solve_and_update.1.update_ref = f32[512,2048]{1,0:T(8,128)} custom-call(s32[6]{0:T(128)S(1)} %copy-done.3, f32[512,1536]{1,0:T(8,128)S(1)} %copy-done.2, f32[512,1536]{1,0:T(8,128)} %copy-done.1, f32[2,512,1536]{2,1,0:T(8,128)} %get-tuple-element.42.d_ref.panels_ref, bf16[2048,1536]{1,0:T(8,128)(2,1)} %get-tuple-element.43.factor_high_ref, ...), custom_call_target="tpu_custom_call" | custom-call | flops 1 | bytes 1 | tf_op jit(solution)/shard_map/solve_and_update/pallas_call | solution.py:324
  152.0 9.7 %place_rows.1 = f32[512,2048]{1,0:T(8,128)} custom-call(s32[6]{0:T(128)S(1)} %copy-done.3, s32[1,512]{1,0:T(1,128)S(1)} %copy-done.4, f32[8192,128]{1,0:T(8,128)} %bitcast.18.received_ref, f32[512,2048]{1,0:T(8,128)} %solve_and_update.1.update_ref), custom_call_target="tpu_custom_call" | custom-call | tf_op jit(solution)/shard_map/place_rows/pallas_call | solution.py:188
  (98 shorter events, 19.0 us)
Async XLA Ops:
  3.5 26.5 %all-to-all-start = ((f32[32,8,1024]{2,1,0:T(8,128)}), f32[32,8,1024]{2,1,0:T(8,128)S(1)}, u32[]{:S(2)}, u32[]{:S(2)}) async-start(f32[32,8,1024]{2,1,0:T(8,128)} %bitcast.31), calls=%async_computation | async-start | bytes 2097152 | tf_op jit(solution)/shard_map/all_to_all | solution.py:413
  31.1 5.5 %collective-permute-start = (f32[12,1536]{1,0:T(8,128)S(1)}, f32[12,1536]{1,0:T(8,128)S(1)}, u32[]{:S(2)}, u32[]{:S(2)}) collective-permute-start(f32[12,1536]{1,0:T(8,128)S(1)} %get-tuple-element.54), channel_id=1, source_target_pairs={{0,1},{1,2},{2,3},{3,0},{4,5},{5,6},{6,7},{7,4},{8,9},{9,10},{10,1... | collective-permute-start | bytes 221192 | tf_op jit(solution)/shard_map/ppermute | solution.py:350
  32.4 7.8 %collective-permute-start.4 = (f32[12,1536]{1,0:T(8,128)S(1)}, f32[12,1536]{1,0:T(8,128)S(1)}, u32[]{:S(2)}, u32[]{:S(2)}) collective-permute-start(f32[12,1536]{1,0:T(8,128)S(1)} %get-tuple-element.52), channel_id=1, source_target_pairs={{0,2},{1,3},{2,0},{3,1},{4,6},{5,7},{6,4},{7,5},{8,10},{9,11},{10,... | collective-permute-start | bytes 221192 | tf_op jit(solution)/shard_map/ppermute | solution.py:350
  34.8 5.4 %collective-permute-start.5 = (f32[12,1536]{1,0:T(8,128)S(1)}, f32[12,1536]{1,0:T(8,128)S(1)}, u32[]{:S(2)}, u32[]{:S(2)}) collective-permute-start(f32[12,1536]{1,0:T(8,128)S(1)} %get-tuple-element.53), channel_id=1, source_target_pairs={{0,3},{1,0},{2,1},{3,2},{4,7},{5,4},{6,5},{7,6},{8,11},{9,8},{10,9... | collective-permute-start | bytes 221192 | tf_op jit(solution)/shard_map/ppermute | solution.py:350
  36.7 6.6 %collective-permute-start.3 = (f32[1,24,1536]{2,1,0:T(8,128)S(1)}, f32[1,24,1536]{2,1,0:T(8,128)S(1)}, u32[]{:S(2)}, u32[]{:S(2)}) collective-permute-start(f32[1,24,1536]{2,1,0:T(8,128)S(1)} %maximum_bitcast_fusion), channel_id=1, source_target_pairs={{0,24},{4,28},{8,0},{12,4},{16,8},{20,12},{24,16},{28,20},{32,56},... | collective-permute-start | bytes 442376 | tf_op jit(solution)/shard_map/ppermute | solution.py:354
  39.0 5.6 %collective-permute-start.2 = (f32[1,24,1536]{2,1,0:T(8,128)S(1)}, f32[1,24,1536]{2,1,0:T(8,128)S(1)}, u32[]{:S(2)}, u32[]{:S(2)}) collective-permute-start(f32[1,24,1536]{2,1,0:T(8,128)S(1)} %maximum_bitcast_fusion), channel_id=1, source_target_pairs={{0,16},{4,20},{8,24},{12,28},{16,0},{20,4},{24,8},{28,12},{32,48},... | collective-permute-start | bytes 442376 | tf_op jit(solution)/shard_map/ppermute | solution.py:354
  39.5 9.3 %collective-permute-start.1 = (f32[1,24,1536]{2,1,0:T(8,128)S(1)}, f32[1,24,1536]{2,1,0:T(8,128)S(1)}, u32[]{:S(2)}, u32[]{:S(2)}) collective-permute-start(f32[1,24,1536]{2,1,0:T(8,128)S(1)} %maximum_bitcast_fusion), channel_id=1, source_target_pairs={{0,8},{4,12},{8,16},{12,20},{16,24},{20,28},{24,0},{28,4},{32,40},... | collective-permute-start | bytes 442376 | tf_op jit(solution)/shard_map/ppermute | solution.py:354
  40.2 8.6 %collective-permute-start.8 = (f32[1,24,1536]{2,1,0:T(8,128)S(1)}, f32[1,24,1536]{2,1,0:T(8,128)S(1)}, u32[]{:S(2)}, u32[]{:S(2)}) collective-permute-start(f32[1,24,1536]{2,1,0:T(8,128)S(1)} %maximum_bitcast_fusion.1), channel_id=1, source_target_pairs={{0,96},{4,100},{8,104},{12,108},{16,112},{20,116},{24,120},{28,124... | collective-permute-start | bytes 442376 | tf_op jit(solution)/shard_map/ppermute | solution.py:354
  42.7 6.1 %collective-permute-start.7 = (f32[1,24,1536]{2,1,0:T(8,128)S(1)}, f32[1,24,1536]{2,1,0:T(8,128)S(1)}, u32[]{:S(2)}, u32[]{:S(2)}) collective-permute-start(f32[1,24,1536]{2,1,0:T(8,128)S(1)} %maximum_bitcast_fusion.1), channel_id=1, source_target_pairs={{0,64},{4,68},{8,72},{12,76},{16,80},{20,84},{24,88},{28,92},{32,9... | collective-permute-start | bytes 442376 | tf_op jit(solution)/shard_map/ppermute | solution.py:354
  43.3 7.1 %collective-permute-start.6 = (f32[1,24,1536]{2,1,0:T(8,128)S(1)}, f32[1,24,1536]{2,1,0:T(8,128)S(1)}, u32[]{:S(2)}, u32[]{:S(2)}) collective-permute-start(f32[1,24,1536]{2,1,0:T(8,128)S(1)} %maximum_bitcast_fusion.1), channel_id=1, source_target_pairs={{0,32},{4,36},{8,40},{12,44},{16,48},{20,52},{24,56},{28,60},{32,6... | collective-permute-start | bytes 442376 | tf_op jit(solution)/shard_map/ppermute | solution.py:354
  50.5 11.7 %collective-permute-start.11 = (f32[4,24,1536]{2,1,0:T(8,128)S(1)}, f32[4,24,1536]{2,1,0:T(8,128)S(1)}, u32[]{:S(2)}, u32[]{:S(2)}) collective-permute-start(f32[4,24,1536]{2,1,0:T(8,128)S(1)} %pad_maximum_fusion.refs_0_), channel_id=1, source_target_pairs={{0,96},{4,100},{8,104},{12,108},{16,112},{20,116},{24,120},{28,124... | collective-permute-start | bytes 1769480 | tf_op jit(solution)/shard_map/ppermute | solution.py:354
  51.5 23.8 %collective-permute-start.10 = (f32[4,24,1536]{2,1,0:T(8,128)S(1)}, f32[4,24,1536]{2,1,0:T(8,128)S(1)}, u32[]{:S(2)}, u32[]{:S(2)}) collective-permute-start(f32[4,24,1536]{2,1,0:T(8,128)S(1)} %pad_maximum_fusion.refs_0_), channel_id=1, source_target_pairs={{0,64},{4,68},{8,72},{12,76},{16,80},{20,84},{24,88},{28,92},{32,9... | collective-permute-start | bytes 1769480 | tf_op jit(solution)/shard_map/ppermute | solution.py:354
  51.9 29.1 %collective-permute-start.9 = (f32[4,24,1536]{2,1,0:T(8,128)S(1)}, f32[4,24,1536]{2,1,0:T(8,128)S(1)}, u32[]{:S(2)}, u32[]{:S(2)}) collective-permute-start(f32[4,24,1536]{2,1,0:T(8,128)S(1)} %pad_maximum_fusion.refs_0_), channel_id=1, source_target_pairs={{0,32},{4,36},{8,40},{12,44},{16,48},{20,52},{24,56},{28,60},{32,6... | collective-permute-start | bytes 1769480 | tf_op jit(solution)/shard_map/ppermute | solution.py:354
  52.6 28.4 %collective-permute-start.14 = (f32[4,24,1536]{2,1,0:T(8,128)S(1)}, f32[4,24,1536]{2,1,0:T(8,128)S(1)}, u32[]{:S(2)}, u32[]{:S(2)}) collective-permute-start(f32[4,24,1536]{2,1,0:T(8,128)S(1)} %pad_maximum_fusion.1.refs_4_), channel_id=1, source_target_pairs={{0,24},{4,28},{8,0},{12,4},{16,8},{20,12},{24,16},{28,20},{32,56},... | collective-permute-start | bytes 1769480 | tf_op jit(solution)/shard_map/ppermute | solution.py:354
  55.3 25.7 %collective-permute-start.13 = (f32[4,24,1536]{2,1,0:T(8,128)S(1)}, f32[4,24,1536]{2,1,0:T(8,128)}, u32[]{:S(2)}, u32[]{:S(2)}) collective-permute-start(f32[4,24,1536]{2,1,0:T(8,128)S(1)} %pad_maximum_fusion.1.refs_4_), channel_id=1, source_target_pairs={{0,16},{4,20},{8,24},{12,28},{16,0},{20,4},{24,8},{28,12},{32,48},... | collective-permute-start | bytes 1769480 | tf_op jit(solution)/shard_map/ppermute | solution.py:354
  62.1 20.2 %collective-permute-start.12 = (f32[4,24,1536]{2,1,0:T(8,128)S(1)}, f32[4,24,1536]{2,1,0:T(8,128)}, u32[]{:S(2)}, u32[]{:S(2)}) collective-permute-start(f32[4,24,1536]{2,1,0:T(8,128)S(1)} %pad_maximum_fusion.1.refs_4_), channel_id=1, source_target_pairs={{0,8},{4,12},{8,16},{12,20},{16,24},{20,28},{24,0},{28,4},{32,40},... | collective-permute-start | bytes 1769480 | tf_op jit(solution)/shard_map/ppermute | solution.py:354
  82.3 69.7 %all-to-all-start.1 = ((f32[128,4,2,8,128]{4,3,2,1,0:T(8,128)}), f32[128,4,2,8,128]{4,3,2,1,0:T(8,128)}, u32[]{:S(2)}, u32[]{:S(2)}) async-start(f32[128,4,2,8,128]{4,3,2,1,0:T(8,128)} %bitcast.30), calls=%async_computation.1 | async-start | bytes 8388608 | tf_op jit(solution)/shard_map/all_to_all | solution.py:421
  92.1 4.1 %collective-permute-start.15 = (f32[4,24,1536]{2,1,0:T(8,128)S(1)}, f32[4,24,1536]{2,1,0:T(8,128)S(1)}, u32[]{:S(2)}, u32[]{:S(2)}) collective-permute-start(f32[4,24,1536]{2,1,0:T(8,128)S(1)} %pad_maximum_fusion.refs_0_), channel_id=1, source_target_pairs={{0,4},{4,0},{8,12},{12,8},{16,20},{20,16},{24,28},{28,24},{32,36},... | collective-permute-start | bytes 1769480 | tf_op jit(solution)/shard_map/ppermute | solution.py:382
  93.4 3.3 %collective-permute-start.16 = (f32[4,24,1536]{2,1,0:T(8,128)S(1)}, f32[4,24,1536]{2,1,0:T(8,128)S(1)}, u32[]{:S(2)}, u32[]{:S(2)}) collective-permute-start(f32[4,24,1536]{2,1,0:T(8,128)S(1)} %collective-permute-done.9.refs_1_), channel_id=1, source_target_pairs={{0,4},{4,0},{8,12},{12,8},{16,20},{20,16},{24,28},{28,24},{32,36},... | collective-permute-start | bytes 1769480 | tf_op jit(solution)/shard_map/ppermute | solution.py:382
  95.7 7.2 %collective-permute-start.17 = (f32[4,24,1536]{2,1,0:T(8,128)S(1)}, f32[4,24,1536]{2,1,0:T(8,128)}, u32[]{:S(2)}, u32[]{:S(2)}) collective-permute-start(f32[4,24,1536]{2,1,0:T(8,128)S(1)} %collective-permute-done.10.refs_2_), channel_id=1, source_target_pairs={{0,4},{4,0},{8,12},{12,8},{16,20},{20,16},{24,28},{28,24},{32,36},... | collective-permute-start | bytes 1769480 | tf_op jit(solution)/shard_map/ppermute | solution.py:382
  95.8 7.0 %collective-permute-start.18 = (f32[4,24,1536]{2,1,0:T(8,128)S(1)}, f32[4,24,1536]{2,1,0:T(8,128)}, u32[]{:S(2)}, u32[]{:S(2)}) collective-permute-start(f32[4,24,1536]{2,1,0:T(8,128)S(1)} %collective-permute-done.11.refs_3_), channel_id=1, source_target_pairs={{0,4},{4,0},{8,12},{12,8},{16,20},{20,16},{24,28},{28,24},{32,36},... | collective-permute-start | bytes 1769480 | tf_op jit(solution)/shard_map/ppermute | solution.py:382
  96.2 6.6 %collective-permute-start.20 = (f32[4,24,1536]{2,1,0:T(8,128)}, f32[4,24,1536]{2,1,0:T(8,128)S(1)}, u32[]{:S(2)}, u32[]{:S(2)}) collective-permute-start(f32[4,24,1536]{2,1,0:T(8,128)} %collective-permute-done.12.refs_5_), channel_id=1, source_target_pairs={{0,4},{4,0},{8,12},{12,8},{16,20},{20,16},{24,28},{28,24},{32,36},... | collective-permute-start | bytes 1769480 | tf_op jit(solution)/shard_map/ppermute | solution.py:382
  96.4 6.5 %collective-permute-start.21 = (f32[4,24,1536]{2,1,0:T(8,128)}, f32[4,24,1536]{2,1,0:T(8,128)S(1)}, u32[]{:S(2)}, u32[]{:S(2)}) collective-permute-start(f32[4,24,1536]{2,1,0:T(8,128)} %collective-permute-done.13.refs_6_), channel_id=1, source_target_pairs={{0,4},{4,0},{8,12},{12,8},{16,20},{20,16},{24,28},{28,24},{32,36},... | collective-permute-start | bytes 1769480 | tf_op jit(solution)/shard_map/ppermute | solution.py:382
  97.1 5.8 %collective-permute-start.22 = (f32[4,24,1536]{2,1,0:T(8,128)S(1)}, f32[4,24,1536]{2,1,0:T(8,128)}, u32[]{:S(2)}, u32[]{:S(2)}) collective-permute-start(f32[4,24,1536]{2,1,0:T(8,128)S(1)} %collective-permute-done.14.refs_7_), channel_id=1, source_target_pairs={{0,4},{4,0},{8,12},{12,8},{16,20},{20,16},{24,28},{28,24},{32,36},... | collective-permute-start | bytes 1769480 | tf_op jit(solution)/shard_map/ppermute | solution.py:382
  (18 other events, 267.8 us)

commit v3 on v2

--- a/solution.py
+++ b/solution.py
@@ -136,20 +136,6 @@
         size *= 2
 
 
-def invert_panels(panels):
-    _, rows, width = panels.shape
-    return pl.pallas_call(
-        invert_kernel,
-        grid=(1,),
-        in_specs=[pl.BlockSpec((1, rows, width), lambda i: (0, 0, 0))],
-        out_specs=pl.BlockSpec((rows, width), lambda i: (0, 0)),
-        out_shape=jax.ShapeDtypeStruct((rows, width), jnp.float32),
-        compiler_params=pltpu.CompilerParams(vmem_limit_bytes=40 * 2**20),
-        cost_estimate=SMALL,
-        name="invert_panels",
-    )(panels)
-
-
 def split(value):
     high = value.astype(jnp.bfloat16)
     return high, (value - high.astype(jnp.float32)).astype(jnp.bfloat16)
@@ -160,43 +146,54 @@
     return jnp.where(pair == pairs, 1.0, 0.0).astype(jnp.bfloat16)
 
 
-def place_kernel(place_ref, pairs_ref, received_ref, update_ref, out_ref, chosen_ref):
-    part = pl.program_id(0)
-    total, rank = out_ref.shape
-    stride = received_ref.shape[0] // total
-    lanes = rank // 128
-    parts = stride // lanes
-
-    @pl.when(part == 0)
+def place_kernel(place_ref, pairs_ref, received_ref, update_ref, out_ref, high_ref, low_ref):
+    step = pl.program_id(0)
+    rows = out_ref.shape[0]
+    parts, total, rank = high_ref.shape
+
+    @pl.when(step == 0)
     def _():
-        chosen_ref[...] = one_hot(pairs_ref[...], 0, total)
-
-    value = jnp.concatenate(
-        [received_ref[pl.ds(h * parts + part, total, stride=stride), :] for h in range(lanes)], axis=1
-    )
-    own = (place_ref[1] == 1) & (part * rank < PANEL)
-    high, low = split(jnp.where(own, 0.0, value))
-    placed = jnp.dot(chosen_ref[...], high, preferred_element_type=jnp.float32)
-    placed += jnp.dot(chosen_ref[...], low, preferred_element_type=jnp.float32)
-    out_ref[...] = placed - update_ref[...]
+        for i in range(parts):
+            lanes = rank // 128
+            value = jnp.concatenate(
+                [
+                    received_ref[pl.ds(h * parts + i, total, stride=lanes * parts), :]
+                    for h in range(lanes)
+                ],
+                axis=1,
+            )
+            if i * rank < PANEL:
+                value = jnp.where(place_ref[1] == 1, 0.0, value)
+            high_ref[i], low_ref[i] = split(value)
+
+    chosen = one_hot(pairs_ref[...], step * rows, rows)
+    for i in range(parts):
+        placed = jnp.dot(chosen, high_ref[i], preferred_element_type=jnp.float32)
+        placed += jnp.dot(chosen, low_ref[i], preferred_element_type=jnp.float32)
+        columns = slice(i * rank, (i + 1) * rank)
+        out_ref[:, columns] = placed - update_ref[:, columns]
 
 
 def place_rows(place, slot_pair, received, update):
     total, width = update.shape
-    rank = 256
-    columns = pl.BlockSpec((total, rank), lambda i: (0, i))
+    rank = 2 * received.shape[1]
+    parts = width // rank
+    rows = 128
     return pl.pallas_call(
         place_kernel,
-        grid=(width // rank,),
+        grid=(total // rows,),
         in_specs=[
             pl.BlockSpec(memory_space=pltpu.SMEM),
             pl.BlockSpec((1, total), lambda i: (0, 0)),
             pl.BlockSpec(received.shape, lambda i: (0, 0)),
-            columns,
-        ],
-        out_specs=columns,
+            pl.BlockSpec((rows, width), lambda i: (i, 0)),
+        ],
+        out_specs=pl.BlockSpec((rows, width), lambda i: (i, 0)),
         out_shape=jax.ShapeDtypeStruct((total, width), jnp.float32),
-        scratch_shapes=[pltpu.VMEM((total, total), jnp.bfloat16)],
+        scratch_shapes=[
+            pltpu.VMEM((parts, total, rank), jnp.bfloat16),
+            pltpu.VMEM((parts, total, rank), jnp.bfloat16),
+        ],
         compiler_params=pltpu.CompilerParams(vmem_limit_bytes=48 * 2**20),
         name="place_rows",
     )(place, slot_pair, received, update)
@@ -259,36 +256,16 @@
     )(place, pairs, *pieces)
 
 
-def split_kernel(value_ref, high_ref, low_ref):
-    high_ref[...], low_ref[...] = split(value_ref[...])
-
-
-def split_factor(factor_panels):
-    rows, depth = factor_panels.shape
-    block = pl.BlockSpec((256, depth), lambda i: (i, 0))
-    return pl.pallas_call(
-        split_kernel,
-        grid=(rows // 256,),
-        in_specs=[block],
-        out_specs=[block, block],
-        out_shape=[jax.ShapeDtypeStruct((rows, depth), jnp.bfloat16)] * 2,
-        compiler_params=pltpu.CompilerParams(vmem_limit_bytes=60 * 2**20),
-        cost_estimate=pl.CostEstimate(
-            flops=3 * rows * depth, bytes_accessed=8 * rows * depth, transcendentals=0
-        ),
-        name="split_factor",
-    )(factor_panels)
-
-
 def solve_kernel(
-    place_ref, right_ref, inverse_ref, panels_ref, factor_high_ref, factor_low_ref, out_ref,
-    solved_ref, high_ref, low_ref,
+    place_ref, right_ref, panels_ref, factor_ref, out_ref,
+    inverse_ref, solved_ref, high_ref, low_ref,
 ):
     step = pl.program_id(0)
     width = out_ref.shape[1]
 
     @pl.when(step == 0)
     def _():
+        invert_kernel(panels_ref, inverse_ref)
 
         def factor(ref, k):
             return split(ref[:, k * PANEL : (k + 1) * PANEL])
@@ -299,14 +276,12 @@
             for j in range(k):
                 before = slice(j * PANEL, (j + 1) * PANEL)
                 solved = (high_ref[:, before], low_ref[:, before])
-                right -= dot_split(solved, factor(panels_ref.at[0], k * (k - 1) // 2 + j))
+                right -= dot_split(solved, factor(panels_ref.at[1], k * (k - 1) // 2 + j))
             value = dot_split(split(right), factor(inverse_ref, k))
             solved_ref[k] = value
             high_ref[:, columns], low_ref[:, columns] = split(value)
 
-    out_ref[...] = dot_split(
-        (high_ref[...], low_ref[...]), (factor_high_ref[...], factor_low_ref[...])
-    )
+    out_ref[...] = dot_split((high_ref[...], low_ref[...]), split(factor_ref[...]))
 
     for i in range(PANEL // width):
 
@@ -315,8 +290,8 @@
             out_ref[...] = -solved_ref[place_ref[0], :, i * width : (i + 1) * width]
 
 
-def solve_and_update(place, right, inverse, panels, factor_parts):
-    rows, depth = factor_parts[0].shape
+def solve_and_update(place, right, panels, factor_panels):
+    rows, depth = factor_panels.shape
     total = right.shape[0]
     width = 256
     whole = lambda v: pl.BlockSpec(v.shape, lambda i: (0, 0))
@@ -327,22 +302,21 @@
         in_specs=[
             pl.BlockSpec(memory_space=pltpu.SMEM),
             whole(right),
-            whole(inverse),
-            pl.BlockSpec((1,) + panels.shape[1:], lambda i: (1, 0, 0)),
-            block,
+            pl.BlockSpec(panels.shape, lambda i: (0, 0, 0)),
             block,
         ],
         out_specs=pl.BlockSpec((total, width), lambda i: (0, i)),
         out_shape=jax.ShapeDtypeStruct((total, rows), jnp.float32),
         scratch_shapes=[
+            pltpu.VMEM(panels.shape[1:], jnp.float32),
             pltpu.VMEM((PANELS, total, PANEL), jnp.float32),
             pltpu.VMEM((total, depth), jnp.bfloat16),
             pltpu.VMEM((total, depth), jnp.bfloat16),
         ],
-        compiler_params=pltpu.CompilerParams(vmem_limit_bytes=48 * 2**20),
+        compiler_params=pltpu.CompilerParams(vmem_limit_bytes=56 * 2**20),
         cost_estimate=SMALL,
         name="solve_and_update",
-    )(place, right, inverse, panels, *factor_parts)
+    )(place, right, panels, factor_panels)
 
 
 def along(value, axis, shift):
@@ -354,7 +328,7 @@
     return lax.ppermute(value, "feat", [(f, ring(f)) for f in range(n_feat)])
 
 
-def gather_panels(arrived, panel_part, send, factor_panels, feat, pair, slot_pair):
+def gather_panels(arrived, panel_part, send, feat, pair, slot_pair):
     slots, width = panel_part.shape
     first = jnp.concatenate([arrived[k, :, :PANEL] for k in range(3)], axis=1)
     second = jnp.concatenate([arrived[1, :, :PANEL], arrived[2]], axis=1)
@@ -373,13 +347,7 @@
         [part] + [along(part, axis, k) for k in range(1, 4)], axis=0
     )
     halves = [ring(part, order[0]) for part, order in zip(halves, orders)]
-    halves, factor_panels = lax.optimization_barrier((halves, factor_panels))
-    parts = split_factor(factor_panels)
-    a, b = [[along(part, order[1], k) for k in range(1, 4)] for part, order in zip(halves, orders)]
-    a, b, send, parts = lax.optimization_barrier((a, b, send, parts))
-    near = [halves[0]] + a + [halves[1]] + b
-    cores = [(f, f ^ 1) for f in range(lax.axis_size("feat"))]
-    pieces = near + [lax.ppermute(piece, "feat", cores) for piece in near]
+    halves, slot_pair = lax.optimization_barrier((halves, slot_pair))
     n = lax.broadcasted_iota(jnp.int32, (128, 128), 0)
     other_core, second, outer, inner, back = n // 64, n // 32 % 2, n // 8 % 4, n // 2 % 4, n % 2
     y_back = jnp.where(second == 0, outer, inner)
@@ -393,7 +361,12 @@
     table = slot_pair.reshape(128, slots // 4).astype(jnp.float32)
     pairs = jnp.dot(chosen, table, precision=HIGHEST, preferred_element_type=jnp.float32)
     pairs = jnp.round(pairs).astype(jnp.int32).reshape(1, 32 * slots)
-    return pieces, pairs, send, parts
+    a, b = [[along(part, order[1], k) for k in range(1, 4)] for part, order in zip(halves, orders)]
+    a, b, send, pairs = lax.optimization_barrier((a, b, send, pairs))
+    near = [halves[0]] + a + [halves[1]] + b
+    cores = [(f, f ^ 1) for f in range(lax.axis_size("feat"))]
+    pieces = near + [lax.ppermute(piece, "feat", cores) for piece in near]
+    return pieces, pairs, send
 
 
 def per_device(in_factors, out_factors, token_counts, slot_pair, factor_panels):
@@ -415,9 +388,7 @@
     )
     send, panel_part = slot_gradients(token_counts, out_factors, in_factors, n_feat, n_pair)
     arrived, panel_part = lax.optimization_barrier((arrived, panel_part))
-    pieces, pairs, send, parts = gather_panels(
-        arrived, panel_part, send, factor_panels, feat, pair, slot_pair
-    )
+    pieces, pairs, send = gather_panels(arrived, panel_part, send, feat, pair, slot_pair)
     received = lax.all_to_all(
         send.reshape((n_feat * n_pair,) + send.shape[2:]),
         ("feat", "pair"),
@@ -426,8 +397,7 @@
         tiled=True,
     ).reshape(total * (rank // 128) * (rank // n_feat), 128)
     right, panels = arrange_rows(place, pairs, pieces)
-    inverse = invert_panels(panels)
-    update = solve_and_update(place, right, inverse, panels, parts)
+    update = solve_and_update(place, right, panels, factor_panels)
     return place_rows(place, slot_pair, received, update)
 
 

time: 163 us -> 159 us (0.975)
  Pallas kernels: 83.8 us -> 71.7 us
  waiting for transfers between devices: 20.5 us -> 29.5 us
  local copies, waits for them, and re-layouts: 11.8 us -> 7.58 us
    pallas_call x3 -> x1, Pallas kernels: 33.8 us -> 8.83 us  [place_rows(): pl.pallas_call(place_kernel, grid=(total // rows,), in_specs=[pl.BlockSpe...]
    pallas_call x1, Pallas kernels: 21.6 us -> 34.6 us  [solve_and_update(): pl.pallas_call(solve_kernel, grid=(rows // width,), in_specs=[pl.BlockSpe...]
    ppermute x8, waiting for transfers between devices: 0.02 us -> 4.73 us  [gather_panels(): pieces = near + [lax.ppermute(piece, 'feat', cores) for piece in near]]
    ppermute x12, waiting for transfers between devices: 19.7 us -> 24 us  [along(): return lax.ppermute(value, 'feat', [(f, ring(f)) for f in range(n_feat)])]
    unnamed x35, local copies, waits for them, and re-layouts: 7.2 us -> 2.97 us
  transfers between devices with their start and end apart: 25 -> 25, of which waited for: 8 -> 14; matrix products, arithmetic and copies ran while one was open for 5% -> 6% of each run, Pallas kernels for 44% -> 38%
where the time goes in v3:
time: 159 us; the launch traced here: 158 us
  Pallas kernels  71.7 us (45%)
  starting transfers between devices  43 us (27%)
  waiting for transfers between devices  29.5 us (19%)
  local copies, waits for them, and re-layouts  7.58 us (5%)
  other arithmetic  4.13 us (3%)
    pallas_call x1, Pallas kernels, solve_and_update(): pl.pallas_call(solve_kernel, grid=(rows // width,), in_specs=[pl.BlockSpe...  34.6 us
    ppermute x12, waiting for transfers between devices, along(): return lax.ppermute(value, 'feat', [(f, ring(f)) for f in range(n_feat)])  24 us
    pallas_call x1, Pallas kernels, slot_gradients(): pl.pallas_call(gradient_kernel, grid_spec=pltpu.PrefetchScalarGridSpec(nu...  16 us
    ppermute x12, starting transfers between devices, along(): return lax.ppermute(value, 'feat', [(f, ring(f)) for f in range(n_feat)])  14.2 us
    all_to_all x1, starting transfers between devices, per_device(): lax.all_to_all(send.reshape((n_feat * n_pair,) + send.shape[2:]), ('feat'...  10.9 us
    all_to_all x1, starting transfers between devices, per_device(): lax.all_to_all(outgoing.reshape((n_feat,) + outgoing.shape[2:]), 'feat',...  9.6 us
    pallas_call x1, Pallas kernels, arrange_rows(): pl.pallas_call(arrange_kernel, grid=(width // PANEL,), in_specs=[pl.Block...  9.29 us
    pallas_call x1, Pallas kernels, place_rows(): pl.pallas_call(place_kernel, grid=(total // rows,), in_specs=[pl.BlockSpe...  8.83 us
  transfers between devices with their start and end apart: 25, of which 14 were waited for; matrix products, arithmetic and copies ran while one was open for 6% of the time, Pallas kernels for 38%

profile of v3, /device:TPU:1, one launch (start us, length us, event | category | flops | bytes accessed | tf_op | source)
XLA Modules:
  0.0 157.6 jit_solution(14674535791221931454)
XLA Ops:
  0.6 3.0 %cut_panel.1 = f32[16,2,8,1024]{3,2,1,0:T(8,128)} custom-call(s32[6]{0:T(128)} %stack.31.place_ref, f32[2048,1536]{1,0:T(8,128)} %factor_ref.1), custom_call_target="tpu_custom_call" | custom-call | tf_op jit(solution)/shard_map/cut_panel/pallas_call | solution.py:90
  3.6 9.6 %all-to-all-start = ((f32[32,8,1024]{2,1,0:T(8,128)}), f32[32,8,1024]{2,1,0:T(8,128)S(1)}, u32[]{:S(2)}, u32[]{:S(2)}) async-start(f32[32,8,1024]{2,1,0:T(8,128)} %bitcast.31), calls=%async_computation | async-start | bytes 2097152 | tf_op jit(solution)/shard_map/all_to_all | solution.py:386
  13.9 16.0 %slot_gradients.1 = (f32[32,4,4,2,8,128]{5,4,3,2,1,0:T(8,128)}, f32[16,1536]{1,0:T(8,128)}) custom-call(s32[16,2]{1,0:T(8,128)} %copy.8.counts_ref, bf16[16,2,512,256]{3,2,1,0:T(8,128)(2,1)} %out_ref.1, bf16[16,2,512,256]{3,2,1,0:T(8,128)(2,1)} %in_ref.1), custom_call_target="tpu_custom_call" | custom-call | flops 2147483648 | bytes 25165824 | tf_op jit(solution)/shard_map/slot_gradients/pallas_call | solution.py:43
  31.1 1.3 collective-permute-start
  32.4 2.5 %collective-permute-start.4 = (f32[12,1536]{1,0:T(8,128)S(1)}, f32[12,1536]{1,0:T(8,128)S(1)}, u32[]{:S(2)}, u32[]{:S(2)}) collective-permute-start(f32[12,1536]{1,0:T(8,128)S(1)} %get-tuple-element.46), channel_id=1, source_target_pairs={{0,2},{1,3},{2,0},{3,1},{4,6},{5,7},{6,4},{7,5},{8,10},{9,11},{10,... | collective-permute-start | bytes 221192 | tf_op jit(solution)/shard_map/ppermute | solution.py:324
  34.8 1.2 collective-permute-start.5
  36.7 2.3 %collective-permute-start.3 = (f32[1,24,1536]{2,1,0:T(8,128)S(1)}, f32[1,24,1536]{2,1,0:T(8,128)S(1)}, u32[]{:S(2)}, u32[]{:S(2)}) collective-permute-start(f32[1,24,1536]{2,1,0:T(8,128)S(1)} %maximum_bitcast_fusion), channel_id=1, source_target_pairs={{0,24},{4,28},{8,0},{12,4},{16,8},{20,12},{24,16},{28,20},{32,56},... | collective-permute-start | bytes 442376 | tf_op jit(solution)/shard_map/ppermute | solution.py:328
  40.2 2.6 %collective-permute-start.8 = (f32[1,24,1536]{2,1,0:T(8,128)S(1)}, f32[1,24,1536]{2,1,0:T(8,128)S(1)}, u32[]{:S(2)}, u32[]{:S(2)}) collective-permute-start(f32[1,24,1536]{2,1,0:T(8,128)S(1)} %maximum_bitcast_fusion.1), channel_id=1, source_target_pairs={{0,96},{4,100},{8,104},{12,108},{16,112},{20,116},{24,120},{28,124... | collective-permute-start | bytes 442376 | tf_op jit(solution)/shard_map/ppermute | solution.py:328
  44.6 4.2 %collective-permute-done.1 = f32[1,24,1536]{2,1,0:T(8,128)S(1)} collective-permute-done((f32[1,24,1536]{2,1,0:T(8,128)S(1)}, f32[1,24,1536]{2,1,0:T(8,128)S(1)}, u32[]{:S(2)}, u32[]{:S(2)}) %collective-permute-start.1) | collective-permute-done | bytes 147488 | tf_op jit(solution)/shard_map/ppermute | solution.py:328
  48.9 1.6 %collective-permute-done.6 = f32[1,24,1536]{2,1,0:T(8,128)S(1)} collective-permute-done((f32[1,24,1536]{2,1,0:T(8,128)S(1)}, f32[1,24,1536]{2,1,0:T(8,128)S(1)}, u32[]{:S(2)}, u32[]{:S(2)}) %collective-permute-start.6) | collective-permute-done | bytes 147488 | tf_op jit(solution)/shard_map/ppermute | solution.py:328
  54.8 1.7 %collective-permute-start.14 = (f32[4,24,1536]{2,1,0:T(8,128)S(1)}, f32[4,24,1536]{2,1,0:T(8,128)S(1)}, u32[]{:S(2)}, u32[]{:S(2)}) collective-permute-start(f32[4,24,1536]{2,1,0:T(8,128)S(1)} %pad_maximum_fusion.1.refs_4_), channel_id=1, source_target_pairs={{0,24},{4,28},{8,0},{12,4},{16,8},{20,12},{24,16},{28,20},{32,56},... | collective-permute-start | bytes 1769480 | tf_op jit(solution)/shard_map/ppermute | solution.py:328
  56.5 1.9 %collective-permute-start.13 = (f32[4,24,1536]{2,1,0:T(8,128)S(1)}, f32[4,24,1536]{2,1,0:T(8,128)}, u32[]{:S(2)}, u32[]{:S(2)}) collective-permute-start(f32[4,24,1536]{2,1,0:T(8,128)S(1)} %pad_maximum_fusion.1.refs_4_), channel_id=1, source_target_pairs={{0,16},{4,20},{8,24},{12,28},{16,0},{20,4},{24,8},{28,12},{32,48},... | collective-permute-start | bytes 1769480 | tf_op jit(solution)/shard_map/ppermute | solution.py:328
  58.3 3.8 %collective-permute-done.11.refs_3_ = f32[4,24,1536]{2,1,0:T(8,128)S(1)} collective-permute-done((f32[4,24,1536]{2,1,0:T(8,128)S(1)}, f32[4,24,1536]{2,1,0:T(8,128)S(1)}, u32[]{:S(2)}, u32[]{:S(2)}) %collective-permute-start.11) | collective-permute-done | bytes 589856 | tf_op jit(solution)/shard_map/ppermute | solution.py:328
  62.2 1.5 collective-permute-start.12
  66.2 1.4 fusion
  68.3 1.5 reshape.19.pairs_ref
  69.8 13.4 %collective-permute-done.9.refs_1_ = f32[4,24,1536]{2,1,0:T(8,128)S(1)} collective-permute-done((f32[4,24,1536]{2,1,0:T(8,128)S(1)}, f32[4,24,1536]{2,1,0:T(8,128)S(1)}, u32[]{:S(2)}, u32[]{:S(2)}) %collective-permute-start.9) | collective-permute-done | bytes 589856 | tf_op jit(solution)/shard_map/ppermute | solution.py:328
  83.5 10.9 %all-to-all-start.1 = ((f32[128,4,2,8,128]{4,3,2,1,0:T(8,128)}), f32[128,4,2,8,128]{4,3,2,1,0:T(8,128)}, u32[]{:S(2)}, u32[]{:S(2)}) async-start(f32[128,4,2,8,128]{4,3,2,1,0:T(8,128)} %bitcast.30), calls=%async_computation.1 | async-start | bytes 8388608 | tf_op jit(solution)/shard_map/all_to_all | solution.py:392
  94.4 1.2 collective-permute-start.15
  99.4 1.3 collective-permute-done.17.refs_10_
  100.7 1.7 %collective-permute-done.18.refs_11_ = f32[4,24,1536]{2,1,0:T(8,128)S(1)} collective-permute-done((f32[4,24,1536]{2,1,0:T(8,128)S(1)}, f32[4,24,1536]{2,1,0:T(8,128)S(1)}, u32[]{:S(2)}, u32[]{:S(2)}) %collective-permute-start.18) | collective-permute-done | bytes 589856 | tf_op jit(solution)/shard_map/ppermute | solution.py:368
  104.8 9.3 %arrange_rows.1 = (f32[512,1536]{1,0:T(8,128)}, f32[2,512,1536]{2,1,0:T(8,128)}) custom-call(s32[6]{0:T(128)} %stack.31.place_ref, s32[1,512]{1,0:T(1,128)} %reshape.19.pairs_ref, f32[4,24,1536]{2,1,0:T(8,128)} %copy-done.2, f32[4,24,1536]{2,1,0:T(8,128)} %copy-done.6, f32[4,24,1536]{2,1,0:T(8,128)} %copy-done.5, f32[4,24,1536]{2,1,0:T(8,128)} %copy-done.4, ...), custom_call_target="tpu_custom_call" | custom-call | flops 1 | bytes 1 | tf_op jit(solution)/shard_map/arrange_rows/pallas_call | solution.py:237
  114.1 34.6 %solve_and_update.1.update_ref = f32[512,2048]{1,0:T(8,128)} custom-call(s32[6]{0:T(128)} %stack.31.place_ref, f32[512,1536]{1,0:T(8,128)} %get-tuple-element.37.right_ref, f32[2,512,1536]{2,1,0:T(8,128)} %get-tuple-element.38.panels_ref, f32[2048,1536]{1,0:T(8,128)} %factor_ref.1), custom_call_target="tpu_custom_call" | custom-call | flops 1 | bytes 1 | tf_op jit(solution)/shard_map/solve_and_update/pallas_call | solution.py:299
  148.8 8.8 %place_rows.1 = f32[512,2048]{1,0:T(8,128)} custom-call(s32[6]{0:T(128)S(1)} %copy-done, s32[1,512]{1,0:T(1,128)S(1)} %copy-done.1, f32[8192,128]{1,0:T(8,128)} %bitcast.18.received_ref, f32[512,2048]{1,0:T(8,128)} %solve_and_update.1.update_ref), custom_call_target="tpu_custom_call" | custom-call | tf_op jit(solution)/shard_map/place_rows/pallas_call | solution.py:182
  (96 shorter events, 20.1 us)
Async XLA Ops:
  3.6 26.5 %all-to-all-start = ((f32[32,8,1024]{2,1,0:T(8,128)}), f32[32,8,1024]{2,1,0:T(8,128)S(1)}, u32[]{:S(2)}, u32[]{:S(2)}) async-start(f32[32,8,1024]{2,1,0:T(8,128)} %bitcast.31), calls=%async_computation | async-start | bytes 2097152 | tf_op jit(solution)/shard_map/all_to_all | solution.py:386
  31.1 5.5 %collective-permute-start = (f32[12,1536]{1,0:T(8,128)S(1)}, f32[12,1536]{1,0:T(8,128)S(1)}, u32[]{:S(2)}, u32[]{:S(2)}) collective-permute-start(f32[12,1536]{1,0:T(8,128)S(1)} %get-tuple-element.48), channel_id=1, source_target_pairs={{0,1},{1,2},{2,3},{3,0},{4,5},{5,6},{6,7},{7,4},{8,9},{9,10},{10,1... | collective-permute-start | bytes 221192 | tf_op jit(solution)/shard_map/ppermute | solution.py:324
  32.4 7.8 %collective-permute-start.4 = (f32[12,1536]{1,0:T(8,128)S(1)}, f32[12,1536]{1,0:T(8,128)S(1)}, u32[]{:S(2)}, u32[]{:S(2)}) collective-permute-start(f32[12,1536]{1,0:T(8,128)S(1)} %get-tuple-element.46), channel_id=1, source_target_pairs={{0,2},{1,3},{2,0},{3,1},{4,6},{5,7},{6,4},{7,5},{8,10},{9,11},{10,... | collective-permute-start | bytes 221192 | tf_op jit(solution)/shard_map/ppermute | solution.py:324
  34.8 5.3 %collective-permute-start.5 = (f32[12,1536]{1,0:T(8,128)S(1)}, f32[12,1536]{1,0:T(8,128)S(1)}, u32[]{:S(2)}, u32[]{:S(2)}) collective-permute-start(f32[12,1536]{1,0:T(8,128)S(1)} %get-tuple-element.47), channel_id=1, source_target_pairs={{0,3},{1,0},{2,1},{3,2},{4,7},{5,4},{6,5},{7,6},{8,11},{9,8},{10,9... | collective-permute-start | bytes 221192 | tf_op jit(solution)/shard_map/ppermute | solution.py:324
  36.7 6.6 %collective-permute-start.3 = (f32[1,24,1536]{2,1,0:T(8,128)S(1)}, f32[1,24,1536]{2,1,0:T(8,128)S(1)}, u32[]{:S(2)}, u32[]{:S(2)}) collective-permute-start(f32[1,24,1536]{2,1,0:T(8,128)S(1)} %maximum_bitcast_fusion), channel_id=1, source_target_pairs={{0,24},{4,28},{8,0},{12,4},{16,8},{20,12},{24,16},{28,20},{32,56},... | collective-permute-start | bytes 442376 | tf_op jit(solution)/shard_map/ppermute | solution.py:328
  39.0 5.6 %collective-permute-start.2 = (f32[1,24,1536]{2,1,0:T(8,128)S(1)}, f32[1,24,1536]{2,1,0:T(8,128)S(1)}, u32[]{:S(2)}, u32[]{:S(2)}) collective-permute-start(f32[1,24,1536]{2,1,0:T(8,128)S(1)} %maximum_bitcast_fusion), channel_id=1, source_target_pairs={{0,16},{4,20},{8,24},{12,28},{16,0},{20,4},{24,8},{28,12},{32,48},... | collective-permute-start | bytes 442376 | tf_op jit(solution)/shard_map/ppermute | solution.py:328
  39.6 9.2 %collective-permute-start.1 = (f32[1,24,1536]{2,1,0:T(8,128)S(1)}, f32[1,24,1536]{2,1,0:T(8,128)S(1)}, u32[]{:S(2)}, u32[]{:S(2)}) collective-permute-start(f32[1,24,1536]{2,1,0:T(8,128)S(1)} %maximum_bitcast_fusion), channel_id=1, source_target_pairs={{0,8},{4,12},{8,16},{12,20},{16,24},{20,28},{24,0},{28,4},{32,40},... | collective-permute-start | bytes 442376 | tf_op jit(solution)/shard_map/ppermute | solution.py:328
  40.2 8.6 %collective-permute-start.8 = (f32[1,24,1536]{2,1,0:T(8,128)S(1)}, f32[1,24,1536]{2,1,0:T(8,128)S(1)}, u32[]{:S(2)}, u32[]{:S(2)}) collective-permute-start(f32[1,24,1536]{2,1,0:T(8,128)S(1)} %maximum_bitcast_fusion.1), channel_id=1, source_target_pairs={{0,96},{4,100},{8,104},{12,108},{16,112},{20,116},{24,120},{28,124... | collective-permute-start | bytes 442376 | tf_op jit(solution)/shard_map/ppermute | solution.py:328
  42.8 6.1 %collective-permute-start.7 = (f32[1,24,1536]{2,1,0:T(8,128)S(1)}, f32[1,24,1536]{2,1,0:T(8,128)S(1)}, u32[]{:S(2)}, u32[]{:S(2)}) collective-permute-start(f32[1,24,1536]{2,1,0:T(8,128)S(1)} %maximum_bitcast_fusion.1), channel_id=1, source_target_pairs={{0,64},{4,68},{8,72},{12,76},{16,80},{20,84},{24,88},{28,92},{32,9... | collective-permute-start | bytes 442376 | tf_op jit(solution)/shard_map/ppermute | solution.py:328
  43.3 7.2 %collective-permute-start.6 = (f32[1,24,1536]{2,1,0:T(8,128)S(1)}, f32[1,24,1536]{2,1,0:T(8,128)S(1)}, u32[]{:S(2)}, u32[]{:S(2)}) collective-permute-start(f32[1,24,1536]{2,1,0:T(8,128)S(1)} %maximum_bitcast_fusion.1), channel_id=1, source_target_pairs={{0,32},{4,36},{8,40},{12,44},{16,48},{20,52},{24,56},{28,60},{32,6... | collective-permute-start | bytes 442376 | tf_op jit(solution)/shard_map/ppermute | solution.py:328
  50.5 11.7 %collective-permute-start.11 = (f32[4,24,1536]{2,1,0:T(8,128)S(1)}, f32[4,24,1536]{2,1,0:T(8,128)S(1)}, u32[]{:S(2)}, u32[]{:S(2)}) collective-permute-start(f32[4,24,1536]{2,1,0:T(8,128)S(1)} %pad_maximum_fusion.refs_0_), channel_id=1, source_target_pairs={{0,96},{4,100},{8,104},{12,108},{16,112},{20,116},{24,120},{28,124... | collective-permute-start | bytes 1769480 | tf_op jit(solution)/shard_map/ppermute | solution.py:328
  53.7 16.1 %collective-permute-start.10 = (f32[4,24,1536]{2,1,0:T(8,128)S(1)}, f32[4,24,1536]{2,1,0:T(8,128)S(1)}, u32[]{:S(2)}, u32[]{:S(2)}) collective-permute-start(f32[4,24,1536]{2,1,0:T(8,128)S(1)} %pad_maximum_fusion.refs_0_), channel_id=1, source_target_pairs={{0,64},{4,68},{8,72},{12,76},{16,80},{20,84},{24,88},{28,92},{32,9... | collective-permute-start | bytes 1769480 | tf_op jit(solution)/shard_map/ppermute | solution.py:328
  54.3 29.0 %collective-permute-start.9 = (f32[4,24,1536]{2,1,0:T(8,128)S(1)}, f32[4,24,1536]{2,1,0:T(8,128)S(1)}, u32[]{:S(2)}, u32[]{:S(2)}) collective-permute-start(f32[4,24,1536]{2,1,0:T(8,128)S(1)} %pad_maximum_fusion.refs_0_), channel_id=1, source_target_pairs={{0,32},{4,36},{8,40},{12,44},{16,48},{20,52},{24,56},{28,60},{32,6... | collective-permute-start | bytes 1769480 | tf_op jit(solution)/shard_map/ppermute | solution.py:328
  54.8 28.4 %collective-permute-start.14 = (f32[4,24,1536]{2,1,0:T(8,128)S(1)}, f32[4,24,1536]{2,1,0:T(8,128)S(1)}, u32[]{:S(2)}, u32[]{:S(2)}) collective-permute-start(f32[4,24,1536]{2,1,0:T(8,128)S(1)} %pad_maximum_fusion.1.refs_4_), channel_id=1, source_target_pairs={{0,24},{4,28},{8,0},{12,4},{16,8},{20,12},{24,16},{28,20},{32,56},... | collective-permute-start | bytes 1769480 | tf_op jit(solution)/shard_map/ppermute | solution.py:328
  56.5 26.8 %collective-permute-start.13 = (f32[4,24,1536]{2,1,0:T(8,128)S(1)}, f32[4,24,1536]{2,1,0:T(8,128)}, u32[]{:S(2)}, u32[]{:S(2)}) collective-permute-start(f32[4,24,1536]{2,1,0:T(8,128)S(1)} %pad_maximum_fusion.1.refs_4_), channel_id=1, source_target_pairs={{0,16},{4,20},{8,24},{12,28},{16,0},{20,4},{24,8},{28,12},{32,48},... | collective-permute-start | bytes 1769480 | tf_op jit(solution)/shard_map/ppermute | solution.py:328
  62.2 21.3 %collective-permute-start.12 = (f32[4,24,1536]{2,1,0:T(8,128)S(1)}, f32[4,24,1536]{2,1,0:T(8,128)}, u32[]{:S(2)}, u32[]{:S(2)}) collective-permute-start(f32[4,24,1536]{2,1,0:T(8,128)S(1)} %pad_maximum_fusion.1.refs_4_), channel_id=1, source_target_pairs={{0,8},{4,12},{8,16},{12,20},{16,24},{20,28},{24,0},{28,4},{32,40},... | collective-permute-start | bytes 1769480 | tf_op jit(solution)/shard_map/ppermute | solution.py:328
  83.5 65.3 %all-to-all-start.1 = ((f32[128,4,2,8,128]{4,3,2,1,0:T(8,128)}), f32[128,4,2,8,128]{4,3,2,1,0:T(8,128)}, u32[]{:S(2)}, u32[]{:S(2)}) async-start(f32[128,4,2,8,128]{4,3,2,1,0:T(8,128)} %bitcast.30), calls=%async_computation.1 | async-start | bytes 8388608 | tf_op jit(solution)/shard_map/all_to_all | solution.py:392
  94.4 2.9 %collective-permute-start.15 = (f32[4,24,1536]{2,1,0:T(8,128)S(1)}, f32[4,24,1536]{2,1,0:T(8,128)S(1)}, u32[]{:S(2)}, u32[]{:S(2)}) collective-permute-start(f32[4,24,1536]{2,1,0:T(8,128)S(1)} %pad_maximum_fusion.refs_0_), channel_id=1, source_target_pairs={{0,4},{4,0},{8,12},{12,8},{16,20},{20,16},{24,28},{28,24},{32,36},... | collective-permute-start | bytes 1769480 | tf_op jit(solution)/shard_map/ppermute | solution.py:368
  95.8 3.2 %collective-permute-start.16 = (f32[4,24,1536]{2,1,0:T(8,128)S(1)}, f32[4,24,1536]{2,1,0:T(8,128)S(1)}, u32[]{:S(2)}, u32[]{:S(2)}) collective-permute-start(f32[4,24,1536]{2,1,0:T(8,128)S(1)} %collective-permute-done.9.refs_1_), channel_id=1, source_target_pairs={{0,4},{4,0},{8,12},{12,8},{16,20},{20,16},{24,28},{28,24},{32,36},... | collective-permute-start | bytes 1769480 | tf_op jit(solution)/shard_map/ppermute | solution.py:368
  96.2 4.5 %collective-permute-start.17 = (f32[4,24,1536]{2,1,0:T(8,128)S(1)}, f32[4,24,1536]{2,1,0:T(8,128)S(1)}, u32[]{:S(2)}, u32[]{:S(2)}) collective-permute-start(f32[4,24,1536]{2,1,0:T(8,128)S(1)} %collective-permute-done.10.refs_2_), channel_id=1, source_target_pairs={{0,4},{4,0},{8,12},{12,8},{16,20},{20,16},{24,28},{28,24},{32,36},... | collective-permute-start | bytes 1769480 | tf_op jit(solution)/shard_map/ppermute | solution.py:368
  96.3 6.1 %collective-permute-start.18 = (f32[4,24,1536]{2,1,0:T(8,128)S(1)}, f32[4,24,1536]{2,1,0:T(8,128)S(1)}, u32[]{:S(2)}, u32[]{:S(2)}) collective-permute-start(f32[4,24,1536]{2,1,0:T(8,128)S(1)} %collective-permute-done.11.refs_3_), channel_id=1, source_target_pairs={{0,4},{4,0},{8,12},{12,8},{16,20},{20,16},{24,28},{28,24},{32,36},... | collective-permute-start | bytes 1769480 | tf_op jit(solution)/shard_map/ppermute | solution.py:368
  97.3 5.1 %collective-permute-start.20 = (f32[4,24,1536]{2,1,0:T(8,128)}, f32[4,24,1536]{2,1,0:T(8,128)S(1)}, u32[]{:S(2)}, u32[]{:S(2)}) collective-permute-start(f32[4,24,1536]{2,1,0:T(8,128)} %collective-permute-done.12.refs_5_), channel_id=1, source_target_pairs={{0,4},{4,0},{8,12},{12,8},{16,20},{20,16},{24,28},{28,24},{32,36},... | collective-permute-start | bytes 1769480 | tf_op jit(solution)/shard_map/ppermute | solution.py:368
  98.1 4.4 %collective-permute-start.21 = (f32[4,24,1536]{2,1,0:T(8,128)}, f32[4,24,1536]{2,1,0:T(8,128)S(1)}, u32[]{:S(2)}, u32[]{:S(2)}) collective-permute-start(f32[4,24,1536]{2,1,0:T(8,128)} %collective-permute-done.13.refs_6_), channel_id=1, source_target_pairs={{0,4},{4,0},{8,12},{12,8},{16,20},{20,16},{24,28},{28,24},{32,36},... | collective-permute-start | bytes 1769480 | tf_op jit(solution)/shard_map/ppermute | solution.py:368
  99.0 4.2 %collective-permute-start.22 = (f32[4,24,1536]{2,1,0:T(8,128)S(1)}, f32[4,24,1536]{2,1,0:T(8,128)S(1)}, u32[]{:S(2)}, u32[]{:S(2)}) collective-permute-start(f32[4,24,1536]{2,1,0:T(8,128)S(1)} %collective-permute-done.14.refs_7_), channel_id=1, source_target_pairs={{0,4},{4,0},{8,12},{12,8},{16,20},{20,16},{24,28},{28,24},{32,36},... | collective-permute-start | bytes 1769480 | tf_op jit(solution)/shard_map/ppermute | solution.py:368
  (18 other events, 282.9 us)

commit v4 on v3

--- a/solution.py
+++ b/solution.py
@@ -103,7 +103,9 @@
 
 def invert_kernel(d_ref, x_ref):
     def dot(a, b):
-        return jnp.dot(a, b, precision=HIGHEST, preferred_element_type=jnp.float32)
+        (a, a_low), (b, b_low) = split(a), split(b)
+        product = lambda x, y: jnp.dot(x, y, preferred_element_type=jnp.float32)
+        return product(a, b) + (product(a, b_low) + product(a_low, b))
 
     base = 128
     row = lax.broadcasted_iota(jnp.int32, (base, base), 0)

time: 159 us -> 157 us (0.987)
  Pallas kernels: 71.7 us -> 65.2 us
  waiting for transfers between devices: 29.5 us -> 34.8 us
    pallas_call x1, Pallas kernels: 34.6 us -> 28.2 us  [solve_and_update(): pl.pallas_call(solve_kernel, grid=(rows // width,), in_specs=[pl.BlockSpe...]
    all_to_all x1, waiting for transfers between devices: 0.01 us -> 5.26 us  [per_device(): lax.all_to_all(send.reshape((n_feat * n_pair,) + send.shape[2:]), ('feat'...]
  transfers between devices with their start and end apart: 25 -> 25, of which waited for: 14 -> 15; matrix products, arithmetic and copies ran while one was open for 6% -> 6% of each run, Pallas kernels for 38% -> 34%
where the time goes in v4:
time: 157 us; the launch traced here: 156 us
  Pallas kernels  65.2 us (42%)
  starting transfers between devices  43 us (27%)
  waiting for transfers between devices  34.8 us (22%)
  local copies, waits for them, and re-layouts  7.58 us (5%)
  other arithmetic  4.13 us (3%)
    pallas_call x1, Pallas kernels, solve_and_update(): pl.pallas_call(solve_kernel, grid=(rows // width,), in_specs=[pl.BlockSpe...  28.2 us
    ppermute x12, waiting for transfers between devices, along(): return lax.ppermute(value, 'feat', [(f, ring(f)) for f in range(n_feat)])  24 us
    pallas_call x1, Pallas kernels, slot_gradients(): pl.pallas_call(gradient_kernel, grid_spec=pltpu.PrefetchScalarGridSpec(nu...  16 us
    ppermute x12, starting transfers between devices, along(): return lax.ppermute(value, 'feat', [(f, ring(f)) for f in range(n_feat)])  14.2 us
    all_to_all x1, starting transfers between devices, per_device(): lax.all_to_all(send.reshape((n_feat * n_pair,) + send.shape[2:]), ('feat'...  10.9 us
    all_to_all x1, starting transfers between devices, per_device(): lax.all_to_all(outgoing.reshape((n_feat,) + outgoing.shape[2:]), 'feat',...  9.6 us
    pallas_call x1, Pallas kernels, arrange_rows(): pl.pallas_call(arrange_kernel, grid=(width // PANEL,), in_specs=[pl.Block...  9.29 us
    pallas_call x1, Pallas kernels, place_rows(): pl.pallas_call(place_kernel, grid=(total // rows,), in_specs=[pl.BlockSpe...  8.8 us
  transfers between devices with their start and end apart: 25, of which 15 were waited for; matrix products, arithmetic and copies ran while one was open for 6% of the time, Pallas kernels for 34%

profile of v4, /device:TPU:1, one launch (start us, length us, event | category | flops | bytes accessed | tf_op | source)
XLA Modules:
  0.0 156.3 jit_solution(766106337525303840)
XLA Ops:
  0.6 3.0 %cut_panel.1 = f32[16,2,8,1024]{3,2,1,0:T(8,128)} custom-call(s32[6]{0:T(128)} %stack.31.place_ref, f32[2048,1536]{1,0:T(8,128)} %factor_ref.1), custom_call_target="tpu_custom_call" | custom-call | tf_op jit(solution)/shard_map/cut_panel/pallas_call | solution.py:90
  3.6 9.6 %all-to-all-start = ((f32[32,8,1024]{2,1,0:T(8,128)}), f32[32,8,1024]{2,1,0:T(8,128)S(1)}, u32[]{:S(2)}, u32[]{:S(2)}) async-start(f32[32,8,1024]{2,1,0:T(8,128)} %bitcast.31), calls=%async_computation | async-start | bytes 2097152 | tf_op jit(solution)/shard_map/all_to_all | solution.py:388
  13.9 16.0 %slot_gradients.1 = (f32[32,4,4,2,8,128]{5,4,3,2,1,0:T(8,128)}, f32[16,1536]{1,0:T(8,128)}) custom-call(s32[16,2]{1,0:T(8,128)} %copy.8.counts_ref, bf16[16,2,512,256]{3,2,1,0:T(8,128)(2,1)} %out_ref.1, bf16[16,2,512,256]{3,2,1,0:T(8,128)(2,1)} %in_ref.1), custom_call_target="tpu_custom_call" | custom-call | flops 2147483648 | bytes 25165824 | tf_op jit(solution)/shard_map/slot_gradients/pallas_call | solution.py:43
  31.1 1.3 collective-permute-start
  32.4 2.5 %collective-permute-start.4 = (f32[12,1536]{1,0:T(8,128)S(1)}, f32[12,1536]{1,0:T(8,128)S(1)}, u32[]{:S(2)}, u32[]{:S(2)}) collective-permute-start(f32[12,1536]{1,0:T(8,128)S(1)} %get-tuple-element.46), channel_id=1, source_target_pairs={{0,2},{1,3},{2,0},{3,1},{4,6},{5,7},{6,4},{7,5},{8,10},{9,11},{10,... | collective-permute-start | bytes 221192 | tf_op jit(solution)/shard_map/ppermute | solution.py:326
  36.7 2.3 %collective-permute-start.3 = (f32[1,24,1536]{2,1,0:T(8,128)S(1)}, f32[1,24,1536]{2,1,0:T(8,128)S(1)}, u32[]{:S(2)}, u32[]{:S(2)}) collective-permute-start(f32[1,24,1536]{2,1,0:T(8,128)S(1)} %maximum_bitcast_fusion), channel_id=1, source_target_pairs={{0,24},{4,28},{8,0},{12,4},{16,8},{20,12},{24,16},{28,20},{32,56},... | collective-permute-start | bytes 442376 | tf_op jit(solution)/shard_map/ppermute | solution.py:330
  40.2 2.6 %collective-permute-start.8 = (f32[1,24,1536]{2,1,0:T(8,128)S(1)}, f32[1,24,1536]{2,1,0:T(8,128)S(1)}, u32[]{:S(2)}, u32[]{:S(2)}) collective-permute-start(f32[1,24,1536]{2,1,0:T(8,128)S(1)} %maximum_bitcast_fusion.1), channel_id=1, source_target_pairs={{0,96},{4,100},{8,104},{12,108},{16,112},{20,116},{24,120},{28,124... | collective-permute-start | bytes 442376 | tf_op jit(solution)/shard_map/ppermute | solution.py:330
  44.6 4.2 %collective-permute-done.1 = f32[1,24,1536]{2,1,0:T(8,128)S(1)} collective-permute-done((f32[1,24,1536]{2,1,0:T(8,128)S(1)}, f32[1,24,1536]{2,1,0:T(8,128)S(1)}, u32[]{:S(2)}, u32[]{:S(2)}) %collective-permute-start.1) | collective-permute-done | bytes 147488 | tf_op jit(solution)/shard_map/ppermute | solution.py:330
  48.9 1.6 %collective-permute-done.6 = f32[1,24,1536]{2,1,0:T(8,128)S(1)} collective-permute-done((f32[1,24,1536]{2,1,0:T(8,128)S(1)}, f32[1,24,1536]{2,1,0:T(8,128)S(1)}, u32[]{:S(2)}, u32[]{:S(2)}) %collective-permute-start.6) | collective-permute-done | bytes 147488 | tf_op jit(solution)/shard_map/ppermute | solution.py:330
  54.8 1.7 %collective-permute-start.14 = (f32[4,24,1536]{2,1,0:T(8,128)S(1)}, f32[4,24,1536]{2,1,0:T(8,128)S(1)}, u32[]{:S(2)}, u32[]{:S(2)}) collective-permute-start(f32[4,24,1536]{2,1,0:T(8,128)S(1)} %pad_maximum_fusion.1.refs_4_), channel_id=1, source_target_pairs={{0,24},{4,28},{8,0},{12,4},{16,8},{20,12},{24,16},{28,20},{32,56},... | collective-permute-start | bytes 1769480 | tf_op jit(solution)/shard_map/ppermute | solution.py:330
  56.5 1.9 %collective-permute-start.13 = (f32[4,24,1536]{2,1,0:T(8,128)S(1)}, f32[4,24,1536]{2,1,0:T(8,128)}, u32[]{:S(2)}, u32[]{:S(2)}) collective-permute-start(f32[4,24,1536]{2,1,0:T(8,128)S(1)} %pad_maximum_fusion.1.refs_4_), channel_id=1, source_target_pairs={{0,16},{4,20},{8,24},{12,28},{16,0},{20,4},{24,8},{28,12},{32,48},... | collective-permute-start | bytes 1769480 | tf_op jit(solution)/shard_map/ppermute | solution.py:330
  58.3 3.8 %collective-permute-done.11.refs_3_ = f32[4,24,1536]{2,1,0:T(8,128)S(1)} collective-permute-done((f32[4,24,1536]{2,1,0:T(8,128)S(1)}, f32[4,24,1536]{2,1,0:T(8,128)S(1)}, u32[]{:S(2)}, u32[]{:S(2)}) %collective-permute-start.11) | collective-permute-done | bytes 589856 | tf_op jit(solution)/shard_map/ppermute | solution.py:330
  62.2 1.5 collective-permute-start.12
  66.2 1.4 fusion
  68.3 1.5 reshape.19.pairs_ref
  69.8 13.4 %collective-permute-done.9.refs_1_ = f32[4,24,1536]{2,1,0:T(8,128)S(1)} collective-permute-done((f32[4,24,1536]{2,1,0:T(8,128)S(1)}, f32[4,24,1536]{2,1,0:T(8,128)S(1)}, u32[]{:S(2)}, u32[]{:S(2)}) %collective-permute-start.9) | collective-permute-done | bytes 589856 | tf_op jit(solution)/shard_map/ppermute | solution.py:330
  83.5 10.9 %all-to-all-start.1 = ((f32[128,4,2,8,128]{4,3,2,1,0:T(8,128)}), f32[128,4,2,8,128]{4,3,2,1,0:T(8,128)}, u32[]{:S(2)}, u32[]{:S(2)}) async-start(f32[128,4,2,8,128]{4,3,2,1,0:T(8,128)} %bitcast.30), calls=%async_computation.1 | async-start | bytes 8388608 | tf_op jit(solution)/shard_map/all_to_all | solution.py:394
  94.4 1.2 collective-permute-start.15
  99.4 1.3 collective-permute-done.17.refs_10_
  100.7 1.7 %collective-permute-done.18.refs_11_ = f32[4,24,1536]{2,1,0:T(8,128)S(1)} collective-permute-done((f32[4,24,1536]{2,1,0:T(8,128)S(1)}, f32[4,24,1536]{2,1,0:T(8,128)S(1)}, u32[]{:S(2)}, u32[]{:S(2)}) %collective-permute-start.18) | collective-permute-done | bytes 589856 | tf_op jit(solution)/shard_map/ppermute | solution.py:370
  104.8 9.3 %arrange_rows.1 = (f32[512,1536]{1,0:T(8,128)}, f32[2,512,1536]{2,1,0:T(8,128)}) custom-call(s32[6]{0:T(128)} %stack.31.place_ref, s32[1,512]{1,0:T(1,128)} %reshape.19.pairs_ref, f32[4,24,1536]{2,1,0:T(8,128)} %copy-done.2, f32[4,24,1536]{2,1,0:T(8,128)} %copy-done.6, f32[4,24,1536]{2,1,0:T(8,128)} %copy-done.5, f32[4,24,1536]{2,1,0:T(8,128)} %copy-done.4, ...), custom_call_target="tpu_custom_call" | custom-call | flops 1 | bytes 1 | tf_op jit(solution)/shard_map/arrange_rows/pallas_call | solution.py:239
  114.1 28.2 %solve_and_update.1.update_ref = f32[512,2048]{1,0:T(8,128)} custom-call(s32[6]{0:T(128)} %stack.31.place_ref, f32[512,1536]{1,0:T(8,128)} %get-tuple-element.37.right_ref, f32[2,512,1536]{2,1,0:T(8,128)} %get-tuple-element.38.panels_ref, f32[2048,1536]{1,0:T(8,128)} %factor_ref.1), custom_call_target="tpu_custom_call" | custom-call | flops 1 | bytes 1 | tf_op jit(solution)/shard_map/solve_and_update/pallas_call | solution.py:301
  142.3 5.3 %all-to-all-done.1 = f32[128,4,2,8,128]{4,3,2,1,0:T(8,128)} async-done(((f32[128,4,2,8,128]{4,3,2,1,0:T(8,128)}), f32[128,4,2,8,128]{4,3,2,1,0:T(8,128)}, u32[]{:S(2)}, u32[]{:S(2)}) %all-to-all-start.1) | async-done | bytes 4194336 | tf_op jit(solution)/shard_map/all_to_all | solution.py:394
  147.5 8.8 %place_rows.1 = f32[512,2048]{1,0:T(8,128)} custom-call(s32[6]{0:T(128)S(1)} %copy-done, s32[1,512]{1,0:T(1,128)S(1)} %copy-done.1, f32[8192,128]{1,0:T(8,128)} %bitcast.18.received_ref, f32[512,2048]{1,0:T(8,128)} %solve_and_update.1.update_ref), custom_call_target="tpu_custom_call" | custom-call | tf_op jit(solution)/shard_map/place_rows/pallas_call | solution.py:184
  (96 shorter events, 21.2 us)
Async XLA Ops:
  3.6 26.5 %all-to-all-start = ((f32[32,8,1024]{2,1,0:T(8,128)}), f32[32,8,1024]{2,1,0:T(8,128)S(1)}, u32[]{:S(2)}, u32[]{:S(2)}) async-start(f32[32,8,1024]{2,1,0:T(8,128)} %bitcast.31), calls=%async_computation | async-start | bytes 2097152 | tf_op jit(solution)/shard_map/all_to_all | solution.py:388
  31.1 5.5 %collective-permute-start = (f32[12,1536]{1,0:T(8,128)S(1)}, f32[12,1536]{1,0:T(8,128)S(1)}, u32[]{:S(2)}, u32[]{:S(2)}) collective-permute-start(f32[12,1536]{1,0:T(8,128)S(1)} %get-tuple-element.48), channel_id=1, source_target_pairs={{0,1},{1,2},{2,3},{3,0},{4,5},{5,6},{6,7},{7,4},{8,9},{9,10},{10,1... | collective-permute-start | bytes 221192 | tf_op jit(solution)/shard_map/ppermute | solution.py:326
  32.4 7.8 %collective-permute-start.4 = (f32[12,1536]{1,0:T(8,128)S(1)}, f32[12,1536]{1,0:T(8,128)S(1)}, u32[]{:S(2)}, u32[]{:S(2)}) collective-permute-start(f32[12,1536]{1,0:T(8,128)S(1)} %get-tuple-element.46), channel_id=1, source_target_pairs={{0,2},{1,3},{2,0},{3,1},{4,6},{5,7},{6,4},{7,5},{8,10},{9,11},{10,... | collective-permute-start | bytes 221192 | tf_op jit(solution)/shard_map/ppermute | solution.py:326
  34.8 5.3 %collective-permute-start.5 = (f32[12,1536]{1,0:T(8,128)S(1)}, f32[12,1536]{1,0:T(8,128)S(1)}, u32[]{:S(2)}, u32[]{:S(2)}) collective-permute-start(f32[12,1536]{1,0:T(8,128)S(1)} %get-tuple-element.47), channel_id=1, source_target_pairs={{0,3},{1,0},{2,1},{3,2},{4,7},{5,4},{6,5},{7,6},{8,11},{9,8},{10,9... | collective-permute-start | bytes 221192 | tf_op jit(solution)/shard_map/ppermute | solution.py:326
  36.7 6.6 %collective-permute-start.3 = (f32[1,24,1536]{2,1,0:T(8,128)S(1)}, f32[1,24,1536]{2,1,0:T(8,128)S(1)}, u32[]{:S(2)}, u32[]{:S(2)}) collective-permute-start(f32[1,24,1536]{2,1,0:T(8,128)S(1)} %maximum_bitcast_fusion), channel_id=1, source_target_pairs={{0,24},{4,28},{8,0},{12,4},{16,8},{20,12},{24,16},{28,20},{32,56},... | collective-permute-start | bytes 442376 | tf_op jit(solution)/shard_map/ppermute | solution.py:330
  39.0 5.6 %collective-permute-start.2 = (f32[1,24,1536]{2,1,0:T(8,128)S(1)}, f32[1,24,1536]{2,1,0:T(8,128)S(1)}, u32[]{:S(2)}, u32[]{:S(2)}) collective-permute-start(f32[1,24,1536]{2,1,0:T(8,128)S(1)} %maximum_bitcast_fusion), channel_id=1, source_target_pairs={{0,16},{4,20},{8,24},{12,28},{16,0},{20,4},{24,8},{28,12},{32,48},... | collective-permute-start | bytes 442376 | tf_op jit(solution)/shard_map/ppermute | solution.py:330
  39.6 9.2 %collective-permute-start.1 = (f32[1,24,1536]{2,1,0:T(8,128)S(1)}, f32[1,24,1536]{2,1,0:T(8,128)S(1)}, u32[]{:S(2)}, u32[]{:S(2)}) collective-permute-start(f32[1,24,1536]{2,1,0:T(8,128)S(1)} %maximum_bitcast_fusion), channel_id=1, source_target_pairs={{0,8},{4,12},{8,16},{12,20},{16,24},{20,28},{24,0},{28,4},{32,40},... | collective-permute-start | bytes 442376 | tf_op jit(solution)/shard_map/ppermute | solution.py:330
  40.2 8.6 %collective-permute-start.8 = (f32[1,24,1536]{2,1,0:T(8,128)S(1)}, f32[1,24,1536]{2,1,0:T(8,128)S(1)}, u32[]{:S(2)}, u32[]{:S(2)}) collective-permute-start(f32[1,24,1536]{2,1,0:T(8,128)S(1)} %maximum_bitcast_fusion.1), channel_id=1, source_target_pairs={{0,96},{4,100},{8,104},{12,108},{16,112},{20,116},{24,120},{28,124... | collective-permute-start | bytes 442376 | tf_op jit(solution)/shard_map/ppermute | solution.py:330
  42.8 6.1 %collective-permute-start.7 = (f32[1,24,1536]{2,1,0:T(8,128)S(1)}, f32[1,24,1536]{2,1,0:T(8,128)S(1)}, u32[]{:S(2)}, u32[]{:S(2)}) collective-permute-start(f32[1,24,1536]{2,1,0:T(8,128)S(1)} %maximum_bitcast_fusion.1), channel_id=1, source_target_pairs={{0,64},{4,68},{8,72},{12,76},{16,80},{20,84},{24,88},{28,92},{32,9... | collective-permute-start | bytes 442376 | tf_op jit(solution)/shard_map/ppermute | solution.py:330
  43.3 7.2 %collective-permute-start.6 = (f32[1,24,1536]{2,1,0:T(8,128)S(1)}, f32[1,24,1536]{2,1,0:T(8,128)S(1)}, u32[]{:S(2)}, u32[]{:S(2)}) collective-permute-start(f32[1,24,1536]{2,1,0:T(8,128)S(1)} %maximum_bitcast_fusion.1), channel_id=1, source_target_pairs={{0,32},{4,36},{8,40},{12,44},{16,48},{20,52},{24,56},{28,60},{32,6... | collective-permute-start | bytes 442376 | tf_op jit(solution)/shard_map/ppermute | solution.py:330
  50.5 11.7 %collective-permute-start.11 = (f32[4,24,1536]{2,1,0:T(8,128)S(1)}, f32[4,24,1536]{2,1,0:T(8,128)S(1)}, u32[]{:S(2)}, u32[]{:S(2)}) collective-permute-start(f32[4,24,1536]{2,1,0:T(8,128)S(1)} %pad_maximum_fusion.refs_0_), channel_id=1, source_target_pairs={{0,96},{4,100},{8,104},{12,108},{16,112},{20,116},{24,120},{28,124... | collective-permute-start | bytes 1769480 | tf_op jit(solution)/shard_map/ppermute | solution.py:330
  53.7 16.1 %collective-permute-start.10 = (f32[4,24,1536]{2,1,0:T(8,128)S(1)}, f32[4,24,1536]{2,1,0:T(8,128)S(1)}, u32[]{:S(2)}, u32[]{:S(2)}) collective-permute-start(f32[4,24,1536]{2,1,0:T(8,128)S(1)} %pad_maximum_fusion.refs_0_), channel_id=1, source_target_pairs={{0,64},{4,68},{8,72},{12,76},{16,80},{20,84},{24,88},{28,92},{32,9... | collective-permute-start | bytes 1769480 | tf_op jit(solution)/shard_map/ppermute | solution.py:330
  54.3 29.0 %collective-permute-start.9 = (f32[4,24,1536]{2,1,0:T(8,128)S(1)}, f32[4,24,1536]{2,1,0:T(8,128)S(1)}, u32[]{:S(2)}, u32[]{:S(2)}) collective-permute-start(f32[4,24,1536]{2,1,0:T(8,128)S(1)} %pad_maximum_fusion.refs_0_), channel_id=1, source_target_pairs={{0,32},{4,36},{8,40},{12,44},{16,48},{20,52},{24,56},{28,60},{32,6... | collective-permute-start | bytes 1769480 | tf_op jit(solution)/shard_map/ppermute | solution.py:330
  54.8 28.4 %collective-permute-start.14 = (f32[4,24,1536]{2,1,0:T(8,128)S(1)}, f32[4,24,1536]{2,1,0:T(8,128)S(1)}, u32[]{:S(2)}, u32[]{:S(2)}) collective-permute-start(f32[4,24,1536]{2,1,0:T(8,128)S(1)} %pad_maximum_fusion.1.refs_4_), channel_id=1, source_target_pairs={{0,24},{4,28},{8,0},{12,4},{16,8},{20,12},{24,16},{28,20},{32,56},... | collective-permute-start | bytes 1769480 | tf_op jit(solution)/shard_map/ppermute | solution.py:330
  56.5 26.8 %collective-permute-start.13 = (f32[4,24,1536]{2,1,0:T(8,128)S(1)}, f32[4,24,1536]{2,1,0:T(8,128)}, u32[]{:S(2)}, u32[]{:S(2)}) collective-permute-start(f32[4,24,1536]{2,1,0:T(8,128)S(1)} %pad_maximum_fusion.1.refs_4_), channel_id=1, source_target_pairs={{0,16},{4,20},{8,24},{12,28},{16,0},{20,4},{24,8},{28,12},{32,48},... | collective-permute-start | bytes 1769480 | tf_op jit(solution)/shard_map/ppermute | solution.py:330
  62.2 21.3 %collective-permute-start.12 = (f32[4,24,1536]{2,1,0:T(8,128)S(1)}, f32[4,24,1536]{2,1,0:T(8,128)}, u32[]{:S(2)}, u32[]{:S(2)}) collective-permute-start(f32[4,24,1536]{2,1,0:T(8,128)S(1)} %pad_maximum_fusion.1.refs_4_), channel_id=1, source_target_pairs={{0,8},{4,12},{8,16},{12,20},{16,24},{20,28},{24,0},{28,4},{32,40},... | collective-permute-start | bytes 1769480 | tf_op jit(solution)/shard_map/ppermute | solution.py:330
  83.5 64.1 %all-to-all-start.1 = ((f32[128,4,2,8,128]{4,3,2,1,0:T(8,128)}), f32[128,4,2,8,128]{4,3,2,1,0:T(8,128)}, u32[]{:S(2)}, u32[]{:S(2)}) async-start(f32[128,4,2,8,128]{4,3,2,1,0:T(8,128)} %bitcast.30), calls=%async_computation.1 | async-start | bytes 8388608 | tf_op jit(solution)/shard_map/all_to_all | solution.py:394
  94.4 2.9 %collective-permute-start.15 = (f32[4,24,1536]{2,1,0:T(8,128)S(1)}, f32[4,24,1536]{2,1,0:T(8,128)S(1)}, u32[]{:S(2)}, u32[]{:S(2)}) collective-permute-start(f32[4,24,1536]{2,1,0:T(8,128)S(1)} %pad_maximum_fusion.refs_0_), channel_id=1, source_target_pairs={{0,4},{4,0},{8,12},{12,8},{16,20},{20,16},{24,28},{28,24},{32,36},... | collective-permute-start | bytes 1769480 | tf_op jit(solution)/shard_map/ppermute | solution.py:370
  95.8 3.2 %collective-permute-start.16 = (f32[4,24,1536]{2,1,0:T(8,128)S(1)}, f32[4,24,1536]{2,1,0:T(8,128)S(1)}, u32[]{:S(2)}, u32[]{:S(2)}) collective-permute-start(f32[4,24,1536]{2,1,0:T(8,128)S(1)} %collective-permute-done.9.refs_1_), channel_id=1, source_target_pairs={{0,4},{4,0},{8,12},{12,8},{16,20},{20,16},{24,28},{28,24},{32,36},... | collective-permute-start | bytes 1769480 | tf_op jit(solution)/shard_map/ppermute | solution.py:370
  96.2 4.5 %collective-permute-start.17 = (f32[4,24,1536]{2,1,0:T(8,128)S(1)}, f32[4,24,1536]{2,1,0:T(8,128)S(1)}, u32[]{:S(2)}, u32[]{:S(2)}) collective-permute-start(f32[4,24,1536]{2,1,0:T(8,128)S(1)} %collective-permute-done.10.refs_2_), channel_id=1, source_target_pairs={{0,4},{4,0},{8,12},{12,8},{16,20},{20,16},{24,28},{28,24},{32,36},... | collective-permute-start | bytes 1769480 | tf_op jit(solution)/shard_map/ppermute | solution.py:370
  96.3 6.1 %collective-permute-start.18 = (f32[4,24,1536]{2,1,0:T(8,128)S(1)}, f32[4,24,1536]{2,1,0:T(8,128)S(1)}, u32[]{:S(2)}, u32[]{:S(2)}) collective-permute-start(f32[4,24,1536]{2,1,0:T(8,128)S(1)} %collective-permute-done.11.refs_3_), channel_id=1, source_target_pairs={{0,4},{4,0},{8,12},{12,8},{16,20},{20,16},{24,28},{28,24},{32,36},... | collective-permute-start | bytes 1769480 | tf_op jit(solution)/shard_map/ppermute | solution.py:370
  97.3 5.1 %collective-permute-start.20 = (f32[4,24,1536]{2,1,0:T(8,128)}, f32[4,24,1536]{2,1,0:T(8,128)S(1)}, u32[]{:S(2)}, u32[]{:S(2)}) collective-permute-start(f32[4,24,1536]{2,1,0:T(8,128)} %collective-permute-done.12.refs_5_), channel_id=1, source_target_pairs={{0,4},{4,0},{8,12},{12,8},{16,20},{20,16},{24,28},{28,24},{32,36},... | collective-permute-start | bytes 1769480 | tf_op jit(solution)/shard_map/ppermute | solution.py:370
  98.1 4.4 %collective-permute-start.21 = (f32[4,24,1536]{2,1,0:T(8,128)}, f32[4,24,1536]{2,1,0:T(8,128)S(1)}, u32[]{:S(2)}, u32[]{:S(2)}) collective-permute-start(f32[4,24,1536]{2,1,0:T(8,128)} %collective-permute-done.13.refs_6_), channel_id=1, source_target_pairs={{0,4},{4,0},{8,12},{12,8},{16,20},{20,16},{24,28},{28,24},{32,36},... | collective-permute-start | bytes 1769480 | tf_op jit(solution)/shard_map/ppermute | solution.py:370
  99.0 4.2 %collective-permute-start.22 = (f32[4,24,1536]{2,1,0:T(8,128)S(1)}, f32[4,24,1536]{2,1,0:T(8,128)S(1)}, u32[]{:S(2)}, u32[]{:S(2)}) collective-permute-start(f32[4,24,1536]{2,1,0:T(8,128)S(1)} %collective-permute-done.14.refs_7_), channel_id=1, source_target_pairs={{0,4},{4,0},{8,12},{12,8},{16,20},{20,16},{24,28},{28,24},{32,36},... | collective-permute-start | bytes 1769480 | tf_op jit(solution)/shard_map/ppermute | solution.py:370
  (18 other events, 281.7 us)

commit v5 on v4

--- a/solution.py
+++ b/solution.py
@@ -155,18 +155,16 @@
 
     @pl.when(step == 0)
     def _():
-        for i in range(parts):
-            lanes = rank // 128
-            value = jnp.concatenate(
-                [
-                    received_ref[pl.ds(h * parts + i, total, stride=lanes * parts), :]
-                    for h in range(lanes)
-                ],
-                axis=1,
-            )
-            if i * rank < PANEL:
-                value = jnp.where(place_ref[1] == 1, 0.0, value)
-            high_ref[i], low_ref[i] = split(value)
+        lanes = rank // 128
+        tiles = received_ref[...].reshape(total // 8, 8, lanes, parts, 128)
+        for h in range(lanes):
+            turned = jnp.swapaxes(tiles[:, :, h], 1, 2)
+            columns = slice(h * 128, (h + 1) * 128)
+            for i in range(parts):
+                value = turned[:, i].reshape(total, 128)
+                if i * rank < PANEL:
+                    value = jnp.where(place_ref[1] == 1, 0.0, value)
+                high_ref[i, :, columns], low_ref[i, :, columns] = split(value)
 
     chosen = one_hot(pairs_ref[...], step * rows, rows)
     for i in range(parts):

time: 157 us -> 158 us (level)
  no operation moved by 1% of the time
where the time goes in v5:
time: 158 us; the launch traced here: 157 us
  Pallas kernels  65.4 us (41%)
  starting transfers between devices  43 us (27%)
  waiting for transfers between devices  34.8 us (22%)
  local copies, waits for them, and re-layouts  7.58 us (5%)
  other arithmetic  4.13 us (3%)
    pallas_call x1, Pallas kernels, solve_and_update(): pl.pallas_call(solve_kernel, grid=(rows // width,), in_specs=[pl.BlockSpe...  28.2 us
    ppermute x12, waiting for transfers between devices, along(): return lax.ppermute(value, 'feat', [(f, ring(f)) for f in range(n_feat)])  24 us
    pallas_call x1, Pallas kernels, slot_gradients(): pl.pallas_call(gradient_kernel, grid_spec=pltpu.PrefetchScalarGridSpec(nu...  16 us
    ppermute x12, starting transfers between devices, along(): return lax.ppermute(value, 'feat', [(f, ring(f)) for f in range(n_feat)])  14.2 us
    all_to_all x1, starting transfers between devices, per_device(): lax.all_to_all(send.reshape((n_feat * n_pair,) + send.shape[2:]), ('feat'...  10.9 us
    all_to_all x1, starting transfers between devices, per_device(): lax.all_to_all(outgoing.reshape((n_feat,) + outgoing.shape[2:]), 'feat',...  9.6 us
    pallas_call x1, Pallas kernels, arrange_rows(): pl.pallas_call(arrange_kernel, grid=(width // PANEL,), in_specs=[pl.Block...  9.29 us
    pallas_call x1, Pallas kernels, place_rows(): pl.pallas_call(place_kernel, grid=(total // rows,), in_specs=[pl.BlockSpe...  8.96 us
  transfers between devices with their start and end apart: 25, of which 15 were waited for; matrix products, arithmetic and copies ran while one was open for 6% of the time, Pallas kernels for 34%

profile of v5, /device:TPU:1, one launch (start us, length us, event | category | flops | bytes accessed | tf_op | source)
XLA Modules:
  0.0 156.5 jit_solution(11403099643790009500)
XLA Ops:
  0.6 3.0 %cut_panel.1 = f32[16,2,8,1024]{3,2,1,0:T(8,128)} custom-call(s32[6]{0:T(128)} %stack.31.place_ref, f32[2048,1536]{1,0:T(8,128)} %factor_ref.1), custom_call_target="tpu_custom_call" | custom-call | tf_op jit(solution)/shard_map/cut_panel/pallas_call | solution.py:90
  3.6 9.6 %all-to-all-start = ((f32[32,8,1024]{2,1,0:T(8,128)}), f32[32,8,1024]{2,1,0:T(8,128)S(1)}, u32[]{:S(2)}, u32[]{:S(2)}) async-start(f32[32,8,1024]{2,1,0:T(8,128)} %bitcast.31), calls=%async_computation | async-start | bytes 2097152 | tf_op jit(solution)/shard_map/all_to_all | solution.py:386
  13.9 16.0 %slot_gradients.1 = (f32[32,4,4,2,8,128]{5,4,3,2,1,0:T(8,128)}, f32[16,1536]{1,0:T(8,128)}) custom-call(s32[16,2]{1,0:T(8,128)} %copy.8.counts_ref, bf16[16,2,512,256]{3,2,1,0:T(8,128)(2,1)} %out_ref.1, bf16[16,2,512,256]{3,2,1,0:T(8,128)(2,1)} %in_ref.1), custom_call_target="tpu_custom_call" | custom-call | flops 2147483648 | bytes 25165824 | tf_op jit(solution)/shard_map/slot_gradients/pallas_call | solution.py:43
  31.1 1.3 collective-permute-start
  32.4 2.5 %collective-permute-start.4 = (f32[12,1536]{1,0:T(8,128)S(1)}, f32[12,1536]{1,0:T(8,128)S(1)}, u32[]{:S(2)}, u32[]{:S(2)}) collective-permute-start(f32[12,1536]{1,0:T(8,128)S(1)} %get-tuple-element.46), channel_id=1, source_target_pairs={{0,2},{1,3},{2,0},{3,1},{4,6},{5,7},{6,4},{7,5},{8,10},{9,11},{10,... | collective-permute-start | bytes 221192 | tf_op jit(solution)/shard_map/ppermute | solution.py:324
  36.7 2.3 %collective-permute-start.3 = (f32[1,24,1536]{2,1,0:T(8,128)S(1)}, f32[1,24,1536]{2,1,0:T(8,128)S(1)}, u32[]{:S(2)}, u32[]{:S(2)}) collective-permute-start(f32[1,24,1536]{2,1,0:T(8,128)S(1)} %maximum_bitcast_fusion), channel_id=1, source_target_pairs={{0,24},{4,28},{8,0},{12,4},{16,8},{20,12},{24,16},{28,20},{32,56},... | collective-permute-start | bytes 442376 | tf_op jit(solution)/shard_map/ppermute | solution.py:328
  40.2 2.6 %collective-permute-start.8 = (f32[1,24,1536]{2,1,0:T(8,128)S(1)}, f32[1,24,1536]{2,1,0:T(8,128)S(1)}, u32[]{:S(2)}, u32[]{:S(2)}) collective-permute-start(f32[1,24,1536]{2,1,0:T(8,128)S(1)} %maximum_bitcast_fusion.1), channel_id=1, source_target_pairs={{0,96},{4,100},{8,104},{12,108},{16,112},{20,116},{24,120},{28,124... | collective-permute-start | bytes 442376 | tf_op jit(solution)/shard_map/ppermute | solution.py:328
  44.6 4.2 %collective-permute-done.1 = f32[1,24,1536]{2,1,0:T(8,128)S(1)} collective-permute-done((f32[1,24,1536]{2,1,0:T(8,128)S(1)}, f32[1,24,1536]{2,1,0:T(8,128)S(1)}, u32[]{:S(2)}, u32[]{:S(2)}) %collective-permute-start.1) | collective-permute-done | bytes 147488 | tf_op jit(solution)/shard_map/ppermute | solution.py:328
  48.9 1.6 %collective-permute-done.6 = f32[1,24,1536]{2,1,0:T(8,128)S(1)} collective-permute-done((f32[1,24,1536]{2,1,0:T(8,128)S(1)}, f32[1,24,1536]{2,1,0:T(8,128)S(1)}, u32[]{:S(2)}, u32[]{:S(2)}) %collective-permute-start.6) | collective-permute-done | bytes 147488 | tf_op jit(solution)/shard_map/ppermute | solution.py:328
  54.8 1.7 %collective-permute-start.14 = (f32[4,24,1536]{2,1,0:T(8,128)S(1)}, f32[4,24,1536]{2,1,0:T(8,128)S(1)}, u32[]{:S(2)}, u32[]{:S(2)}) collective-permute-start(f32[4,24,1536]{2,1,0:T(8,128)S(1)} %pad_maximum_fusion.1.refs_4_), channel_id=1, source_target_pairs={{0,24},{4,28},{8,0},{12,4},{16,8},{20,12},{24,16},{28,20},{32,56},... | collective-permute-start | bytes 1769480 | tf_op jit(solution)/shard_map/ppermute | solution.py:328
  56.5 1.9 %collective-permute-start.13 = (f32[4,24,1536]{2,1,0:T(8,128)S(1)}, f32[4,24,1536]{2,1,0:T(8,128)}, u32[]{:S(2)}, u32[]{:S(2)}) collective-permute-start(f32[4,24,1536]{2,1,0:T(8,128)S(1)} %pad_maximum_fusion.1.refs_4_), channel_id=1, source_target_pairs={{0,16},{4,20},{8,24},{12,28},{16,0},{20,4},{24,8},{28,12},{32,48},... | collective-permute-start | bytes 1769480 | tf_op jit(solution)/shard_map/ppermute | solution.py:328
  58.3 3.8 %collective-permute-done.11.refs_3_ = f32[4,24,1536]{2,1,0:T(8,128)S(1)} collective-permute-done((f32[4,24,1536]{2,1,0:T(8,128)S(1)}, f32[4,24,1536]{2,1,0:T(8,128)S(1)}, u32[]{:S(2)}, u32[]{:S(2)}) %collective-permute-start.11) | collective-permute-done | bytes 589856 | tf_op jit(solution)/shard_map/ppermute | solution.py:328
  62.2 1.5 collective-permute-start.12
  66.2 1.4 fusion
  68.3 1.5 reshape.19.pairs_ref
  69.8 13.4 %collective-permute-done.9.refs_1_ = f32[4,24,1536]{2,1,0:T(8,128)S(1)} collective-permute-done((f32[4,24,1536]{2,1,0:T(8,128)S(1)}, f32[4,24,1536]{2,1,0:T(8,128)S(1)}, u32[]{:S(2)}, u32[]{:S(2)}) %collective-permute-start.9) | collective-permute-done | bytes 589856 | tf_op jit(solution)/shard_map/ppermute | solution.py:328
  83.5 10.9 %all-to-all-start.1 = ((f32[128,4,2,8,128]{4,3,2,1,0:T(8,128)}), f32[128,4,2,8,128]{4,3,2,1,0:T(8,128)}, u32[]{:S(2)}, u32[]{:S(2)}) async-start(f32[128,4,2,8,128]{4,3,2,1,0:T(8,128)} %bitcast.30), calls=%async_computation.1 | async-start | bytes 8388608 | tf_op jit(solution)/shard_map/all_to_all | solution.py:392
  94.4 1.2 collective-permute-start.15
  99.4 1.3 collective-permute-done.17.refs_10_
  100.7 1.7 %collective-permute-done.18.refs_11_ = f32[4,24,1536]{2,1,0:T(8,128)S(1)} collective-permute-done((f32[4,24,1536]{2,1,0:T(8,128)S(1)}, f32[4,24,1536]{2,1,0:T(8,128)S(1)}, u32[]{:S(2)}, u32[]{:S(2)}) %collective-permute-start.18) | collective-permute-done | bytes 589856 | tf_op jit(solution)/shard_map/ppermute | solution.py:368
  104.8 9.3 %arrange_rows.1 = (f32[512,1536]{1,0:T(8,128)}, f32[2,512,1536]{2,1,0:T(8,128)}) custom-call(s32[6]{0:T(128)} %stack.31.place_ref, s32[1,512]{1,0:T(1,128)} %reshape.19.pairs_ref, f32[4,24,1536]{2,1,0:T(8,128)} %copy-done.2, f32[4,24,1536]{2,1,0:T(8,128)} %copy-done.6, f32[4,24,1536]{2,1,0:T(8,128)} %copy-done.5, f32[4,24,1536]{2,1,0:T(8,128)} %copy-done.4, ...), custom_call_target="tpu_custom_call" | custom-call | flops 1 | bytes 1 | tf_op jit(solution)/shard_map/arrange_rows/pallas_call | solution.py:237
  114.1 28.2 %solve_and_update.1.update_ref = f32[512,2048]{1,0:T(8,128)} custom-call(s32[6]{0:T(128)} %stack.31.place_ref, f32[512,1536]{1,0:T(8,128)} %get-tuple-element.37.right_ref, f32[2,512,1536]{2,1,0:T(8,128)} %get-tuple-element.38.panels_ref, f32[2048,1536]{1,0:T(8,128)} %factor_ref.1), custom_call_target="tpu_custom_call" | custom-call | flops 1 | bytes 1 | tf_op jit(solution)/shard_map/solve_and_update/pallas_call | solution.py:299
  142.3 5.3 %all-to-all-done.1 = f32[128,4,2,8,128]{4,3,2,1,0:T(8,128)} async-done(((f32[128,4,2,8,128]{4,3,2,1,0:T(8,128)}), f32[128,4,2,8,128]{4,3,2,1,0:T(8,128)}, u32[]{:S(2)}, u32[]{:S(2)}) %all-to-all-start.1) | async-done | bytes 4194336 | tf_op jit(solution)/shard_map/all_to_all | solution.py:392
  147.5 9.0 %place_rows.1 = f32[512,2048]{1,0:T(8,128)} custom-call(s32[6]{0:T(128)S(1)} %copy-done, s32[1,512]{1,0:T(1,128)S(1)} %copy-done.1, f32[8192,128]{1,0:T(8,128)} %bitcast.18.received_ref, f32[512,2048]{1,0:T(8,128)} %solve_and_update.1.update_ref), custom_call_target="tpu_custom_call" | custom-call | tf_op jit(solution)/shard_map/place_rows/pallas_call | solution.py:182
  (96 shorter events, 21.2 us)
Async XLA Ops:
  3.6 26.5 %all-to-all-start = ((f32[32,8,1024]{2,1,0:T(8,128)}), f32[32,8,1024]{2,1,0:T(8,128)S(1)}, u32[]{:S(2)}, u32[]{:S(2)}) async-start(f32[32,8,1024]{2,1,0:T(8,128)} %bitcast.31), calls=%async_computation | async-start | bytes 2097152 | tf_op jit(solution)/shard_map/all_to_all | solution.py:386
  31.1 5.5 %collective-permute-start = (f32[12,1536]{1,0:T(8,128)S(1)}, f32[12,1536]{1,0:T(8,128)S(1)}, u32[]{:S(2)}, u32[]{:S(2)}) collective-permute-start(f32[12,1536]{1,0:T(8,128)S(1)} %get-tuple-element.48), channel_id=1, source_target_pairs={{0,1},{1,2},{2,3},{3,0},{4,5},{5,6},{6,7},{7,4},{8,9},{9,10},{10,1... | collective-permute-start | bytes 221192 | tf_op jit(solution)/shard_map/ppermute | solution.py:324
  32.4 7.8 %collective-permute-start.4 = (f32[12,1536]{1,0:T(8,128)S(1)}, f32[12,1536]{1,0:T(8,128)S(1)}, u32[]{:S(2)}, u32[]{:S(2)}) collective-permute-start(f32[12,1536]{1,0:T(8,128)S(1)} %get-tuple-element.46), channel_id=1, source_target_pairs={{0,2},{1,3},{2,0},{3,1},{4,6},{5,7},{6,4},{7,5},{8,10},{9,11},{10,... | collective-permute-start | bytes 221192 | tf_op jit(solution)/shard_map/ppermute | solution.py:324
  34.8 5.3 %collective-permute-start.5 = (f32[12,1536]{1,0:T(8,128)S(1)}, f32[12,1536]{1,0:T(8,128)S(1)}, u32[]{:S(2)}, u32[]{:S(2)}) collective-permute-start(f32[12,1536]{1,0:T(8,128)S(1)} %get-tuple-element.47), channel_id=1, source_target_pairs={{0,3},{1,0},{2,1},{3,2},{4,7},{5,4},{6,5},{7,6},{8,11},{9,8},{10,9... | collective-permute-start | bytes 221192 | tf_op jit(solution)/shard_map/ppermute | solution.py:324
  36.7 6.6 %collective-permute-start.3 = (f32[1,24,1536]{2,1,0:T(8,128)S(1)}, f32[1,24,1536]{2,1,0:T(8,128)S(1)}, u32[]{:S(2)}, u32[]{:S(2)}) collective-permute-start(f32[1,24,1536]{2,1,0:T(8,128)S(1)} %maximum_bitcast_fusion), channel_id=1, source_target_pairs={{0,24},{4,28},{8,0},{12,4},{16,8},{20,12},{24,16},{28,20},{32,56},... | collective-permute-start | bytes 442376 | tf_op jit(solution)/shard_map/ppermute | solution.py:328
  39.0 5.6 %collective-permute-start.2 = (f32[1,24,1536]{2,1,0:T(8,128)S(1)}, f32[1,24,1536]{2,1,0:T(8,128)S(1)}, u32[]{:S(2)}, u32[]{:S(2)}) collective-permute-start(f32[1,24,1536]{2,1,0:T(8,128)S(1)} %maximum_bitcast_fusion), channel_id=1, source_target_pairs={{0,16},{4,20},{8,24},{12,28},{16,0},{20,4},{24,8},{28,12},{32,48},... | collective-permute-start | bytes 442376 | tf_op jit(solution)/shard_map/ppermute | solution.py:328
  39.6 9.2 %collective-permute-start.1 = (f32[1,24,1536]{2,1,0:T(8,128)S(1)}, f32[1,24,1536]{2,1,0:T(8,128)S(1)}, u32[]{:S(2)}, u32[]{:S(2)}) collective-permute-start(f32[1,24,1536]{2,1,0:T(8,128)S(1)} %maximum_bitcast_fusion), channel_id=1, source_target_pairs={{0,8},{4,12},{8,16},{12,20},{16,24},{20,28},{24,0},{28,4},{32,40},... | collective-permute-start | bytes 442376 | tf_op jit(solution)/shard_map/ppermute | solution.py:328
  40.2 8.6 %collective-permute-start.8 = (f32[1,24,1536]{2,1,0:T(8,128)S(1)}, f32[1,24,1536]{2,1,0:T(8,128)S(1)}, u32[]{:S(2)}, u32[]{:S(2)}) collective-permute-start(f32[1,24,1536]{2,1,0:T(8,128)S(1)} %maximum_bitcast_fusion.1), channel_id=1, source_target_pairs={{0,96},{4,100},{8,104},{12,108},{16,112},{20,116},{24,120},{28,124... | collective-permute-start | bytes 442376 | tf_op jit(solution)/shard_map/ppermute | solution.py:328
  42.8 6.1 %collective-permute-start.7 = (f32[1,24,1536]{2,1,0:T(8,128)S(1)}, f32[1,24,1536]{2,1,0:T(8,128)S(1)}, u32[]{:S(2)}, u32[]{:S(2)}) collective-permute-start(f32[1,24,1536]{2,1,0:T(8,128)S(1)} %maximum_bitcast_fusion.1), channel_id=1, source_target_pairs={{0,64},{4,68},{8,72},{12,76},{16,80},{20,84},{24,88},{28,92},{32,9... | collective-permute-start | bytes 442376 | tf_op jit(solution)/shard_map/ppermute | solution.py:328
  43.3 7.2 %collective-permute-start.6 = (f32[1,24,1536]{2,1,0:T(8,128)S(1)}, f32[1,24,1536]{2,1,0:T(8,128)S(1)}, u32[]{:S(2)}, u32[]{:S(2)}) collective-permute-start(f32[1,24,1536]{2,1,0:T(8,128)S(1)} %maximum_bitcast_fusion.1), channel_id=1, source_target_pairs={{0,32},{4,36},{8,40},{12,44},{16,48},{20,52},{24,56},{28,60},{32,6... | collective-permute-start | bytes 442376 | tf_op jit(solution)/shard_map/ppermute | solution.py:328
  50.5 11.7 %collective-permute-start.11 = (f32[4,24,1536]{2,1,0:T(8,128)S(1)}, f32[4,24,1536]{2,1,0:T(8,128)S(1)}, u32[]{:S(2)}, u32[]{:S(2)}) collective-permute-start(f32[4,24,1536]{2,1,0:T(8,128)S(1)} %pad_maximum_fusion.refs_0_), channel_id=1, source_target_pairs={{0,96},{4,100},{8,104},{12,108},{16,112},{20,116},{24,120},{28,124... | collective-permute-start | bytes 1769480 | tf_op jit(solution)/shard_map/ppermute | solution.py:328
  53.7 16.1 %collective-permute-start.10 = (f32[4,24,1536]{2,1,0:T(8,128)S(1)}, f32[4,24,1536]{2,1,0:T(8,128)S(1)}, u32[]{:S(2)}, u32[]{:S(2)}) collective-permute-start(f32[4,24,1536]{2,1,0:T(8,128)S(1)} %pad_maximum_fusion.refs_0_), channel_id=1, source_target_pairs={{0,64},{4,68},{8,72},{12,76},{16,80},{20,84},{24,88},{28,92},{32,9... | collective-permute-start | bytes 1769480 | tf_op jit(solution)/shard_map/ppermute | solution.py:328
  54.3 29.0 %collective-permute-start.9 = (f32[4,24,1536]{2,1,0:T(8,128)S(1)}, f32[4,24,1536]{2,1,0:T(8,128)S(1)}, u32[]{:S(2)}, u32[]{:S(2)}) collective-permute-start(f32[4,24,1536]{2,1,0:T(8,128)S(1)} %pad_maximum_fusion.refs_0_), channel_id=1, source_target_pairs={{0,32},{4,36},{8,40},{12,44},{16,48},{20,52},{24,56},{28,60},{32,6... | collective-permute-start | bytes 1769480 | tf_op jit(solution)/shard_map/ppermute | solution.py:328
  54.8 28.4 %collective-permute-start.14 = (f32[4,24,1536]{2,1,0:T(8,128)S(1)}, f32[4,24,1536]{2,1,0:T(8,128)S(1)}, u32[]{:S(2)}, u32[]{:S(2)}) collective-permute-start(f32[4,24,1536]{2,1,0:T(8,128)S(1)} %pad_maximum_fusion.1.refs_4_), channel_id=1, source_target_pairs={{0,24},{4,28},{8,0},{12,4},{16,8},{20,12},{24,16},{28,20},{32,56},... | collective-permute-start | bytes 1769480 | tf_op jit(solution)/shard_map/ppermute | solution.py:328
  56.5 26.8 %collective-permute-start.13 = (f32[4,24,1536]{2,1,0:T(8,128)S(1)}, f32[4,24,1536]{2,1,0:T(8,128)}, u32[]{:S(2)}, u32[]{:S(2)}) collective-permute-start(f32[4,24,1536]{2,1,0:T(8,128)S(1)} %pad_maximum_fusion.1.refs_4_), channel_id=1, source_target_pairs={{0,16},{4,20},{8,24},{12,28},{16,0},{20,4},{24,8},{28,12},{32,48},... | collective-permute-start | bytes 1769480 | tf_op jit(solution)/shard_map/ppermute | solution.py:328
  62.2 21.3 %collective-permute-start.12 = (f32[4,24,1536]{2,1,0:T(8,128)S(1)}, f32[4,24,1536]{2,1,0:T(8,128)}, u32[]{:S(2)}, u32[]{:S(2)}) collective-permute-start(f32[4,24,1536]{2,1,0:T(8,128)S(1)} %pad_maximum_fusion.1.refs_4_), channel_id=1, source_target_pairs={{0,8},{4,12},{8,16},{12,20},{16,24},{20,28},{24,0},{28,4},{32,40},... | collective-permute-start | bytes 1769480 | tf_op jit(solution)/shard_map/ppermute | solution.py:328
  83.5 64.1 %all-to-all-start.1 = ((f32[128,4,2,8,128]{4,3,2,1,0:T(8,128)}), f32[128,4,2,8,128]{4,3,2,1,0:T(8,128)}, u32[]{:S(2)}, u32[]{:S(2)}) async-start(f32[128,4,2,8,128]{4,3,2,1,0:T(8,128)} %bitcast.30), calls=%async_computation.1 | async-start | bytes 8388608 | tf_op jit(solution)/shard_map/all_to_all | solution.py:392
  94.4 2.9 %collective-permute-start.15 = (f32[4,24,1536]{2,1,0:T(8,128)S(1)}, f32[4,24,1536]{2,1,0:T(8,128)S(1)}, u32[]{:S(2)}, u32[]{:S(2)}) collective-permute-start(f32[4,24,1536]{2,1,0:T(8,128)S(1)} %pad_maximum_fusion.refs_0_), channel_id=1, source_target_pairs={{0,4},{4,0},{8,12},{12,8},{16,20},{20,16},{24,28},{28,24},{32,36},... | collective-permute-start | bytes 1769480 | tf_op jit(solution)/shard_map/ppermute | solution.py:368
  95.8 3.2 %collective-permute-start.16 = (f32[4,24,1536]{2,1,0:T(8,128)S(1)}, f32[4,24,1536]{2,1,0:T(8,128)S(1)}, u32[]{:S(2)}, u32[]{:S(2)}) collective-permute-start(f32[4,24,1536]{2,1,0:T(8,128)S(1)} %collective-permute-done.9.refs_1_), channel_id=1, source_target_pairs={{0,4},{4,0},{8,12},{12,8},{16,20},{20,16},{24,28},{28,24},{32,36},... | collective-permute-start | bytes 1769480 | tf_op jit(solution)/shard_map/ppermute | solution.py:368
  96.2 4.5 %collective-permute-start.17 = (f32[4,24,1536]{2,1,0:T(8,128)S(1)}, f32[4,24,1536]{2,1,0:T(8,128)S(1)}, u32[]{:S(2)}, u32[]{:S(2)}) collective-permute-start(f32[4,24,1536]{2,1,0:T(8,128)S(1)} %collective-permute-done.10.refs_2_), channel_id=1, source_target_pairs={{0,4},{4,0},{8,12},{12,8},{16,20},{20,16},{24,28},{28,24},{32,36},... | collective-permute-start | bytes 1769480 | tf_op jit(solution)/shard_map/ppermute | solution.py:368
  96.3 6.1 %collective-permute-start.18 = (f32[4,24,1536]{2,1,0:T(8,128)S(1)}, f32[4,24,1536]{2,1,0:T(8,128)S(1)}, u32[]{:S(2)}, u32[]{:S(2)}) collective-permute-start(f32[4,24,1536]{2,1,0:T(8,128)S(1)} %collective-permute-done.11.refs_3_), channel_id=1, source_target_pairs={{0,4},{4,0},{8,12},{12,8},{16,20},{20,16},{24,28},{28,24},{32,36},... | collective-permute-start | bytes 1769480 | tf_op jit(solution)/shard_map/ppermute | solution.py:368
  97.3 5.1 %collective-permute-start.20 = (f32[4,24,1536]{2,1,0:T(8,128)}, f32[4,24,1536]{2,1,0:T(8,128)S(1)}, u32[]{:S(2)}, u32[]{:S(2)}) collective-permute-start(f32[4,24,1536]{2,1,0:T(8,128)} %collective-permute-done.12.refs_5_), channel_id=1, source_target_pairs={{0,4},{4,0},{8,12},{12,8},{16,20},{20,16},{24,28},{28,24},{32,36},... | collective-permute-start | bytes 1769480 | tf_op jit(solution)/shard_map/ppermute | solution.py:368
  98.1 4.4 %collective-permute-start.21 = (f32[4,24,1536]{2,1,0:T(8,128)}, f32[4,24,1536]{2,1,0:T(8,128)S(1)}, u32[]{:S(2)}, u32[]{:S(2)}) collective-permute-start(f32[4,24,1536]{2,1,0:T(8,128)} %collective-permute-done.13.refs_6_), channel_id=1, source_target_pairs={{0,4},{4,0},{8,12},{12,8},{16,20},{20,16},{24,28},{28,24},{32,36},... | collective-permute-start | bytes 1769480 | tf_op jit(solution)/shard_map/ppermute | solution.py:368
  99.0 4.2 %collective-permute-start.22 = (f32[4,24,1536]{2,1,0:T(8,128)S(1)}, f32[4,24,1536]{2,1,0:T(8,128)S(1)}, u32[]{:S(2)}, u32[]{:S(2)}) collective-permute-start(f32[4,24,1536]{2,1,0:T(8,128)S(1)} %collective-permute-done.14.refs_7_), channel_id=1, source_target_pairs={{0,4},{4,0},{8,12},{12,8},{16,20},{20,16},{24,28},{28,24},{32,36},... | collective-permute-start | bytes 1769480 | tf_op jit(solution)/shard_map/ppermute | solution.py:368
  (18 other events, 281.7 us)
